TPU v7x, 256 devices: a whole 4x4x8 slice. The times are simulated.
256 devices in a mesh: tm: 2 (over x_lo), sx: 32 (over z, x_hi, core), sy: 4 (over y).
Axes of the slice: x: 4 (x_hi: 2, x_lo: 2; x = x_hi * 2 + x_lo), y: 4, z: 8, core: 2. Of those that a mesh axis runs over, the one named last changes fastest.
Arguments:
- forcing: float32 [8, 256, 64, 16, 128], P('tm', 'sx', 'sy'), may hold values from -6 to 6
- initial: float32 [8, 256, 64, 16, 128], P('tm', 'sx', 'sy'), may hold values from -3 to 3
- conductance: float32 [8, 256, 64, 16], P('tm', 'sx', 'sy'), may hold values from 0.5 to 1.5
- counts: int32 [32, 4], P('sx', 'sy'), may hold values from 1024 to 2048, as said below
- block_matrix: float32 [128, 128], replicated, may hold values from -1.1 to 11.1
- precond: float32 [128, 128], replicated, may hold values from -0.011 to 0.111
- face_coupling: float32 [6, 128, 128], replicated, may hold values from -1 to 1
- time_coupling: float32 [64, 128], replicated, may hold values from -3 to 23
Outputs:
- adjoint: float32 [8, 256, 64, 16, 128], P('tm', 'sx', 'sy')
Inputs may be any that keep to these rules, and one draw needn't show every extreme that they name: `counts`: active elements of a tile are those whose position in the order x, y, z (z fastest) is below the tile's count; some tile has all 2048 active.
All inputs are finite; a program needn't handle non-finite values.
Results may differ from a plain program's by a relative error of at most 0.00012.
Values sent between devices are 32-bit elements; how exact they have to be, the bound alone decides.
No kernel may reach another device: no remote copies, remote signals or barrier semaphores. Data moves between devices by JAX's collectives and lax.ppermute only.
A program may use at most 128 MiB of HBM per device.

v0:
```python
import functools

import jax
import jax.numpy as jnp
from jax import lax
from jax.experimental import pallas as pl
from jax.experimental.pallas import tpu as pltpu
from jax.sharding import PartitionSpec as P

SWEEPS = 2
OMEGA = 0.7
NTD, EX, EY, EZ, BLOCK = 4, 8, 16, 16, 128
SPACE = BLOCK // 2
LAYER = EY * EZ
F32, BF16 = jnp.float32, jnp.bfloat16
VMEM = pltpu.VMEM
ANY = pl.BlockSpec(memory_space=pl.ANY)
INV = pl.BlockSpec(memory_space=VMEM)
INS = pl.BlockSpec(memory_space=pltpu.SMEM)
INNER = (1, 6)
OUTER = ((0, 1), (7, 1))


def params(mib):
    return pltpu.CompilerParams(vmem_limit_bytes=mib << 20)


def cost(us):
    return pl.CostEstimate(flops=int(us * 1.0e9), bytes_accessed=0, transcendentals=0)


def split(value):
    high = value.astype(BF16)
    low = (value - high.astype(F32)).astype(BF16)
    return high, low


def dot(rows, matrix):
    return jnp.dot(rows, matrix, preferred_element_type=F32)


def both(value):
    return jnp.concatenate(split(value), axis=-1)


def folded(rows, matrix):
    out = dot(rows, matrix)
    return out[:, :BLOCK] + out[:, BLOCK:]


def mask(info, first, rows):
    position = lax.broadcasted_iota(jnp.int32, (rows, BLOCK), 0) + first * LAYER
    return position < info[0]


def faces_kernel(info, initial, left, right, front, back, sems):
    copies = [
        pltpu.make_async_copy(initial.at[:, 0], left, sems.at[0]),
        pltpu.make_async_copy(initial.at[:, EX - 1], right, sems.at[1]),
        pltpu.make_async_copy(initial.at[:, :, pl.ds(0, EZ)], front, sems.at[2]),
        pltpu.make_async_copy(initial.at[:, :, pl.ds(LAYER - EZ, EZ)], back, sems.at[3]),
    ]
    for copy in copies:
        copy.start()
    for copy, ref, at in zip(copies, (left, right), (0, EX - 1)):
        copy.wait()
        keep = mask(info, at, LAYER)
        for t in range(NTD):
            ref[t] = jnp.where(keep, ref[t], 0.0)
    for copy, ref, at in zip(copies[2:], (front, back), (0, LAYER - EZ)):
        copy.wait()
        for x in range(EX):
            position = lax.broadcasted_iota(jnp.int32, (EZ, BLOCK), 0) + (x * LAYER + at)
            for t in range(NTD):
                ref[t, x] = jnp.where(position < info[0], ref[t, x], 0.0)


def faces_of_initial(info, initial):
    return pl.pallas_call(
        faces_kernel,
        out_shape=[
            VMEM((NTD, LAYER, BLOCK), F32),
            VMEM((NTD, LAYER, BLOCK), F32),
            VMEM((NTD, EX, EZ, BLOCK), F32),
            VMEM((NTD, EX, EZ, BLOCK), F32),
        ],
        in_specs=[INS, ANY],
        out_specs=[INV] * 4,
        scratch_shapes=[pltpu.SemaphoreType.DMA((4,))],
        compiler_params=params(4),
        cost_estimate=cost(2),
        name="faces",
    )(info, initial)


def stencil_setup(high, low):
    for ref in (high, low):
        for x in (0, EX + 1):
            ref[x] = jnp.zeros(ref.shape[1:], BF16)
        for x in range(1, EX + 1):
            for t in range(NTD):
                ref[x, t, 0:EZ] = jnp.zeros((EZ, BLOCK), BF16)
                ref[x, t, EZ + LAYER :] = jnp.zeros((EZ, BLOCK), BF16)


def stencil_split(x, value, high, low):
    h, l = split(value)
    high[x + 1, :, pl.ds(EZ, LAYER)] = h
    low[x + 1, :, pl.ds(EZ, LAYER)] = l


def flat(value):
    return value.reshape(NTD * LAYER, BLOCK)


def stencil_layer(x, adjoint, high, low, lateral, central):
    pieces = []
    for ref in (high, low):
        pieces += [
            flat(ref[x, :, pl.ds(EZ, LAYER)]),
            flat(ref[x + 2, :, pl.ds(EZ, LAYER)]),
            flat(ref[x + 1, :, pl.ds(0, LAYER)]),
            flat(ref[x + 1, :, pl.ds(2 * EZ, LAYER)]),
        ]
    around = folded(jnp.concatenate(pieces, axis=1), lateral[...])
    own = [flat(ref[x + 1, :, pl.ds(EZ, LAYER)]) for ref in (high, low)]
    out = dot(jnp.concatenate(own, axis=1), central[...])
    own, below, above = (
        out[:, k * BLOCK : (k + 1) * BLOCK] + out[:, (k + 3) * BLOCK : (k + 4) * BLOCK] for k in range(3)
    )
    depth = lax.broadcasted_iota(jnp.int32, (NTD * LAYER, BLOCK), 0) % EZ
    below = jnp.where(depth == 0, 0.0, pltpu.roll(below, 1, 0))
    above = jnp.where(depth == EZ - 1, 0.0, pltpu.roll(above, NTD * LAYER - 1, 0))
    return adjoint - own, around + below + above


def first_kernel(
    info, initial, forcing, relaxed, block_matrix, precond, faces, coupling,
    pred, loads, lateral, central, carry,
    adjoint, load, high, low, given, sems,
):
    def fetch(x, which):
        source, target = ((initial, adjoint), (forcing, load))[which]
        return pltpu.make_async_copy(source.at[:, x], target.at[:, x], sems.at[which, x])

    for x in range(EX):
        fetch(x, 0).start()
        fetch(x, 1).start()

    def matrices(value):
        matrix = jnp.dot(value, precond[...], precision=lax.Precision.HIGHEST, preferred_element_type=F32)
        return split(matrix)

    zero = jnp.zeros((BLOCK, BLOCK), BF16)
    for d in range(4):
        h, l = matrices(faces[d])
        lateral[d * BLOCK : (d + 1) * BLOCK, :] = jnp.concatenate([h, l], axis=1)
        lateral[(d + 4) * BLOCK : (d + 5) * BLOCK, :] = jnp.concatenate([h, zero], axis=1)
    parts = [matrices(OMEGA * block_matrix[...]), matrices(faces[4]), matrices(faces[5])]
    central[0:BLOCK, :] = jnp.concatenate([h for h, _ in parts] + [l for _, l in parts], axis=1)
    central[BLOCK:, :] = jnp.concatenate([h for h, _ in parts] + [zero] * 3, axis=1)
    h, l = matrices(coupling[...])
    none = jnp.zeros((SPACE, 2 * BLOCK), BF16)
    carry[...] = jnp.concatenate(
        [jnp.concatenate([h, l], axis=1), none, jnp.concatenate([h, zero[:SPACE]], axis=1), none], axis=0
    )
    h, l = split(precond[...])
    given[0:BLOCK, :] = jnp.concatenate([h, l], axis=1)
    given[BLOCK:, :] = jnp.concatenate([h, zero], axis=1)

    stencil_setup(high, low)

    def enter(x):
        fetch(x, 0).wait()
        position = lax.broadcasted_iota(jnp.int32, (NTD, LAYER, BLOCK), 1) + x * LAYER
        value = jnp.where(position < info[0], adjoint[:, x], 0.0)
        adjoint[:, x] = value
        stencil_split(x, value, high, low)

    def layer(x):
        fetch(x, 1).wait()
        factor = flat(relaxed[:, x])
        rest = factor * folded(both(flat(load[:, x])), given[...])
        loads[:, x] = rest.reshape(NTD, LAYER, BLOCK)
        own, around = stencil_layer(x, flat(adjoint[:, x]), high, low, lateral, central)
        pred[:, x] = (own + rest - factor * around).reshape(NTD, LAYER, BLOCK)

    enter(0)

    def step(x, _):
        enter(x + 1)
        layer(x)
        return 0

    lax.fori_loop(0, EX - 1, step, 0)
    layer(EX - 1)


STACK = (NTD, EX, LAYER, BLOCK)
PADDED = (EX + 2, NTD, LAYER + 2 * EZ, BLOCK)


def first_prediction(info, initial, forcing, relaxed, block_matrix, precond, faces, coupling):
    return pl.pallas_call(
        first_kernel,
        out_shape=[
            VMEM(STACK, F32),
            VMEM(STACK, F32),
            VMEM((8 * BLOCK, 2 * BLOCK), BF16),
            VMEM((2 * BLOCK, 6 * BLOCK), BF16),
            VMEM((2 * BLOCK, 2 * BLOCK), BF16),
        ],
        in_specs=[INS, ANY, ANY] + [INV] * 5,
        out_specs=[INV] * 5,
        scratch_shapes=[
            pltpu.VMEM(STACK, F32),
            pltpu.VMEM(STACK, F32),
            pltpu.VMEM(PADDED, BF16),
            pltpu.VMEM(PADDED, BF16),
            pltpu.VMEM((2 * BLOCK, 2 * BLOCK), BF16),
            pltpu.SemaphoreType.DMA((2, EX)),
        ],
        compiler_params=params(28),
        cost_estimate=cost(10),
        name="first",
    )(info, initial, forcing, relaxed, block_matrix, precond, faces, coupling)


def next_kernel(adjoint, loads, relaxed, lateral, central, pred, high, low):
    stencil_setup(high, low)

    def enter(x):
        stencil_split(x, adjoint[:, x], high, low)

    def layer(x):
        own, around = stencil_layer(x, flat(adjoint[:, x]), high, low, lateral, central)
        value = own + flat(loads[:, x]) - flat(relaxed[:, x]) * around
        pred[:, x] = value.reshape(NTD, LAYER, BLOCK)

    enter(0)

    def step(x, _):
        enter(x + 1)
        layer(x)
        return 0

    lax.fori_loop(0, EX - 1, step, 0)
    layer(EX - 1)


def next_prediction(adjoint, loads, relaxed, lateral, central):
    return pl.pallas_call(
        next_kernel,
        out_shape=VMEM(STACK, F32),
        in_specs=[INV] * 5,
        out_specs=INV,
        scratch_shapes=[pltpu.VMEM(PADDED, BF16), pltpu.VMEM(PADDED, BF16)],
        compiler_params=params(16),
        cost_estimate=cost(8),
        name="next",
    )(adjoint, loads, relaxed, lateral, central)


def chain(info, field, relaxed, carry, runs, incoming):
    traces = incoming
    for t in reversed(range(NTD)):
        fresh = []
        for k, (first, count) in enumerate(runs):
            rows = count * LAYER
            value = field[t, first : first + count].reshape(rows, BLOCK)
            if traces is not None:
                factor = relaxed[t, first : first + count].reshape(rows, BLOCK)
                value = value - factor * folded(both(traces[k]), carry[...])
            value = jnp.where(mask(info, first, rows), value, 0.0)
            field[t, first : first + count] = value.reshape(count, LAYER, BLOCK)
            fresh.append(value)
        traces = fresh
    return traces


def packed(traces):
    if len(traces) == 1:
        half = traces[0].shape[0] // 2
        top, bottom = traces[0][:half], traces[0][half:]
    else:
        top, bottom = traces
    lane = lax.broadcasted_iota(jnp.int32, top.shape, 1)
    return jnp.where(lane < SPACE, top, pltpu.roll(bottom, SPACE, 1))


def unpacked(value, runs):
    swapped = pltpu.roll(value, SPACE, 1)
    if len(runs) == 1:
        return [jnp.concatenate([value, swapped], axis=0)]
    return [value, swapped]


def y_halo_terms(pred, relaxed, lateral, halo, d, at, layers):
    matrix = jnp.concatenate([lateral[d * BLOCK : (d + 1) * BLOCK, :], lateral[(d + 4) * BLOCK : (d + 5) * BLOCK, :]], axis=0)
    first, count = layers
    values = halo[:, first : first + count].reshape(NTD * count * EZ, BLOCK)
    term = folded(both(values), matrix).reshape(NTD, count, EZ, BLOCK)
    rows = pl.ds(at, EZ)
    area = (slice(None), pl.ds(first, count), rows)
    pred[area] = pred[area] - relaxed[area] * term


def inner_kernel(info, pred, relaxed, lateral, carry, front, back, field, trace):
    y_halo_terms(field, relaxed, lateral, front, 2, 0, INNER)
    y_halo_terms(field, relaxed, lateral, back, 3, LAYER - EZ, INNER)

    @pl.when(info[1] == 1)
    def _():
        trace[...] = packed(chain(info, field, relaxed, carry, (INNER,), None))


def x_halo_terms(pred, relaxed, lateral, halo, d, x):
    matrix = jnp.concatenate([lateral[d * BLOCK : (d + 1) * BLOCK, :], lateral[(d + 4) * BLOCK : (d + 5) * BLOCK, :]], axis=0)
    term = folded(both(flat(halo[...])), matrix).reshape(NTD, LAYER, BLOCK)
    pred[:, x] = pred[:, x] - relaxed[:, x] * term


def outer_kernel(info, pred, relaxed, lateral, carry, left, right, front, back, field, trace):
    for run in OUTER:
        y_halo_terms(field, relaxed, lateral, front, 2, 0, run)
        y_halo_terms(field, relaxed, lateral, back, 3, LAYER - EZ, run)
    x_halo_terms(field, relaxed, lateral, left, 0, 0)
    x_halo_terms(field, relaxed, lateral, right, 1, EX - 1)

    @pl.when(info[1] == 1)
    def _():
        trace[...] = packed(chain(info, field, relaxed, carry, OUTER, None))


def with_halos(info, pred, relaxed, lateral, carry, halos, inner):
    rows = (INNER[1] if inner else 2) * LAYER // 2
    return pl.pallas_call(
        inner_kernel if inner else outer_kernel,
        out_shape=[VMEM(STACK, F32), VMEM((rows, BLOCK), F32)],
        in_specs=[INS] + [INV] * (4 + len(halos)),
        out_specs=[INV, INV],
        input_output_aliases={1: 0},
        compiler_params=params(8),
        cost_estimate=cost(2),
        name="halo_inner" if inner else "halo_outer",
    )(info, pred, relaxed, lateral, carry, *halos)


def late_chain(info, field, relaxed, carry, trace, runs):
    @pl.when(info[1] == 0)
    def _():
        chain(info, field, relaxed, carry, runs, unpacked(trace[...], runs))


def late_inner_kernel(info, field, relaxed, carry, trace, out):
    late_chain(info, out, relaxed, carry, trace, (INNER,))


def late_outer_kernel(info, field, relaxed, carry, trace, out, left, right, front, back):
    late_chain(info, out, relaxed, carry, trace, OUTER)
    left[...] = out[:, 0]
    right[...] = out[:, EX - 1]
    front[...] = out[:, :, pl.ds(0, EZ)]
    back[...] = out[:, :, pl.ds(LAYER - EZ, EZ)]


def after_trace(info, field, relaxed, carry, trace, inner):
    out_shape = [VMEM(STACK, F32)]
    if not inner:
        out_shape += [VMEM((NTD, LAYER, BLOCK), F32)] * 2 + [VMEM((NTD, EX, EZ, BLOCK), F32)] * 2
    return pl.pallas_call(
        late_inner_kernel if inner else late_outer_kernel,
        out_shape=out_shape,
        in_specs=[INS] + [INV] * 4,
        out_specs=[INV] * len(out_shape),
        input_output_aliases={1: 0},
        compiler_params=params(8),
        cost_estimate=cost(2),
        name="late_inner" if inner else "late_outer",
    )(info, field, relaxed, carry, trace)


def last_inner_kernel(info, field, relaxed, carry, trace, kept, out, sem):
    late_chain(info, kept, relaxed, carry, trace, (INNER,))
    first, count = INNER
    copy = pltpu.make_async_copy(kept.at[:, pl.ds(first, count)], out.at[:, pl.ds(first, count)], sem)
    copy.start()
    copy.wait()


def last_outer_kernel(info, field, relaxed, carry, trace, given, kept, out, sems):
    late_chain(info, kept, relaxed, carry, trace, OUTER)
    copies = [
        pltpu.make_async_copy(kept.at[:, x], out.at[:, x], sems.at[k]) for k, (x, _) in enumerate(OUTER)
    ]
    for copy in copies:
        copy.start()
    for copy in copies:
        copy.wait()


def last_inner(info, field, relaxed, carry, trace):
    return pl.pallas_call(
        last_inner_kernel,
        out_shape=[VMEM(STACK, F32), jax.ShapeDtypeStruct(STACK, F32)],
        in_specs=[INS] + [INV] * 4,
        out_specs=[INV, ANY],
        input_output_aliases={1: 0},
        scratch_shapes=[pltpu.SemaphoreType.DMA],
        compiler_params=params(8),
        cost_estimate=cost(3),
        name="last_inner",
    )(info, field, relaxed, carry, trace)


def last_outer(info, field, relaxed, carry, trace, given):
    return pl.pallas_call(
        last_outer_kernel,
        out_shape=[VMEM(STACK, F32), jax.ShapeDtypeStruct(STACK, F32)],
        in_specs=[INS] + [INV] * 4 + [ANY],
        out_specs=[INV, ANY],
        input_output_aliases={1: 0, 5: 1},
        scratch_shapes=[pltpu.SemaphoreType.DMA((2,))],
        compiler_params=params(8),
        cost_estimate=cost(2),
        name="last_outer",
    )(info, field, relaxed, carry, trace, given)[1]


def shifted(value, axis, step):
    count = lax.axis_size(axis)
    first, last = max(0, -step), min(count, count - step)
    return lax.ppermute(value, axis, [(i, i + step) for i in range(first, last)])


def halos_of(faces):
    left, right, front, back = faces
    return (shifted(right, "sx", 1), shifted(left, "sx", -1), shifted(back, "sy", 1), shifted(front, "sy", -1))


def body(forcing, initial, conductance, counts, block_matrix, precond, face_coupling, time_coupling):
    shape = forcing.shape
    forcing, initial = forcing.reshape(STACK), initial.reshape(STACK)
    info = jnp.stack([counts[0, 0], lax.axis_index("tm").astype(jnp.int32)])
    relaxed = jnp.broadcast_to((OMEGA / conductance).reshape(NTD, EX, LAYER, 1), STACK)
    halos = halos_of(faces_of_initial(info, initial))
    field, loads, lateral, central, carry = first_prediction(
        info, initial, forcing, relaxed, block_matrix, precond, face_coupling, time_coupling
    )
    for sweep in range(SWEEPS):
        if sweep:
            field = next_prediction(field, loads, relaxed, lateral, central)
        field, inner = with_halos(info, field, relaxed, lateral, carry, halos[2:], True)
        inner = shifted(inner, "tm", -1)
        field, outer = with_halos(info, field, relaxed, lateral, carry, halos, False)
        outer = shifted(outer, "tm", -1)
        if sweep < SWEEPS - 1:
            (field,) = after_trace(info, field, relaxed, carry, inner, True)
            field, *faces = after_trace(info, field, relaxed, carry, outer, False)
            halos = halos_of(faces)
        else:
            field, out = last_inner(info, field, relaxed, carry, inner)
            out = last_outer(info, field, relaxed, carry, outer, out)
    return out.reshape(shape)


def solution(mesh):
    in_specs = (
        P("tm", "sx", "sy", None, None),
        P("tm", "sx", "sy", None, None),
        P("tm", "sx", "sy", None),
        P("sx", "sy"),
        P(),
        P(),
        P(),
        P(),
    )
    out_specs = P("tm", "sx", "sy", None, None)
    return jax.shard_map(body, mesh=mesh, in_specs=in_specs, out_specs=out_specs, check_vma=False)
```

profile of v0, /device:TPU:120, one launch (start us, length us, event | category | flops | bytes accessed | tf_op | source)
XLA Modules:
  0.0 102.0 jit_solution(17074523051517116303)
XLA Ops:
  0.7 2.2 %copy-done = f32[4,8,16,16,128]{4,3,2,1,0:T(8,128)S(1)} copy-done((f32[4,8,16,16,128]{4,3,2,1,0:T(8,128)S(1)}, f32[4,8,16,16,128]{4,3,2,1,0:T(8,128)}, u32[]{:S(2)}) %copy-start) | copy-done | bytes 4194328
  2.9 0.8 faces.3
  3.8 1.4 %collective-permute-start = (f32[4,8,16,128]{3,2,1,0:T(8,128)S(1)}, f32[4,8,16,128]{3,2,1,0:T(8,128)S(1)}, u32[]{:S(2)}, u32[]{:S(2)}) collective-permute-start(f32[4,8,16,128]{3,2,1,0:T(8,128)S(1)} %get-tuple-element.33), channel_id=1, source_target_pairs={{0,1},{1,2},{2,3},{4,5},{5,6},{6,7},{8,9},{9,10},{10,11},{12,13},{... | collective-permute-start | bytes 786440 | tf_op jit(solution)/shard_map/ppermute | solution.py:433
  5.2 4.6 %collective-permute-start.1 = (f32[4,8,16,128]{3,2,1,0:T(8,128)S(1)}, f32[4,8,16,128]{3,2,1,0:T(8,128)S(1)}, u32[]{:S(2)}, u32[]{:S(2)}) collective-permute-start(f32[4,8,16,128]{3,2,1,0:T(8,128)S(1)} %get-tuple-element.34), channel_id=1, source_target_pairs={{1,0},{2,1},{3,2},{5,4},{6,5},{7,6},{9,8},{10,9},{11,10},{13,12},{... | collective-permute-start | bytes 786440 | tf_op jit(solution)/shard_map/ppermute | solution.py:433
  9.8 1.9 %collective-permute-start.2 = (f32[4,256,128]{2,1,0:T(8,128)S(1)}, f32[4,256,128]{2,1,0:T(8,128)S(1)}, u32[]{:S(2)}, u32[]{:S(2)}) collective-permute-start(f32[4,256,128]{2,1,0:T(8,128)S(1)} %get-tuple-element.36), channel_id=1, source_target_pairs={{0,4},{4,8},{8,12},{12,16},{16,20},{20,24},{24,28},{28,32},{32,36}... | collective-permute-start | bytes 1572872 | tf_op jit(solution)/shard_map/ppermute | solution.py:433
  11.7 6.0 %collective-permute-start.3 = (f32[4,256,128]{2,1,0:T(8,128)S(1)}, f32[4,256,128]{2,1,0:T(8,128)S(1)}, u32[]{:S(2)}, u32[]{:S(2)}) collective-permute-start(f32[4,256,128]{2,1,0:T(8,128)S(1)} %get-tuple-element.37), channel_id=1, source_target_pairs={{4,0},{8,4},{12,8},{16,12},{20,16},{24,20},{28,24},{32,28},{36,32}... | collective-permute-start | bytes 1572872 | tf_op jit(solution)/shard_map/ppermute | solution.py:433
  17.8 0.7 broadcast_divide_fusion
  18.5 1.7 %broadcast_in_dim.7 = f32[4,8,256]{2,1,0:T(8,128)} reshape(f32[4,8,16,16]{3,2,1,0:T(8,128)} %broadcast_divide_fusion) | data formatting | bytes 65536 | tf_op jit(solution)/shard_map/broadcast_in_dim | solution.py:445
  20.2 2.0 %broadcast_in_dim.8.relaxed = f32[4,8,256,128]{3,2,1,0:T(8,128)S(1)} broadcast(f32[4,8,256]{2,1,0:T(8,128)} %broadcast_in_dim.7), dimensions={0,1,2} | broadcast | bytes 4227072 | tf_op jit(solution)/shard_map/broadcast_in_dim | solution.py:445
  22.4 2.2 %copy-done.2 = f32[4,8,16,16,128]{4,3,2,1,0:T(8,128)S(1)} copy-done((f32[4,8,16,16,128]{4,3,2,1,0:T(8,128)S(1)}, f32[4,8,16,16,128]{4,3,2,1,0:T(8,128)}, u32[]{:S(2)}) %copy-start.2) | copy-done | bytes 4194328
  24.6 0.8 copy-done.4
  25.4 0.8 copy-done.5
  26.3 13.7 %first.1 = (f32[4,8,256,128]{3,2,1,0:T(8,128)S(1)}, f32[4,8,256,128]{3,2,1,0:T(8,128)S(1)}, bf16[1024,256]{1,0:T(8,128)(2,1)S(1)}, bf16[256,768]{1,0:T(8,128)(2,1)S(1)}, bf16[256,256]{1,0:T(8,128)(2,1)S(1)}) custom-call(s32[2]{0:T(128)S(1)} %pad_add_fusion.info, f32[4,8,256,128]{3,2,1,0:T(8,128)S(1)} %bitcast.9, f32[4,8,256,128]{3,2,1,0:T(8,128)S(1)} %bitcast.10, ...), custom_call_target="tpu_custom_call" | custom-call | flops 10000000000 | tf_op jit(solution)/shard_map/first/pallas_call | solution.py:204
  40.0 0.8 halo_inner.2
  40.8 1.3 %collective-permute-start.4 = (f32[768,128]{1,0:T(8,128)S(1)}, f32[768,128]{1,0:T(8,128)S(1)}, u32[]{:S(2)}, u32[]{:S(2)}) collective-permute-start(f32[768,128]{1,0:T(8,128)S(1)} %get-tuple-element.39), channel_id=1, source_target_pairs={{128,0},{129,1},{130,2},{131,3},{132,4},{133,5},{134,6},{135,7},{1... | collective-permute-start | bytes 1179656 | tf_op jit(solution)/shard_map/ppermute | solution.py:433
  42.2 1.1 %halo_outer.2 = (f32[4,8,256,128]{3,2,1,0:T(8,128)S(1)}, f32[256,128]{1,0:T(8,128)S(1)}) custom-call(s32[2]{0:T(128)S(1)} %pad_add_fusion.info, f32[4,8,256,128]{3,2,1,0:T(8,128)S(1)} %get-tuple-element.35.pred, f32[4,8,256,128]{3,2,1,0:T(8,128)S(1)} %broadcast_in_dim.8.relaxed, ...), custom_call_target="tpu_custom_call", output_to_operand_aliasing={{0}: (1, {})} | custom-call | flops 2000000000 | tf_op jit(solution)/shard_map/halo_outer/pallas_call | solution.py:337
  43.3 1.3 %collective-permute-start.5 = (f32[256,128]{1,0:T(8,128)S(1)}, f32[256,128]{1,0:T(8,128)S(1)}, u32[]{:S(2)}, u32[]{:S(2)}) collective-permute-start(f32[256,128]{1,0:T(8,128)S(1)} %get-tuple-element.40), channel_id=1, source_target_pairs={{128,0},{129,1},{130,2},{131,3},{132,4},{133,5},{134,6},{135,7},{1... | collective-permute-start | bytes 393224 | tf_op jit(solution)/shard_map/ppermute | solution.py:433
  44.6 9.6 %collective-permute-done.4.trace = f32[768,128]{1,0:T(8,128)S(1)} collective-permute-done((f32[768,128]{1,0:T(8,128)S(1)}, f32[768,128]{1,0:T(8,128)S(1)}, u32[]{:S(2)}, u32[]{:S(2)}) %collective-permute-start.4) | collective-permute-done | bytes 393248 | tf_op jit(solution)/shard_map/ppermute | solution.py:433
  54.2 1.8 %late_inner.1.field = f32[4,8,256,128]{3,2,1,0:T(8,128)S(1)} custom-call(s32[2]{0:T(128)S(1)} %pad_add_fusion.info, f32[4,8,256,128]{3,2,1,0:T(8,128)S(1)} %get-tuple-element.38.field, f32[4,8,256,128]{3,2,1,0:T(8,128)S(1)} %broadcast_in_dim.8.relaxed, bf16[256,256]{1,0:T(8,128)(2,1)S(1)} %get-tuple-element.32.carry, ...), custom_call_target="tpu_custom_call", output_to_operand_aliasing={{}: (1, {})} | custom-call | flops 2000000000 | tf_op jit(solution)/shard_map/late_inner/pallas_call | solution.py:371
  56.0 1.3 %late_outer.1 = (f32[4,8,256,128]{3,2,1,0:T(8,128)S(1)}, f32[4,256,128]{2,1,0:T(8,128)S(1)}, f32[4,256,128]{2,1,0:T(8,128)S(1)}, f32[4,8,16,128]{3,2,1,0:T(8,128)S(1)}, f32[4,8,16,128]{3,2,1,0:T(8,128)S(1)}) custom-call(s32[2]{0:T(128)S(1)} %pad_add_fusion.info, f32[4,8,256,128]{3,2,1,0:T(8,128)S(1)} %late_inner.1.field, ...), custom_call_target="tpu_custom_call", output_to_operand_aliasing={{0}: (1, {})} | custom-call | flops 2000000000 | tf_op jit(solution)/shard_map/late_outer/pallas_call | solution.py:371
  57.3 1.3 %collective-permute-start.6 = (f32[4,8,16,128]{3,2,1,0:T(8,128)S(1)}, f32[4,8,16,128]{3,2,1,0:T(8,128)S(1)}, u32[]{:S(2)}, u32[]{:S(2)}) collective-permute-start(f32[4,8,16,128]{3,2,1,0:T(8,128)S(1)} %get-tuple-element.44), channel_id=1, source_target_pairs={{0,1},{1,2},{2,3},{4,5},{5,6},{6,7},{8,9},{9,10},{10,11},{12,13},{... | collective-permute-start | bytes 786440 | tf_op jit(solution)/shard_map/ppermute | solution.py:433
  58.6 4.6 %collective-permute-start.7 = (f32[4,8,16,128]{3,2,1,0:T(8,128)S(1)}, f32[4,8,16,128]{3,2,1,0:T(8,128)S(1)}, u32[]{:S(2)}, u32[]{:S(2)}) collective-permute-start(f32[4,8,16,128]{3,2,1,0:T(8,128)S(1)} %get-tuple-element.45), channel_id=1, source_target_pairs={{1,0},{2,1},{3,2},{5,4},{6,5},{7,6},{9,8},{10,9},{11,10},{13,12},{... | collective-permute-start | bytes 786440 | tf_op jit(solution)/shard_map/ppermute | solution.py:433
  63.1 1.9 %collective-permute-start.8 = (f32[4,256,128]{2,1,0:T(8,128)S(1)}, f32[4,256,128]{2,1,0:T(8,128)S(1)}, u32[]{:S(2)}, u32[]{:S(2)}) collective-permute-start(f32[4,256,128]{2,1,0:T(8,128)S(1)} %get-tuple-element.47), channel_id=1, source_target_pairs={{0,4},{4,8},{8,12},{12,16},{16,20},{20,24},{24,28},{28,32},{32,36}... | collective-permute-start | bytes 1572872 | tf_op jit(solution)/shard_map/ppermute | solution.py:433
  65.1 6.2 %collective-permute-start.9 = (f32[4,256,128]{2,1,0:T(8,128)S(1)}, f32[4,256,128]{2,1,0:T(8,128)S(1)}, u32[]{:S(2)}, u32[]{:S(2)}) collective-permute-start(f32[4,256,128]{2,1,0:T(8,128)S(1)} %get-tuple-element.48), channel_id=1, source_target_pairs={{4,0},{8,4},{12,8},{16,12},{20,16},{24,20},{28,24},{32,28},{36,32}... | collective-permute-start | bytes 1572872 | tf_op jit(solution)/shard_map/ppermute | solution.py:433
  71.3 10.1 %next.1.pred = f32[4,8,256,128]{3,2,1,0:T(8,128)S(1)} custom-call(f32[4,8,256,128]{3,2,1,0:T(8,128)S(1)} %get-tuple-element.41.adjoint, f32[4,8,256,128]{3,2,1,0:T(8,128)S(1)} %get-tuple-element.42.loads, f32[4,8,256,128]{3,2,1,0:T(8,128)S(1)} %broadcast_in_dim.8.relaxed, bf16[1024,256]{1,0:T(8,128)(2,1)S(1)} %get-tuple-element.31.lateral, ...), custom_call_target="tpu_custom_call" | custom-call | flops 8000000000 | tf_op jit(solution)/shard_map/next/pallas_call | solution.py:252
  81.5 0.8 halo_inner.3
  82.3 1.3 %collective-permute-start.10 = (f32[768,128]{1,0:T(8,128)S(1)}, f32[768,128]{1,0:T(8,128)S(1)}, u32[]{:S(2)}, u32[]{:S(2)}) collective-permute-start(f32[768,128]{1,0:T(8,128)S(1)} %get-tuple-element.50), channel_id=1, source_target_pairs={{128,0},{129,1},{130,2},{131,3},{132,4},{133,5},{134,6},{135,7},{1... | collective-permute-start | bytes 1179656 | tf_op jit(solution)/shard_map/ppermute | solution.py:433
  83.6 1.1 %halo_outer.3 = (f32[4,8,256,128]{3,2,1,0:T(8,128)S(1)}, f32[256,128]{1,0:T(8,128)S(1)}) custom-call(s32[2]{0:T(128)S(1)} %pad_add_fusion.info, f32[4,8,256,128]{3,2,1,0:T(8,128)S(1)} %get-tuple-element.46.pred, f32[4,8,256,128]{3,2,1,0:T(8,128)S(1)} %broadcast_in_dim.8.relaxed, ...), custom_call_target="tpu_custom_call", output_to_operand_aliasing={{0}: (1, {})} | custom-call | flops 2000000000 | tf_op jit(solution)/shard_map/halo_outer/pallas_call | solution.py:337
  84.7 1.3 %collective-permute-start.11 = (f32[256,128]{1,0:T(8,128)S(1)}, f32[256,128]{1,0:T(8,128)S(1)}, u32[]{:S(2)}, u32[]{:S(2)}) collective-permute-start(f32[256,128]{1,0:T(8,128)S(1)} %get-tuple-element.52), channel_id=1, source_target_pairs={{128,0},{129,1},{130,2},{131,3},{132,4},{133,5},{134,6},{135,7},{1... | collective-permute-start | bytes 393224 | tf_op jit(solution)/shard_map/ppermute | solution.py:433
  86.0 10.1 %collective-permute-done.10.trace = f32[768,128]{1,0:T(8,128)S(1)} collective-permute-done((f32[768,128]{1,0:T(8,128)S(1)}, f32[768,128]{1,0:T(8,128)S(1)}, u32[]{:S(2)}, u32[]{:S(2)}) %collective-permute-start.10) | collective-permute-done | bytes 393248 | tf_op jit(solution)/shard_map/ppermute | solution.py:433
  96.1 3.5 %last_inner.1 = (f32[4,8,256,128]{3,2,1,0:T(8,128)S(1)}, f32[4,8,256,128]{3,2,1,0:T(8,128)}) custom-call(s32[2]{0:T(128)S(1)} %pad_add_fusion.info, f32[4,8,256,128]{3,2,1,0:T(8,128)S(1)} %get-tuple-element.49.field, f32[4,8,256,128]{3,2,1,0:T(8,128)S(1)} %broadcast_in_dim.8.relaxed, ...), custom_call_target="tpu_custom_call", output_to_operand_aliasing={{0}: (1, {})} | custom-call | flops 3000000000 | tf_op jit(solution)/shard_map/last_inner/pallas_call | solution.py:403
  99.6 2.2 %last_outer.1 = (f32[4,8,256,128]{3,2,1,0:T(8,128)S(1)}, f32[4,8,256,128]{3,2,1,0:T(8,128)}) custom-call(s32[2]{0:T(128)S(1)} %pad_add_fusion.info, f32[4,8,256,128]{3,2,1,0:T(8,128)S(1)} %get-tuple-element.51.field, f32[4,8,256,128]{3,2,1,0:T(8,128)S(1)} %broadcast_in_dim.8.relaxed, ...), custom_call_target="tpu_custom_call", output_to_operand_aliasing={{0}: (1, {}), {1}: (5, {})} | custom-call | flops 2000000000 | tf_op jit(solution)/shard_map/last_outer/pallas_call | solution.py:417
  (23 shorter events, 0.3 us)
Async XLA Ops:
  0.7 2.2 %copy-start = (f32[4,8,16,16,128]{4,3,2,1,0:T(8,128)S(1)}, f32[4,8,16,16,128]{4,3,2,1,0:T(8,128)}, u32[]{:S(2)}) copy-start(f32[4,8,16,16,128]{4,3,2,1,0:T(8,128)} %param.9) | copy-start | bytes 12582916
  2.9 14.8 %copy-start.7 = (f32[4,8,16,16]{3,2,1,0:T(8,128)S(1)}, f32[4,8,16,16]{3,2,1,0:T(8,128)}, u32[]{:S(2)}) copy-start(f32[4,8,16,16]{3,2,1,0:T(8,128)} %param.10) | copy-start | bytes 98308
  3.8 18.5 %copy-start.3 = (f32[6,128,128]{2,1,0:T(8,128)S(1)}, f32[6,128,128]{2,1,0:T(8,128)}, u32[]{:S(2)}) copy-start(f32[6,128,128]{2,1,0:T(8,128)} %faces.2) | copy-start | bytes 1179652
  3.8 36.2 %collective-permute-start = (f32[4,8,16,128]{3,2,1,0:T(8,128)S(1)}, f32[4,8,16,128]{3,2,1,0:T(8,128)S(1)}, u32[]{:S(2)}, u32[]{:S(2)}) collective-permute-start(f32[4,8,16,128]{3,2,1,0:T(8,128)S(1)} %get-tuple-element.33), channel_id=1, source_target_pairs={{0,1},{1,2},{2,3},{4,5},{5,6},{6,7},{8,9},{9,10},{10,11},{12,13},{... | collective-permute-start | bytes 786440 | tf_op jit(solution)/shard_map/ppermute | solution.py:433
  5.2 34.8 %collective-permute-start.1 = (f32[4,8,16,128]{3,2,1,0:T(8,128)S(1)}, f32[4,8,16,128]{3,2,1,0:T(8,128)S(1)}, u32[]{:S(2)}, u32[]{:S(2)}) collective-permute-start(f32[4,8,16,128]{3,2,1,0:T(8,128)S(1)} %get-tuple-element.34), channel_id=1, source_target_pairs={{1,0},{2,1},{3,2},{5,4},{6,5},{7,6},{9,8},{10,9},{11,10},{13,12},{... | collective-permute-start | bytes 786440 | tf_op jit(solution)/shard_map/ppermute | solution.py:433
  9.8 32.4 %collective-permute-start.2 = (f32[4,256,128]{2,1,0:T(8,128)S(1)}, f32[4,256,128]{2,1,0:T(8,128)S(1)}, u32[]{:S(2)}, u32[]{:S(2)}) collective-permute-start(f32[4,256,128]{2,1,0:T(8,128)S(1)} %get-tuple-element.36), channel_id=1, source_target_pairs={{0,4},{4,8},{8,12},{12,16},{16,20},{20,24},{24,28},{28,32},{32,36}... | collective-permute-start | bytes 1572872 | tf_op jit(solution)/shard_map/ppermute | solution.py:433
  11.7 30.5 %collective-permute-start.3 = (f32[4,256,128]{2,1,0:T(8,128)S(1)}, f32[4,256,128]{2,1,0:T(8,128)S(1)}, u32[]{:S(2)}, u32[]{:S(2)}) collective-permute-start(f32[4,256,128]{2,1,0:T(8,128)S(1)} %get-tuple-element.37), channel_id=1, source_target_pairs={{4,0},{8,4},{12,8},{16,12},{20,16},{24,20},{28,24},{32,28},{36,32}... | collective-permute-start | bytes 1572872 | tf_op jit(solution)/shard_map/ppermute | solution.py:433
  20.2 2.2 %copy-start.1 = (f32[4,8,16,16,128]{4,3,2,1,0:T(8,128)S(1)}, f32[4,8,16,16,128]{4,3,2,1,0:T(8,128)}, u32[]{:S(2)}) copy-start(f32[4,8,16,16,128]{4,3,2,1,0:T(8,128)} %param.9) | copy-start | bytes 12582916
  20.2 2.2 %copy-start.6 = (f32[64,128]{1,0:T(8,128)S(1)}, f32[64,128]{1,0:T(8,128)}, u32[]{:S(2)}) copy-start(f32[64,128]{1,0:T(8,128)} %coupling.1) | copy-start | bytes 98308
  22.4 2.2 %copy-start.2 = (f32[4,8,16,16,128]{4,3,2,1,0:T(8,128)S(1)}, f32[4,8,16,16,128]{4,3,2,1,0:T(8,128)}, u32[]{:S(2)}) copy-start(f32[4,8,16,16,128]{4,3,2,1,0:T(8,128)} %param.8) | copy-start | bytes 12582916
  24.6 0.8 copy-start.4
  25.4 0.8 copy-start.5
  40.8 13.3 %collective-permute-start.4 = (f32[768,128]{1,0:T(8,128)S(1)}, f32[768,128]{1,0:T(8,128)S(1)}, u32[]{:S(2)}, u32[]{:S(2)}) collective-permute-start(f32[768,128]{1,0:T(8,128)S(1)} %get-tuple-element.39), channel_id=1, source_target_pairs={{128,0},{129,1},{130,2},{131,3},{132,4},{133,5},{134,6},{135,7},{1... | collective-permute-start | bytes 1179656 | tf_op jit(solution)/shard_map/ppermute | solution.py:433
  43.3 12.7 %collective-permute-start.5 = (f32[256,128]{1,0:T(8,128)S(1)}, f32[256,128]{1,0:T(8,128)S(1)}, u32[]{:S(2)}, u32[]{:S(2)}) collective-permute-start(f32[256,128]{1,0:T(8,128)S(1)} %get-tuple-element.40), channel_id=1, source_target_pairs={{128,0},{129,1},{130,2},{131,3},{132,4},{133,5},{134,6},{135,7},{1... | collective-permute-start | bytes 393224 | tf_op jit(solution)/shard_map/ppermute | solution.py:433
  57.3 24.2 %collective-permute-start.6 = (f32[4,8,16,128]{3,2,1,0:T(8,128)S(1)}, f32[4,8,16,128]{3,2,1,0:T(8,128)S(1)}, u32[]{:S(2)}, u32[]{:S(2)}) collective-permute-start(f32[4,8,16,128]{3,2,1,0:T(8,128)S(1)} %get-tuple-element.44), channel_id=1, source_target_pairs={{0,1},{1,2},{2,3},{4,5},{5,6},{6,7},{8,9},{9,10},{10,11},{12,13},{... | collective-permute-start | bytes 786440 | tf_op jit(solution)/shard_map/ppermute | solution.py:433
  58.6 22.9 %collective-permute-start.7 = (f32[4,8,16,128]{3,2,1,0:T(8,128)S(1)}, f32[4,8,16,128]{3,2,1,0:T(8,128)S(1)}, u32[]{:S(2)}, u32[]{:S(2)}) collective-permute-start(f32[4,8,16,128]{3,2,1,0:T(8,128)S(1)} %get-tuple-element.45), channel_id=1, source_target_pairs={{1,0},{2,1},{3,2},{5,4},{6,5},{7,6},{9,8},{10,9},{11,10},{13,12},{... | collective-permute-start | bytes 786440 | tf_op jit(solution)/shard_map/ppermute | solution.py:433
  63.1 20.4 %collective-permute-start.8 = (f32[4,256,128]{2,1,0:T(8,128)S(1)}, f32[4,256,128]{2,1,0:T(8,128)S(1)}, u32[]{:S(2)}, u32[]{:S(2)}) collective-permute-start(f32[4,256,128]{2,1,0:T(8,128)S(1)} %get-tuple-element.47), channel_id=1, source_target_pairs={{0,4},{4,8},{8,12},{12,16},{16,20},{20,24},{24,28},{28,32},{32,36}... | collective-permute-start | bytes 1572872 | tf_op jit(solution)/shard_map/ppermute | solution.py:433
  65.1 18.5 %collective-permute-start.9 = (f32[4,256,128]{2,1,0:T(8,128)S(1)}, f32[4,256,128]{2,1,0:T(8,128)S(1)}, u32[]{:S(2)}, u32[]{:S(2)}) collective-permute-start(f32[4,256,128]{2,1,0:T(8,128)S(1)} %get-tuple-element.48), channel_id=1, source_target_pairs={{4,0},{8,4},{12,8},{16,12},{20,16},{24,20},{28,24},{32,28},{36,32}... | collective-permute-start | bytes 1572872 | tf_op jit(solution)/shard_map/ppermute | solution.py:433
  82.3 13.8 %collective-permute-start.10 = (f32[768,128]{1,0:T(8,128)S(1)}, f32[768,128]{1,0:T(8,128)S(1)}, u32[]{:S(2)}, u32[]{:S(2)}) collective-permute-start(f32[768,128]{1,0:T(8,128)S(1)} %get-tuple-element.50), channel_id=1, source_target_pairs={{128,0},{129,1},{130,2},{131,3},{132,4},{133,5},{134,6},{135,7},{1... | collective-permute-start | bytes 1179656 | tf_op jit(solution)/shard_map/ppermute | solution.py:433
  84.7 14.9 %collective-permute-start.11 = (f32[256,128]{1,0:T(8,128)S(1)}, f32[256,128]{1,0:T(8,128)S(1)}, u32[]{:S(2)}, u32[]{:S(2)}) collective-permute-start(f32[256,128]{1,0:T(8,128)S(1)} %get-tuple-element.52), channel_id=1, source_target_pairs={{128,0},{129,1},{130,2},{131,3},{132,4},{133,5},{134,6},{135,7},{1... | collective-permute-start | bytes 393224 | tf_op jit(solution)/shard_map/ppermute | solution.py:433
where the time goes:
time: 103 us; the launch traced here: 102 us
  Pallas kernels  37.2 us (36%)
  starting transfers between devices  33.1 us (32%)
  waiting for transfers between devices  19.8 us (19%)
  local copies, waits for them, and re-layouts  9.94 us (10%)
  between operations  1.1 us (1%)
    ppermute x12, starting transfers between devices, shifted(): lax.ppermute(value, axis, [(i, i + step) for i in range(first, last)])  33.1 us
    ppermute x12, waiting for transfers between devices, shifted(): lax.ppermute(value, axis, [(i, i + step) for i in range(first, last)])  19.8 us
    pallas_call x1, Pallas kernels, first_prediction(): pl.pallas_call(first_kernel, out_shape=[VMEM(STACK, F32), VMEM(STACK, F32...  13.7 us
    pallas_call x1, Pallas kernels, next_prediction(): pl.pallas_call(next_kernel, out_shape=VMEM(STACK, F32), in_specs=[INV] *...  10.1 us
    unnamed x16, local copies, waits for them, and re-layouts  6.21 us
    pallas_call x4, Pallas kernels, with_halos(): pl.pallas_call(inner_kernel if inner else outer_kernel, out_shape=[VMEM(S...  3.8 us
    broadcast_in_dim x2, local copies, waits for them, and re-layouts, body(): jnp.broadcast_to((OMEGA / conductance).reshape(NTD, EX, LAYER, 1), STACK)  3.73 us
    pallas_call x1, Pallas kernels, last_inner(): pl.pallas_call(last_inner_kernel, out_shape=[VMEM(STACK, F32), jax.ShapeD...  3.47 us
  transfers between devices with their start and end apart: 12, of which 2 were waited for; matrix products, arithmetic and copies ran while one was open for 4% of the time, Pallas kernels for 32%

commit v1 on v0

v1 whole, which is shorter than its diff:
```python
import functools

import jax
import jax.numpy as jnp
from jax import lax
from jax.experimental import pallas as pl
from jax.experimental.pallas import tpu as pltpu
from jax.sharding import PartitionSpec as P

SWEEPS = 2
OMEGA = 0.7
NTD, EX, EY, EZ, BLOCK = 4, 8, 16, 16, 128
SPACE = BLOCK // 2
LAYER = EY * EZ
F32, BF16 = jnp.float32, jnp.bfloat16
VMEM = pltpu.VMEM
ANY = pl.BlockSpec(memory_space=pl.ANY)
INH = pl.BlockSpec(memory_space=pltpu.HBM)
INV = pl.BlockSpec(memory_space=VMEM)
INS = pl.BlockSpec(memory_space=pltpu.SMEM)
INNER = ((1, 4),)
OUTER = ((0, 1), (5, 3))


def params(mib):
    return pltpu.CompilerParams(vmem_limit_bytes=mib << 20)


def cost(us):
    return pl.CostEstimate(flops=int(us * 1.0e9), bytes_accessed=0, transcendentals=0)


def split(value):
    high = value.astype(BF16)
    low = (value - high.astype(F32)).astype(BF16)
    return high, low


def dot(rows, matrix):
    return jnp.dot(rows, matrix, preferred_element_type=F32)


def both(value):
    return jnp.concatenate(split(value), axis=-1)


def folded(rows, matrix):
    out = dot(rows, matrix)
    return out[:, :BLOCK] + out[:, BLOCK:]


def mask(info, first, rows):
    position = lax.broadcasted_iota(jnp.int32, (rows, BLOCK), 0) + first * LAYER
    return position < info[0]


def near(info, dim):
    return pl.multiple_of(info[3], EZ) if dim else info[2]


def far(info, dim):
    return pl.multiple_of(LAYER - EZ - info[3], EZ) if dim else EX - 1 - info[2]


def faces_kernel(info, initial, x_near, x_far, y_near, y_far, sems):
    places = (near(info, 0), far(info, 0), near(info, 1), far(info, 1))
    refs = (x_near, x_far, y_near, y_far)
    copies = [
        pltpu.make_async_copy(initial.at[:, at] if k < 2 else initial.at[:, :, pl.ds(at, EZ)], ref, sems.at[k])
        for k, (ref, at) in enumerate(zip(refs, places))
    ]
    for copy in copies:
        copy.start()
    for copy, ref, at in zip(copies[:2], refs[:2], places[:2]):
        copy.wait()
        keep = mask(info, at, LAYER)
        for t in range(NTD):
            ref[t] = jnp.where(keep, ref[t], 0.0)
    for copy, ref, at in zip(copies[2:], refs[2:], places[2:]):
        copy.wait()
        for x in range(EX):
            position = lax.broadcasted_iota(jnp.int32, (EZ, BLOCK), 0) + (x * LAYER + at)
            for t in range(NTD):
                ref[t, x] = jnp.where(position < info[0], ref[t, x], 0.0)


FACES = [VMEM((NTD, LAYER, BLOCK), F32)] * 2 + [VMEM((NTD, EX, EZ, BLOCK), F32)] * 2


def faces_of_initial(info, initial):
    return pl.pallas_call(
        faces_kernel,
        out_shape=FACES,
        in_specs=[INS, INH],
        out_specs=[INV] * 4,
        scratch_shapes=[pltpu.SemaphoreType.DMA((4,))],
        compiler_params=params(4),
        cost_estimate=cost(2),
        name="faces",
    )(info, initial)


def stencil_setup(high, low):
    for ref in (high, low):
        for x in (0, EX + 1):
            ref[x] = jnp.zeros(ref.shape[1:], BF16)
        for x in range(1, EX + 1):
            for t in range(NTD):
                ref[x, t, 0:EZ] = jnp.zeros((EZ, BLOCK), BF16)
                ref[x, t, EZ + LAYER :] = jnp.zeros((EZ, BLOCK), BF16)


def stencil_split(x, value, high, low):
    h, l = split(value)
    high[x + 1, :, pl.ds(EZ, LAYER)] = h
    low[x + 1, :, pl.ds(EZ, LAYER)] = l


def flat(value):
    return value.reshape(NTD * LAYER, BLOCK)


def stencil_layer(x, adjoint, high, low, lateral, central):
    pieces = []
    for ref in (high, low):
        pieces += [
            flat(ref[x, :, pl.ds(EZ, LAYER)]),
            flat(ref[x + 2, :, pl.ds(EZ, LAYER)]),
            flat(ref[x + 1, :, pl.ds(0, LAYER)]),
            flat(ref[x + 1, :, pl.ds(2 * EZ, LAYER)]),
        ]
    around = folded(jnp.concatenate(pieces, axis=1), lateral[...])
    own = [flat(ref[x + 1, :, pl.ds(EZ, LAYER)]) for ref in (high, low)]
    out = dot(jnp.concatenate(own, axis=1), central[...])
    own, below, above = (
        out[:, k * BLOCK : (k + 1) * BLOCK] + out[:, (k + 3) * BLOCK : (k + 4) * BLOCK] for k in range(3)
    )
    depth = lax.broadcasted_iota(jnp.int32, (NTD * LAYER, BLOCK), 0) % EZ
    below = jnp.where(depth == 0, 0.0, pltpu.roll(below, 1, 0))
    above = jnp.where(depth == EZ - 1, 0.0, pltpu.roll(above, NTD * LAYER - 1, 0))
    return adjoint - own, around + below + above


STACK = (NTD, EX, LAYER, BLOCK)
PADDED = (EX + 2, NTD, LAYER + 2 * EZ, BLOCK)
LATERAL = (8 * BLOCK, 2 * BLOCK)
CENTRAL = (2 * BLOCK, 6 * BLOCK)
SQUARE = (2 * BLOCK, 2 * BLOCK)


def layers(runs):
    return [x for first, count in runs for x in range(first, first + count)]


def row_factors(conductance, x, relaxed):
    factor = []
    for t in range(NTD):
        inverse = OMEGA / conductance[t, x]
        spread = jnp.broadcast_to(inverse[:, None, :], (EY, EZ, EZ)).reshape(LAYER, EZ)
        lane = lax.broadcasted_iota(jnp.int32, (LAYER, EZ), 1)
        depth = lax.broadcasted_iota(jnp.int32, (LAYER, EZ), 0) % EZ
        column = jnp.sum(jnp.where(lane == depth, spread, 0.0), axis=1, keepdims=True)
        column = jnp.broadcast_to(column, (LAYER, BLOCK))
        relaxed[t, x] = column
        factor.append(column)
    return jnp.concatenate(factor, axis=0)


def predict(x, field, adjoint, loads, relaxed, high, low, lateral, central, given=None, conductance=None):
    if given is None:
        factor, rest = flat(relaxed[:, x]), flat(loads[:, x])
    else:
        factor = row_factors(conductance, x, relaxed)
        rest = factor * folded(both(flat(loads[:, x])), given[...])
        loads[:, x] = rest.reshape(NTD, LAYER, BLOCK)
    own, around = stencil_layer(x, flat(adjoint[:, x]), high, low, lateral, central)
    field[:, x] = (own + rest - factor * around).reshape(NTD, LAYER, BLOCK)


def first_kernel(
    info, initial, forcing, conductance, block_matrix_hbm, precond_hbm, faces_hbm, coupling_hbm,
    field, adjoint, loads, relaxed, high, low, lateral, central, carry, given,
    block_matrix, precond, faces, coupling, sems, small_sems,
):
    small = [
        pltpu.make_async_copy(source, target, small_sems.at[k])
        for k, (source, target) in enumerate(
            [(precond_hbm, precond), (faces_hbm, faces), (block_matrix_hbm, block_matrix), (coupling_hbm, coupling)]
        )
    ]
    for copy in small:
        copy.start()

    def fetch(x, which):
        source, target = ((initial, adjoint), (forcing, loads))[which]
        return pltpu.make_async_copy(source.at[:, x], target.at[:, x], sems.at[which, x])

    order = layers(INNER) + layers(OUTER)
    for which in range(2):
        for x in order:
            fetch(x, which).start()
    stencil_setup(high, low)
    for copy in small:
        copy.wait()

    def matrices(value):
        matrix = jnp.dot(value, precond[...], precision=lax.Precision.HIGHEST, preferred_element_type=F32)
        return split(matrix)

    zero = jnp.zeros((BLOCK, BLOCK), BF16)
    for d in range(4):
        h, l = matrices(faces[d])
        lateral[d * BLOCK : (d + 1) * BLOCK, :] = jnp.concatenate([h, l], axis=1)
        lateral[(d + 4) * BLOCK : (d + 5) * BLOCK, :] = jnp.concatenate([h, zero], axis=1)
    parts = [matrices(OMEGA * block_matrix[...]), matrices(faces[4]), matrices(faces[5])]
    central[0:BLOCK, :] = jnp.concatenate([h for h, _ in parts] + [l for _, l in parts], axis=1)
    central[BLOCK:, :] = jnp.concatenate([h for h, _ in parts] + [zero] * 3, axis=1)
    h, l = matrices(coupling[...])
    none = jnp.zeros((SPACE, 2 * BLOCK), BF16)
    carry[...] = jnp.concatenate(
        [jnp.concatenate([h, l], axis=1), none, jnp.concatenate([h, zero[:SPACE]], axis=1), none], axis=0
    )
    h, l = split(precond[...])
    given[0:BLOCK, :] = jnp.concatenate([h, l], axis=1)
    given[BLOCK:, :] = jnp.concatenate([h, zero], axis=1)

    for x in range(EX):
        fetch(x, 0).wait()
        position = lax.broadcasted_iota(jnp.int32, (NTD, LAYER, BLOCK), 1) + x * LAYER
        value = jnp.where(position < info[0], adjoint[:, x], 0.0)
        adjoint[:, x] = value
        stencil_split(x, value, high, low)
    for x in range(EX):
        fetch(x, 1).wait()
    for x in layers(INNER):
        predict(x, field, adjoint, loads, relaxed, high, low, lateral, central, given, conductance)


def first_prediction(info, initial, forcing, conductance, block_matrix, precond, faces, coupling):
    return pl.pallas_call(
        first_kernel,
        out_shape=[VMEM(STACK, F32)] * 4
        + [VMEM(PADDED, BF16)] * 2
        + [VMEM(LATERAL, BF16), VMEM(CENTRAL, BF16), VMEM(SQUARE, BF16), VMEM(SQUARE, BF16)],
        in_specs=[INS, INH, INH, INV] + [INH] * 4,
        out_specs=[INV] * 10,
        scratch_shapes=[
            pltpu.VMEM((BLOCK, BLOCK), F32),
            pltpu.VMEM((BLOCK, BLOCK), F32),
            pltpu.VMEM((6, BLOCK, BLOCK), F32),
            pltpu.VMEM((SPACE, BLOCK), F32),
            pltpu.SemaphoreType.DMA((2, EX)),
            pltpu.SemaphoreType.DMA((4,)),
        ],
        compiler_params=params(16),
        cost_estimate=cost(8),
        name="first_inner",
    )(info, initial, forcing, conductance, block_matrix, precond, faces, coupling)


def next_kernel(adjoint, loads, relaxed, lateral, central, field, high, low):
    stencil_setup(high, low)
    for x in range(EX):
        stencil_split(x, adjoint[:, x], high, low)
    for x in layers(INNER):
        predict(x, field, adjoint, loads, relaxed, high, low, lateral, central)


def next_prediction(adjoint, loads, relaxed, lateral, central):
    return pl.pallas_call(
        next_kernel,
        out_shape=[VMEM(STACK, F32), VMEM(PADDED, BF16), VMEM(PADDED, BF16)],
        in_specs=[INV] * 5,
        out_specs=[INV] * 3,
        compiler_params=params(16),
        cost_estimate=cost(5),
        name="next_inner",
    )(adjoint, loads, relaxed, lateral, central)


def rows_of(stack, t, runs):
    return jnp.concatenate([stack[t, first : first + count].reshape(count * LAYER, BLOCK) for first, count in runs], axis=0)


def chain(info, field, relaxed, carry, runs, trace):
    keep = jnp.concatenate(
        [
            (lax.broadcasted_iota(jnp.int32, (count * LAYER, BLOCK), 0) + first * LAYER < info[0]).astype(F32)
            for first, count in runs
        ],
        axis=0,
    ) > 0.5
    for t in reversed(range(NTD)):
        value = rows_of(field, t, runs)
        if trace is not None:
            value = value - rows_of(relaxed, t, runs) * folded(both(trace), carry[...])
        trace = jnp.where(keep, value, 0.0)
        at = 0
        for first, count in runs:
            rows = count * LAYER
            field[t, first : first + count] = trace[at : at + rows].reshape(count, LAYER, BLOCK)
            at += rows
    return trace


def packed(trace):
    half = trace.shape[0] // 2
    lane = lax.broadcasted_iota(jnp.int32, (half, BLOCK), 1)
    return jnp.where(lane < SPACE, trace[:half], pltpu.roll(trace[half:], SPACE, 1))


def unpacked(value):
    return jnp.concatenate([value, pltpu.roll(value, SPACE, 1)], axis=0)


def trace_shape(runs):
    return VMEM((len(layers(runs)) * LAYER // 2, BLOCK), F32)


def early_chain(info, field, relaxed, carry, runs, trace):
    @pl.when(info[1] == 1)
    def _():
        trace[...] = packed(chain(info, field, relaxed, carry, runs, None))


def face_matrix(lateral, d):
    top, bottom = pl.multiple_of(d * BLOCK, BLOCK), pl.multiple_of((d + 4) * BLOCK, BLOCK)
    return jnp.concatenate([lateral[pl.ds(top, BLOCK), :], lateral[pl.ds(bottom, BLOCK), :]], axis=0)


def inner_kernel(info, pred, relaxed, lateral, carry, y_near, y_far, field, trace):
    ((first, count),) = INNER
    for halo, at in ((y_near, near(info, 1)), (y_far, far(info, 1))):
        matrix = face_matrix(lateral, 2 + (at > 0).astype(jnp.int32))
        values = halo[:, first : first + count].reshape(NTD * count * EZ, BLOCK)
        term = folded(both(values), matrix).reshape(NTD, count, EZ, BLOCK)
        area = (slice(None), pl.ds(first, count), pl.ds(at, EZ))
        field[area] = field[area] - relaxed[area] * term
    early_chain(info, field, relaxed, carry, INNER, trace)


def inner_halos(info, field, relaxed, lateral, carry, y_halos):
    return pl.pallas_call(
        inner_kernel,
        out_shape=[VMEM(STACK, F32), trace_shape(INNER)],
        in_specs=[INS] + [INV] * 6,
        out_specs=[INV, INV],
        input_output_aliases={1: 0},
        compiler_params=params(8),
        cost_estimate=cost(2),
        name="inner_halos",
    )(info, field, relaxed, lateral, carry, *y_halos)


def outer_kernel(first_sweep, info, *refs):
    if first_sweep:
        conductance, given, *refs = refs
        (_, _, _, _, _, adjoint, lateral, central, carry, x_near, x_far, y_near, y_far,
         field, high, low, loads, relaxed, trace) = refs
    else:
        conductance = given = None
        (_, _, _, adjoint, lateral, central, carry, x_near, x_far, y_near, y_far, loads, relaxed,
         field, high, low, trace) = refs
    for halo, x in ((x_near, near(info, 0)), (x_far, far(info, 0))):
        h, l = split(halo[...])
        place = jnp.where(x > 0, EX + 1, 0)
        high[place, :, pl.ds(EZ, LAYER)] = h
        low[place, :, pl.ds(EZ, LAYER)] = l
    for halo, y in ((y_near, near(info, 1)), (y_far, far(info, 1))):
        place = pl.multiple_of(jnp.where(y > 0, LAYER + EZ, 0), EZ)
        for x in layers(OUTER):
            h, l = split(halo[:, x])
            high[x + 1, :, pl.ds(place, EZ)] = h
            low[x + 1, :, pl.ds(place, EZ)] = l
    for x in layers(OUTER):
        predict(x, field, adjoint, loads, relaxed, high, low, lateral, central, given, conductance)
    early_chain(info, field, relaxed, carry, OUTER, trace)


def outer_prediction(info, field, high, low, adjoint, lateral, central, carry, halos, loads, relaxed, given, conductance):
    first_sweep = given is not None
    if first_sweep:
        args = [info, conductance, given, field, high, low, loads, relaxed, adjoint, lateral, central, carry, *halos]
        outs = [VMEM(STACK, F32), VMEM(PADDED, BF16), VMEM(PADDED, BF16), VMEM(STACK, F32), VMEM(STACK, F32)]
        aliases = {k + 3: k for k in range(5)}
    else:
        args = [info, field, high, low, adjoint, lateral, central, carry, *halos, loads, relaxed]
        outs = [VMEM(STACK, F32), VMEM(PADDED, BF16), VMEM(PADDED, BF16)]
        aliases = {k + 1: k for k in range(3)}
    outs = outs + [trace_shape(OUTER)]
    out = pl.pallas_call(
        functools.partial(outer_kernel, first_sweep),
        out_shape=outs,
        in_specs=[INS] + [INV] * (len(args) - 1),
        out_specs=[INV] * len(outs),
        input_output_aliases=aliases,
        compiler_params=params(16),
        cost_estimate=cost(7),
        name="first_outer" if first_sweep else "next_outer",
    )(*args)
    if first_sweep:
        loads, relaxed = out[3:5]
    return out[0], out[-1], loads, relaxed


def late_chain(info, field, relaxed, carry, trace, runs):
    @pl.when(info[1] == 0)
    def _():
        chain(info, field, relaxed, carry, runs, unpacked(trace[...]))


def late_inner_kernel(info, field, relaxed, carry, trace, out):
    late_chain(info, out, relaxed, carry, trace, INNER)


def late_outer_kernel(info, field, relaxed, carry, trace, out, x_near, x_far, y_near, y_far):
    late_chain(info, out, relaxed, carry, trace, OUTER)
    x_near[...] = out[:, near(info, 0)]
    x_far[...] = out[:, far(info, 0)]
    y_near[...] = out[:, :, pl.ds(near(info, 1), EZ)]
    y_far[...] = out[:, :, pl.ds(far(info, 1), EZ)]


def after_trace(info, field, relaxed, carry, trace, inner):
    outs = [VMEM(STACK, F32)] + ([] if inner else FACES)
    return pl.pallas_call(
        late_inner_kernel if inner else late_outer_kernel,
        out_shape=outs,
        in_specs=[INS] + [INV] * 4,
        out_specs=[INV] * len(outs),
        input_output_aliases={1: 0},
        compiler_params=params(8),
        cost_estimate=cost(2),
        name="late_inner" if inner else "late_outer",
    )(info, field, relaxed, carry, trace)


def finish(runs, kept, out, sems):
    copies = [
        pltpu.make_async_copy(kept.at[:, pl.ds(first, count)], out.at[:, pl.ds(first, count)], sems.at[k])
        for k, (first, count) in enumerate(runs)
    ]
    for copy in copies:
        copy.start()
    for copy in copies:
        copy.wait()


def last_inner_kernel(info, field, relaxed, carry, trace, kept, out, sems):
    late_chain(info, kept, relaxed, carry, trace, INNER)
    finish(INNER, kept, out, sems)


def last_outer_kernel(info, field, relaxed, carry, trace, given, kept, out, sems):
    late_chain(info, kept, relaxed, carry, trace, OUTER)
    finish(OUTER, kept, out, sems)


def last(info, field, relaxed, carry, trace, given):
    inner = given is None
    args = [info, field, relaxed, carry, trace] + ([] if inner else [given])
    return pl.pallas_call(
        last_inner_kernel if inner else last_outer_kernel,
        out_shape=[VMEM(STACK, F32), pltpu.HBM(STACK, F32)],
        in_specs=[INS] + [INV] * 4 + ([] if inner else [INH]),
        out_specs=[INV, INH],
        input_output_aliases={1: 0} if inner else {1: 0, 5: 1},
        scratch_shapes=[pltpu.SemaphoreType.DMA((2,))],
        compiler_params=params(8),
        cost_estimate=cost(3),
        name="last_inner" if inner else "last_outer",
    )(*args)


def exchanged(value, axis, first):
    count = lax.axis_size(axis)
    pairs = [(i, i + 1) for i in range(first, count - 1, 2)]
    return lax.ppermute(value, axis, pairs + [(j, i) for i, j in pairs])


def sent_back(value):
    return lax.ppermute(value, "tm", [(1, 0)])


def body(forcing, initial, conductance, counts, block_matrix, precond, face_coupling, time_coupling):
    shape = forcing.shape
    in_hbm = functools.partial(pltpu.with_memory_space_constraint, memory_space=pltpu.HBM)
    forcing, initial = in_hbm(forcing.reshape(STACK)), in_hbm(initial.reshape(STACK))
    block_matrix, precond, face_coupling, time_coupling = map(
        in_hbm, (block_matrix, precond, face_coupling, time_coupling)
    )
    even_x = 1 - lax.rem(lax.axis_index("sx"), 2).astype(jnp.int32)
    even_y = 1 - lax.rem(lax.axis_index("sy"), 2).astype(jnp.int32)
    info = jnp.stack(
        [counts[0, 0], lax.axis_index("tm").astype(jnp.int32), even_x * (EX - 1), even_y * (LAYER - EZ)]
    )

    def halos_of(x_near, x_far, y_near, y_far):
        return (
            exchanged(x_near, "sx", 0), exchanged(x_far, "sx", 1),
            exchanged(y_near, "sy", 0), exchanged(y_far, "sy", 1),
        )

    halos = halos_of(*faces_of_initial(info, initial))
    field, adjoint, loads, relaxed, high, low, lateral, central, carry, given = first_prediction(
        info, initial, forcing, conductance, block_matrix, precond, face_coupling, time_coupling
    )
    for sweep in range(SWEEPS):
        if sweep:
            adjoint, given = field, None
            field, high, low = next_prediction(adjoint, loads, relaxed, lateral, central)
        field, inner = inner_halos(info, field, relaxed, lateral, carry, halos[2:])
        inner = sent_back(inner)
        field, outer, loads, relaxed = outer_prediction(
            info, field, high, low, adjoint, lateral, central, carry, halos, loads, relaxed, given, conductance
        )
        outer = sent_back(outer)
        if sweep < SWEEPS - 1:
            (field,) = after_trace(info, field, relaxed, carry, inner, True)
            field, *faces = after_trace(info, field, relaxed, carry, outer, False)
            halos = halos_of(*faces)
        else:
            field, out = last(info, field, relaxed, carry, inner, None)
            field, out = last(info, field, relaxed, carry, outer, out)
    return out.reshape(shape)


def solution(mesh):
    in_specs = (
        P("tm", "sx", "sy", None, None),
        P("tm", "sx", "sy", None, None),
        P("tm", "sx", "sy", None),
        P("sx", "sy"),
        P(),
        P(),
        P(),
        P(),
    )
    out_specs = P("tm", "sx", "sy", None, None)
    return jax.shard_map(body, mesh=mesh, in_specs=in_specs, out_specs=out_specs, check_vma=False)
```

time: 103 us -> 83.1 us (0.81)
  the two profiles are of different devices: /device:TPU:120 before, /device:TPU:241 now
where the time goes in v1:
time: 83.1 us; the launch traced here: 82.8 us
  Pallas kernels  39.1 us (47%)
  starting transfers between devices  22 us (26%)
  waiting for transfers between devices  20.5 us (25%)
  between operations  1.1 us (1%)
    ppermute x8, starting transfers between devices, exchanged(): return lax.ppermute(value, axis, pairs + [(j, i) for i, j in pairs])  16.7 us
    ppermute x4, waiting for transfers between devices, sent_back(): return lax.ppermute(value, 'tm', [(1, 0)])  12 us
    pallas_call x1, Pallas kernels, first_prediction(): pl.pallas_call(first_kernel, out_shape=[VMEM(STACK, F32)] * 4 + [VMEM(PAD...  11.2 us
    pallas_call x2, Pallas kernels, outer_prediction(): pl.pallas_call(functools.partial(outer_kernel, first_sweep), out_shape=ou...  10.8 us
    ppermute x8, waiting for transfers between devices, exchanged(): return lax.ppermute(value, axis, pairs + [(j, i) for i, j in pairs])  8.51 us
    pallas_call x2, Pallas kernels, last(): pl.pallas_call(last_inner_kernel if inner else last_outer_kernel, out_sha...  5.64 us
    ppermute x4, starting transfers between devices, sent_back(): return lax.ppermute(value, 'tm', [(1, 0)])  5.35 us
    pallas_call x1, Pallas kernels, next_prediction(): pl.pallas_call(next_kernel, out_shape=[VMEM(STACK, F32), VMEM(PADDED, BF1...  4.84 us
  transfers between devices with their start and end apart: 12, of which 4 were waited for; matrix products, arithmetic and copies ran while one was open for 0% of the time, Pallas kernels for 40%

profile of v1, /device:TPU:241, one launch (start us, length us, event | category | flops | bytes accessed | tf_op | source)
XLA Modules:
  0.0 82.8 jit_solution(9415762418975872748)
XLA Ops:
  0.7 0.1 pad_add_fusion.info
  0.8 1.9 %faces.1 = (f32[4,256,128]{2,1,0:T(8,128)S(1)}, f32[4,256,128]{2,1,0:T(8,128)S(1)}, f32[4,8,16,128]{3,2,1,0:T(8,128)S(1)}, f32[4,8,16,128]{3,2,1,0:T(8,128)S(1)}) custom-call(s32[4]{0:T(128)S(1)} %pad_add_fusion.info, f32[4,8,256,128]{3,2,1,0:T(8,128)} %bitcast.8), custom_call_target="tpu_custom_call" | custom-call | flops 2000000000 | tf_op jit(solution)/shard_map/faces/pallas_call | solution.py:91
  2.7 1.1 %collective-permute-start = (f32[4,8,16,128]{3,2,1,0:T(8,128)S(1)}, f32[4,8,16,128]{3,2,1,0:T(8,128)S(1)}, u32[]{:S(2)}, u32[]{:S(2)}) collective-permute-start(f32[4,8,16,128]{3,2,1,0:T(8,128)S(1)} %get-tuple-element.45), channel_id=1, source_target_pairs={{0,1},{2,3},{1,0},{3,2},{4,5},{6,7},{5,4},{7,6},{8,9},{10,11},{9,8... | collective-permute-start | bytes 786440 | tf_op jit(solution)/shard_map/ppermute | solution.py:478
  3.8 1.9 %collective-permute-start.1 = (f32[4,8,16,128]{3,2,1,0:T(8,128)S(1)}, f32[4,8,16,128]{3,2,1,0:T(8,128)S(1)}, u32[]{:S(2)}, u32[]{:S(2)}) collective-permute-start(f32[4,8,16,128]{3,2,1,0:T(8,128)S(1)} %get-tuple-element.46), channel_id=1, source_target_pairs={{1,2},{2,1},{5,6},{6,5},{9,10},{10,9},{13,14},{14,13},{17,18},{18,... | collective-permute-start | bytes 786440 | tf_op jit(solution)/shard_map/ppermute | solution.py:478
  5.7 1.0 %collective-permute-start.2 = (f32[4,256,128]{2,1,0:T(8,128)S(1)}, f32[4,256,128]{2,1,0:T(8,128)S(1)}, u32[]{:S(2)}, u32[]{:S(2)}) collective-permute-start(f32[4,256,128]{2,1,0:T(8,128)S(1)} %get-tuple-element.53), channel_id=1, source_target_pairs={{0,4},{8,12},{16,20},{24,28},{32,36},{40,44},{48,52},{56,60},{64,6... | collective-permute-start | bytes 1572872 | tf_op jit(solution)/shard_map/ppermute | solution.py:478
  6.8 4.6 %collective-permute-start.3 = (f32[4,256,128]{2,1,0:T(8,128)S(1)}, f32[4,256,128]{2,1,0:T(8,128)S(1)}, u32[]{:S(2)}, u32[]{:S(2)}) collective-permute-start(f32[4,256,128]{2,1,0:T(8,128)S(1)} %get-tuple-element.54), channel_id=1, source_target_pairs={{4,8},{12,16},{20,24},{28,32},{36,40},{44,48},{52,56},{60,64},{68,... | collective-permute-start | bytes 1572872 | tf_op jit(solution)/shard_map/ppermute | solution.py:478
  11.3 11.2 %first_inner.1 = (f32[4,8,256,128]{3,2,1,0:T(8,128)S(1)}, f32[4,8,256,128]{3,2,1,0:T(8,128)S(1)}, f32[4,8,256,128]{3,2,1,0:T(8,128)S(1)}, f32[4,8,256,128]{3,2,1...) custom-call(s32[4]{0:T(128)S(1)} %pad_add_fusion.info, ...), custom_call_target="tpu_custom_call" | custom-call | flops 8000000000 | tf_op jit(solution)/shard_map/first_inner/pallas_call | solution.py:240
  22.6 0.0 collective-permute-done.y_near.refs_13_
  22.6 0.0 collective-permute-done.1.y_far.refs_14_
  22.6 0.8 inner_halos.2
  23.4 1.5 %collective-permute-start.4 = (f32[512,128]{1,0:T(8,128)S(1)}, f32[512,128]{1,0:T(8,128)S(1)}, u32[]{:S(2)}, u32[]{:S(2)}) collective-permute-start(f32[512,128]{1,0:T(8,128)S(1)} %get-tuple-element.57), channel_id=1, source_target_pairs={{128,0},{129,1},{130,2},{131,3},{132,4},{133,5},{134,6},{135,7},{1... | collective-permute-start | bytes 786440 | tf_op jit(solution)/shard_map/ppermute | solution.py:482
  24.9 0.0 collective-permute-done.3.refs_12_
  24.9 5.8 %first_outer.1 = (f32[4,8,256,128]{3,2,1,0:T(8,128)S(1)}, bf16[10,4,288,128]{3,2,1,0:T(8,128)(2,1)S(1)}, bf16[10,4,288,128]{3,2,1,0:T(8,128)(2,1)S(1)}, f32[4,8,...) custom-call(s32[4]{0:T(128)S(1)} %pad_add_fusion.info, ...), custom_call_target="tpu_custom_call", output_to_operand_aliasing={{0}: (3, {}), {1}: (4, {}), {2}: (5, {}), {3}: (6, {}), {4}... | custom-call | flops 7000000000 | tf_op jit(solution)/shard_map/first_outer/pallas_call | solution.py:391
  30.7 1.3 %collective-permute-start.5 = (f32[512,128]{1,0:T(8,128)S(1)}, f32[512,128]{1,0:T(8,128)S(1)}, u32[]{:S(2)}, u32[]{:S(2)}) collective-permute-start(f32[512,128]{1,0:T(8,128)S(1)} %get-tuple-element.58), channel_id=1, source_target_pairs={{128,0},{129,1},{130,2},{131,3},{132,4},{133,5},{134,6},{135,7},{1... | collective-permute-start | bytes 786440 | tf_op jit(solution)/shard_map/ppermute | solution.py:482
  32.0 0.2 collective-permute-done.4.trace
  32.1 1.5 %late_inner.1.field = f32[4,8,256,128]{3,2,1,0:T(8,128)S(1)} custom-call(s32[4]{0:T(128)S(1)} %pad_add_fusion.info, f32[4,8,256,128]{3,2,1,0:T(8,128)S(1)} %get-tuple-element.55.field, f32[4,8,256,128]{3,2,1,0:T(8,128)S(1)} %get-tuple-element.56.relaxed.refs_12_, ...), custom_call_target="tpu_custom_call", output_to_operand_aliasing={{}: (1, {})} | custom-call | flops 2000000000 | tf_op jit(solution)/shard_map/late_inner/pallas_call | solution.py:426
  33.6 6.7 %collective-permute-done.5.trace = f32[512,128]{1,0:T(8,128)S(1)} collective-permute-done((f32[512,128]{1,0:T(8,128)S(1)}, f32[512,128]{1,0:T(8,128)S(1)}, u32[]{:S(2)}, u32[]{:S(2)}) %collective-permute-start.5) | collective-permute-done | bytes 262176 | tf_op jit(solution)/shard_map/ppermute | solution.py:482
  40.3 1.6 %late_outer.1 = (f32[4,8,256,128]{3,2,1,0:T(8,128)S(1)}, f32[4,256,128]{2,1,0:T(8,128)S(1)}, f32[4,256,128]{2,1,0:T(8,128)S(1)}, f32[4,8,16,128]{3,2,1,0:T(8,128)S(1)}, f32[4,8,16,128]{3,2,1,0:T(8,128)S(1)}) custom-call(s32[4]{0:T(128)S(1)} %pad_add_fusion.info, f32[4,8,256,128]{3,2,1,0:T(8,128)S(1)} %late_inner.1.field, ...), custom_call_target="tpu_custom_call", output_to_operand_aliasing={{0}: (1, {})} | custom-call | flops 2000000000 | tf_op jit(solution)/shard_map/late_outer/pallas_call | solution.py:426
  41.9 0.1 collective-permute-start.6
  42.0 3.7 %collective-permute-start.7 = (f32[4,8,16,128]{3,2,1,0:T(8,128)S(1)}, f32[4,8,16,128]{3,2,1,0:T(8,128)S(1)}, u32[]{:S(2)}, u32[]{:S(2)}) collective-permute-start(f32[4,8,16,128]{3,2,1,0:T(8,128)S(1)} %get-tuple-element.63), channel_id=1, source_target_pairs={{1,2},{2,1},{5,6},{6,5},{9,10},{10,9},{13,14},{14,13},{17,18},{18,... | collective-permute-start | bytes 786440 | tf_op jit(solution)/shard_map/ppermute | solution.py:478
  45.7 2.2 %collective-permute-start.8 = (f32[4,256,128]{2,1,0:T(8,128)S(1)}, f32[4,256,128]{2,1,0:T(8,128)S(1)}, u32[]{:S(2)}, u32[]{:S(2)}) collective-permute-start(f32[4,256,128]{2,1,0:T(8,128)S(1)} %get-tuple-element.67), channel_id=1, source_target_pairs={{0,4},{8,12},{16,20},{24,28},{32,36},{40,44},{48,52},{56,60},{64,6... | collective-permute-start | bytes 1572872 | tf_op jit(solution)/shard_map/ppermute | solution.py:478
  47.9 2.1 %collective-permute-start.9 = (f32[4,256,128]{2,1,0:T(8,128)S(1)}, f32[4,256,128]{2,1,0:T(8,128)S(1)}, u32[]{:S(2)}, u32[]{:S(2)}) collective-permute-start(f32[4,256,128]{2,1,0:T(8,128)S(1)} %get-tuple-element.68), channel_id=1, source_target_pairs={{4,8},{12,16},{20,24},{28,32},{36,40},{44,48},{52,56},{60,64},{68,... | collective-permute-start | bytes 1572872 | tf_op jit(solution)/shard_map/ppermute | solution.py:478
  50.0 4.8 %next_inner.1 = (f32[4,8,256,128]{3,2,1,0:T(8,128)S(1)}, bf16[10,4,288,128]{3,2,1,0:T(8,128)(2,1)S(1)}, bf16[10,4,288,128]{3,2,1,0:T(8,128)(2,1)S(1)}) custom-call(f32[4,8,256,128]{3,2,1,0:T(8,128)S(1)} %get-tuple-element.59.adjoint.refs_3_, f32[4,8,256,128]{3,2,1,0:T(8,128)S(1)} %get-tuple-element.60.loads.refs_11_, ...), custom_call_target="tpu_custom_call" | custom-call | flops 5000000000 | tf_op jit(solution)/shard_map/next_inner/pallas_call | solution.py:270
  54.9 0.0 collective-permute-done.7.y_far.refs_10_
  54.9 0.8 inner_halos.3
  55.7 1.3 %collective-permute-start.10 = (f32[512,128]{1,0:T(8,128)S(1)}, f32[512,128]{1,0:T(8,128)S(1)}, u32[]{:S(2)}, u32[]{:S(2)}) collective-permute-start(f32[512,128]{1,0:T(8,128)S(1)} %get-tuple-element.70), channel_id=1, source_target_pairs={{128,0},{129,1},{130,2},{131,3},{132,4},{133,5},{134,6},{135,7},{1... | collective-permute-start | bytes 786440 | tf_op jit(solution)/shard_map/ppermute | solution.py:482
  57.0 8.5 %collective-permute-done.9.refs_8_ = f32[4,256,128]{2,1,0:T(8,128)S(1)} collective-permute-done((f32[4,256,128]{2,1,0:T(8,128)S(1)}, f32[4,256,128]{2,1,0:T(8,128)S(1)}, u32[]{:S(2)}, u32[]{:S(2)}) %collective-permute-start.9) | collective-permute-done | bytes 524320 | tf_op jit(solution)/shard_map/ppermute | solution.py:478
  65.5 5.1 %next_outer.1 = (f32[4,8,256,128]{3,2,1,0:T(8,128)S(1)}, bf16[10,4,288,128]{3,2,1,0:T(8,128)(2,1)S(1)}, bf16[10,4,288,128]{3,2,1,0:T(8,128)(2,1)S(1)}, f32[512,128]{1,0:T(8,128)S(1)}) custom-call(s32[4]{0:T(128)S(1)} %pad_add_fusion.info, ...), custom_call_target="tpu_custom_call", output_to_operand_aliasing={{0}: (1, {}), {1}: (2, {}), {2}: (3, {})} | custom-call | flops 7000000000 | tf_op jit(solution)/shard_map/next_outer/pallas_call | solution.py:391
  70.6 1.3 %collective-permute-start.11 = (f32[512,128]{1,0:T(8,128)S(1)}, f32[512,128]{1,0:T(8,128)S(1)}, u32[]{:S(2)}, u32[]{:S(2)}) collective-permute-start(f32[512,128]{1,0:T(8,128)S(1)} %get-tuple-element.72), channel_id=1, source_target_pairs={{128,0},{129,1},{130,2},{131,3},{132,4},{133,5},{134,6},{135,7},{1... | collective-permute-start | bytes 786440 | tf_op jit(solution)/shard_map/ppermute | solution.py:482
  71.9 2.8 %last_inner.1 = (f32[4,8,256,128]{3,2,1,0:T(8,128)S(1)}, f32[4,8,256,128]{3,2,1,0:T(8,128)}) custom-call(s32[4]{0:T(128)S(1)} %pad_add_fusion.info, f32[4,8,256,128]{3,2,1,0:T(8,128)S(1)} %get-tuple-element.69.field, f32[4,8,256,128]{3,2,1,0:T(8,128)S(1)} %get-tuple-element.56.relaxed.refs_12_, ...), custom_call_target="tpu_custom_call", output_to_operand_aliasing={{0}: (1, {})} | custom-call | flops 3000000000 | tf_op jit(solution)/shard_map/last_inner/pallas_call | solution.py:462
  74.7 5.1 %collective-permute-done.11.trace = f32[512,128]{1,0:T(8,128)S(1)} collective-permute-done((f32[512,128]{1,0:T(8,128)S(1)}, f32[512,128]{1,0:T(8,128)S(1)}, u32[]{:S(2)}, u32[]{:S(2)}) %collective-permute-start.11) | collective-permute-done | bytes 262176 | tf_op jit(solution)/shard_map/ppermute | solution.py:482
  79.8 2.8 %last_outer.1 = (f32[4,8,256,128]{3,2,1,0:T(8,128)S(1)}, f32[4,8,256,128]{3,2,1,0:T(8,128)}) custom-call(s32[4]{0:T(128)S(1)} %pad_add_fusion.info, f32[4,8,256,128]{3,2,1,0:T(8,128)S(1)} %get-tuple-element.71.field, f32[4,8,256,128]{3,2,1,0:T(8,128)S(1)} %get-tuple-element.56.relaxed.refs_12_, ...), custom_call_target="tpu_custom_call", output_to_operand_aliasing={{0}: (1, {}), {1}: (5, {})} | custom-call | flops 3000000000 | tf_op jit(solution)/shard_map/last_outer/pallas_call | solution.py:462
  (6 shorter events, 0.0 us)
Async XLA Ops:
  0.0 11.3 %copy-start = (f32[4,8,16,16]{3,2,1,0:T(8,128)S(1)}, f32[4,8,16,16]{3,2,1,0:T(8,128)}, u32[]{:S(2)}) copy-start(f32[4,8,16,16]{3,2,1,0:T(8,128)} %refs_0_.1) | copy-start | bytes 98308
  2.7 19.8 %collective-permute-start = (f32[4,8,16,128]{3,2,1,0:T(8,128)S(1)}, f32[4,8,16,128]{3,2,1,0:T(8,128)S(1)}, u32[]{:S(2)}, u32[]{:S(2)}) collective-permute-start(f32[4,8,16,128]{3,2,1,0:T(8,128)S(1)} %get-tuple-element.45), channel_id=1, source_target_pairs={{0,1},{2,3},{1,0},{3,2},{4,5},{6,7},{5,4},{7,6},{8,9},{10,11},{9,8... | collective-permute-start | bytes 786440 | tf_op jit(solution)/shard_map/ppermute | solution.py:478
  3.8 18.8 %collective-permute-start.1 = (f32[4,8,16,128]{3,2,1,0:T(8,128)S(1)}, f32[4,8,16,128]{3,2,1,0:T(8,128)S(1)}, u32[]{:S(2)}, u32[]{:S(2)}) collective-permute-start(f32[4,8,16,128]{3,2,1,0:T(8,128)S(1)} %get-tuple-element.46), channel_id=1, source_target_pairs={{1,2},{2,1},{5,6},{6,5},{9,10},{10,9},{13,14},{14,13},{17,18},{18,... | collective-permute-start | bytes 786440 | tf_op jit(solution)/shard_map/ppermute | solution.py:478
  5.7 19.1 %collective-permute-start.2 = (f32[4,256,128]{2,1,0:T(8,128)S(1)}, f32[4,256,128]{2,1,0:T(8,128)S(1)}, u32[]{:S(2)}, u32[]{:S(2)}) collective-permute-start(f32[4,256,128]{2,1,0:T(8,128)S(1)} %get-tuple-element.53), channel_id=1, source_target_pairs={{0,4},{8,12},{16,20},{24,28},{32,36},{40,44},{48,52},{56,60},{64,6... | collective-permute-start | bytes 1572872 | tf_op jit(solution)/shard_map/ppermute | solution.py:478
  6.8 18.1 %collective-permute-start.3 = (f32[4,256,128]{2,1,0:T(8,128)S(1)}, f32[4,256,128]{2,1,0:T(8,128)S(1)}, u32[]{:S(2)}, u32[]{:S(2)}) collective-permute-start(f32[4,256,128]{2,1,0:T(8,128)S(1)} %get-tuple-element.54), channel_id=1, source_target_pairs={{4,8},{12,16},{20,24},{28,32},{36,40},{44,48},{52,56},{60,64},{68,... | collective-permute-start | bytes 1572872 | tf_op jit(solution)/shard_map/ppermute | solution.py:478
  23.4 8.8 %collective-permute-start.4 = (f32[512,128]{1,0:T(8,128)S(1)}, f32[512,128]{1,0:T(8,128)S(1)}, u32[]{:S(2)}, u32[]{:S(2)}) collective-permute-start(f32[512,128]{1,0:T(8,128)S(1)} %get-tuple-element.57), channel_id=1, source_target_pairs={{128,0},{129,1},{130,2},{131,3},{132,4},{133,5},{134,6},{135,7},{1... | collective-permute-start | bytes 786440 | tf_op jit(solution)/shard_map/ppermute | solution.py:482
  30.7 9.6 %collective-permute-start.5 = (f32[512,128]{1,0:T(8,128)S(1)}, f32[512,128]{1,0:T(8,128)S(1)}, u32[]{:S(2)}, u32[]{:S(2)}) collective-permute-start(f32[512,128]{1,0:T(8,128)S(1)} %get-tuple-element.58), channel_id=1, source_target_pairs={{128,0},{129,1},{130,2},{131,3},{132,4},{133,5},{134,6},{135,7},{1... | collective-permute-start | bytes 786440 | tf_op jit(solution)/shard_map/ppermute | solution.py:482
  41.9 13.0 %collective-permute-start.6 = (f32[4,8,16,128]{3,2,1,0:T(8,128)S(1)}, f32[4,8,16,128]{3,2,1,0:T(8,128)S(1)}, u32[]{:S(2)}, u32[]{:S(2)}) collective-permute-start(f32[4,8,16,128]{3,2,1,0:T(8,128)S(1)} %get-tuple-element.62), channel_id=1, source_target_pairs={{0,1},{2,3},{1,0},{3,2},{4,5},{6,7},{5,4},{7,6},{8,9},{10,11},{9,8... | collective-permute-start | bytes 786440 | tf_op jit(solution)/shard_map/ppermute | solution.py:478
  42.0 12.9 %collective-permute-start.7 = (f32[4,8,16,128]{3,2,1,0:T(8,128)S(1)}, f32[4,8,16,128]{3,2,1,0:T(8,128)S(1)}, u32[]{:S(2)}, u32[]{:S(2)}) collective-permute-start(f32[4,8,16,128]{3,2,1,0:T(8,128)S(1)} %get-tuple-element.63), channel_id=1, source_target_pairs={{1,2},{2,1},{5,6},{6,5},{9,10},{10,9},{13,14},{14,13},{17,18},{18,... | collective-permute-start | bytes 786440 | tf_op jit(solution)/shard_map/ppermute | solution.py:478
  45.7 11.3 %collective-permute-start.8 = (f32[4,256,128]{2,1,0:T(8,128)S(1)}, f32[4,256,128]{2,1,0:T(8,128)S(1)}, u32[]{:S(2)}, u32[]{:S(2)}) collective-permute-start(f32[4,256,128]{2,1,0:T(8,128)S(1)} %get-tuple-element.67), channel_id=1, source_target_pairs={{0,4},{8,12},{16,20},{24,28},{32,36},{40,44},{48,52},{56,60},{64,6... | collective-permute-start | bytes 1572872 | tf_op jit(solution)/shard_map/ppermute | solution.py:478
  47.9 17.6 %collective-permute-start.9 = (f32[4,256,128]{2,1,0:T(8,128)S(1)}, f32[4,256,128]{2,1,0:T(8,128)S(1)}, u32[]{:S(2)}, u32[]{:S(2)}) collective-permute-start(f32[4,256,128]{2,1,0:T(8,128)S(1)} %get-tuple-element.68), channel_id=1, source_target_pairs={{4,8},{12,16},{20,24},{28,32},{36,40},{44,48},{52,56},{60,64},{68,... | collective-permute-start | bytes 1572872 | tf_op jit(solution)/shard_map/ppermute | solution.py:478
  55.7 16.2 %collective-permute-start.10 = (f32[512,128]{1,0:T(8,128)S(1)}, f32[512,128]{1,0:T(8,128)S(1)}, u32[]{:S(2)}, u32[]{:S(2)}) collective-permute-start(f32[512,128]{1,0:T(8,128)S(1)} %get-tuple-element.70), channel_id=1, source_target_pairs={{128,0},{129,1},{130,2},{131,3},{132,4},{133,5},{134,6},{135,7},{1... | collective-permute-start | bytes 786440 | tf_op jit(solution)/shard_map/ppermute | solution.py:482
  70.6 9.3 %collective-permute-start.11 = (f32[512,128]{1,0:T(8,128)S(1)}, f32[512,128]{1,0:T(8,128)S(1)}, u32[]{:S(2)}, u32[]{:S(2)}) collective-permute-start(f32[512,128]{1,0:T(8,128)S(1)} %get-tuple-element.72), channel_id=1, source_target_pairs={{128,0},{129,1},{130,2},{131,3},{132,4},{133,5},{134,6},{135,7},{1... | collective-permute-start | bytes 786440 | tf_op jit(solution)/shard_map/ppermute | solution.py:482

commit v2 on v1

--- a/solution.py
+++ b/solution.py
@@ -18,8 +18,8 @@
 INH = pl.BlockSpec(memory_space=pltpu.HBM)
 INV = pl.BlockSpec(memory_space=VMEM)
 INS = pl.BlockSpec(memory_space=pltpu.SMEM)
-INNER = ((1, 4),)
-OUTER = ((0, 1), (5, 3))
+INNER = ((1, 5),)
+OUTER = ((0, 1), (6, 2))
 
 
 def params(mib):
@@ -195,45 +195,54 @@
         source, target = ((initial, adjoint), (forcing, loads))[which]
         return pltpu.make_async_copy(source.at[:, x], target.at[:, x], sems.at[which, x])
 
-    order = layers(INNER) + layers(OUTER)
-    for which in range(2):
-        for x in order:
-            fetch(x, which).start()
+    for x in range(3):
+        fetch(x, 0).start()
+    fetch(1, 1).start()
     stencil_setup(high, low)
     for copy in small:
         copy.wait()
 
-    def matrices(value):
-        matrix = jnp.dot(value, precond[...], precision=lax.Precision.HIGHEST, preferred_element_type=F32)
-        return split(matrix)
-
     zero = jnp.zeros((BLOCK, BLOCK), BF16)
+    h, l = split(precond[...])
+    given[0:BLOCK, :] = jnp.concatenate([h, l], axis=1)
+    given[BLOCK:, :] = jnp.concatenate([h, zero], axis=1)
+    right = jnp.concatenate([jnp.concatenate([h, l], axis=1)] * 2, axis=0)
+    stacked = jnp.concatenate([faces[...].reshape(6 * BLOCK, BLOCK), OMEGA * block_matrix[...], coupling[...]], axis=0)
+    h, l = split(folded(both(stacked), right))
     for d in range(4):
-        h, l = matrices(faces[d])
-        lateral[d * BLOCK : (d + 1) * BLOCK, :] = jnp.concatenate([h, l], axis=1)
-        lateral[(d + 4) * BLOCK : (d + 5) * BLOCK, :] = jnp.concatenate([h, zero], axis=1)
-    parts = [matrices(OMEGA * block_matrix[...]), matrices(faces[4]), matrices(faces[5])]
-    central[0:BLOCK, :] = jnp.concatenate([h for h, _ in parts] + [l for _, l in parts], axis=1)
-    central[BLOCK:, :] = jnp.concatenate([h for h, _ in parts] + [zero] * 3, axis=1)
-    h, l = matrices(coupling[...])
+        rows = slice(d * BLOCK, (d + 1) * BLOCK)
+        lateral[rows, :] = jnp.concatenate([h[rows], l[rows]], axis=1)
+        lateral[(d + 4) * BLOCK : (d + 5) * BLOCK, :] = jnp.concatenate([h[rows], zero], axis=1)
+    parts = [slice(d * BLOCK, (d + 1) * BLOCK) for d in (6, 4, 5)]
+    central[0:BLOCK, :] = jnp.concatenate([h[rows] for rows in parts] + [l[rows] for rows in parts], axis=1)
+    central[BLOCK:, :] = jnp.concatenate([h[rows] for rows in parts] + [zero] * 3, axis=1)
+    h, l = h[7 * BLOCK :], l[7 * BLOCK :]
     none = jnp.zeros((SPACE, 2 * BLOCK), BF16)
     carry[...] = jnp.concatenate(
         [jnp.concatenate([h, l], axis=1), none, jnp.concatenate([h, zero[:SPACE]], axis=1), none], axis=0
     )
-    h, l = split(precond[...])
-    given[0:BLOCK, :] = jnp.concatenate([h, l], axis=1)
-    given[BLOCK:, :] = jnp.concatenate([h, zero], axis=1)
-
-    for x in range(EX):
+
+    def enter(x):
         fetch(x, 0).wait()
         position = lax.broadcasted_iota(jnp.int32, (NTD, LAYER, BLOCK), 1) + x * LAYER
         value = jnp.where(position < info[0], adjoint[:, x], 0.0)
         adjoint[:, x] = value
         stencil_split(x, value, high, low)
-    for x in range(EX):
+
+    enter(0)
+    enter(1)
+    later = {x: [(x + 2, 0), (x + 1, 1)] for x in layers(INNER)}
+    later[2] += [(0, 1)]
+    later[3] += [(EX - 1, 1)]
+    for x in layers(INNER):
+        for piece in later[x]:
+            fetch(*piece).start()
+        enter(x + 1)
         fetch(x, 1).wait()
-    for x in layers(INNER):
         predict(x, field, adjoint, loads, relaxed, high, low, lateral, central, given, conductance)
+    enter(EX - 1)
+    for x in layers(OUTER):
+        fetch(x, 1).wait()
 
 
 def first_prediction(info, initial, forcing, conductance, block_matrix, precond, faces, coupling):
@@ -253,17 +262,19 @@
             pltpu.SemaphoreType.DMA((4,)),
         ],
         compiler_params=params(16),
-        cost_estimate=cost(8),
+        cost_estimate=cost(0.01),
         name="first_inner",
     )(info, initial, forcing, conductance, block_matrix, precond, faces, coupling)
 
 
 def next_kernel(adjoint, loads, relaxed, lateral, central, field, high, low):
     stencil_setup(high, low)
-    for x in range(EX):
+    for x in range(2):
         stencil_split(x, adjoint[:, x], high, low)
     for x in layers(INNER):
+        stencil_split(x + 1, adjoint[:, x + 1], high, low)
         predict(x, field, adjoint, loads, relaxed, high, low, lateral, central)
+    stencil_split(EX - 1, adjoint[:, EX - 1], high, low)
 
 
 def next_prediction(adjoint, loads, relaxed, lateral, central):
@@ -273,7 +284,7 @@
         in_specs=[INV] * 5,
         out_specs=[INV] * 3,
         compiler_params=params(16),
-        cost_estimate=cost(5),
+        cost_estimate=cost(0.01),
         name="next_inner",
     )(adjoint, loads, relaxed, lateral, central)
 
@@ -282,7 +293,7 @@
     return jnp.concatenate([stack[t, first : first + count].reshape(count * LAYER, BLOCK) for first, count in runs], axis=0)
 
 
-def chain(info, field, relaxed, carry, runs, trace):
+def chain(info, field, relaxed, carry, runs, trace, done=None):
     keep = jnp.concatenate(
         [
             (lax.broadcasted_iota(jnp.int32, (count * LAYER, BLOCK), 0) + first * LAYER < info[0]).astype(F32)
@@ -300,6 +311,8 @@
             rows = count * LAYER
             field[t, first : first + count] = trace[at : at + rows].reshape(count, LAYER, BLOCK)
             at += rows
+        if done is not None:
+            done(t)
     return trace
 
 
@@ -435,25 +448,39 @@
     )(info, field, relaxed, carry, trace)
 
 
-def finish(runs, kept, out, sems):
+def last_chain(info, relaxed, carry, trace, kept, out, sems, runs):
     copies = [
-        pltpu.make_async_copy(kept.at[:, pl.ds(first, count)], out.at[:, pl.ds(first, count)], sems.at[k])
-        for k, (first, count) in enumerate(runs)
+        [
+            pltpu.make_async_copy(kept.at[t, pl.ds(first, count)], out.at[t, pl.ds(first, count)], sems.at[t, k])
+            for k, (first, count) in enumerate(runs)
+        ]
+        for t in range(NTD)
     ]
-    for copy in copies:
-        copy.start()
-    for copy in copies:
-        copy.wait()
+
+    def send(t):
+        for copy in copies[t]:
+            copy.start()
+
+    @pl.when(info[1] == 0)
+    def _():
+        chain(info, kept, relaxed, carry, runs, unpacked(trace[...]), send)
+
+    @pl.when(info[1] == 1)
+    def _():
+        for t in range(NTD):
+            send(t)
+
+    for t in range(NTD):
+        for copy in copies[t]:
+            copy.wait()
 
 
 def last_inner_kernel(info, field, relaxed, carry, trace, kept, out, sems):
-    late_chain(info, kept, relaxed, carry, trace, INNER)
-    finish(INNER, kept, out, sems)
+    last_chain(info, relaxed, carry, trace, kept, out, sems, INNER)
 
 
 def last_outer_kernel(info, field, relaxed, carry, trace, given, kept, out, sems):
-    late_chain(info, kept, relaxed, carry, trace, OUTER)
-    finish(OUTER, kept, out, sems)
+    last_chain(info, relaxed, carry, trace, kept, out, sems, OUTER)
 
 
 def last(info, field, relaxed, carry, trace, given):
@@ -465,7 +492,7 @@
         in_specs=[INS] + [INV] * 4 + ([] if inner else [INH]),
         out_specs=[INV, INH],
         input_output_aliases={1: 0} if inner else {1: 0, 5: 1},
-        scratch_shapes=[pltpu.SemaphoreType.DMA((2,))],
+        scratch_shapes=[pltpu.SemaphoreType.DMA((NTD, 2))],
         compiler_params=params(8),
         cost_estimate=cost(3),
         name="last_inner" if inner else "last_outer",

time: 83.1 us -> 74 us (0.89)
  the two profiles are of different devices: /device:TPU:241 before, /device:TPU:41 now
where the time goes in v2:
time: 74 us; the launch traced here: 73.7 us
  Pallas kernels  35.7 us (48%)
  starting transfers between devices  22.4 us (30%)
  waiting for transfers between devices  14.5 us (20%)
  between operations  1.08 us (1%)
    ppermute x8, starting transfers between devices, exchanged(): return lax.ppermute(value, axis, pairs + [(j, i) for i, j in pairs])  17 us
    ppermute x4, waiting for transfers between devices, sent_back(): return lax.ppermute(value, 'tm', [(1, 0)])  11 us
    pallas_call x1, Pallas kernels, first_prediction(): pl.pallas_call(first_kernel, out_shape=[VMEM(STACK, F32)] * 4 + [VMEM(PAD...  9.89 us
    pallas_call x2, Pallas kernels, outer_prediction(): pl.pallas_call(functools.partial(outer_kernel, first_sweep), out_shape=ou...  8.42 us
    pallas_call x1, Pallas kernels, next_prediction(): pl.pallas_call(next_kernel, out_shape=[VMEM(STACK, F32), VMEM(PADDED, BF1...  5.73 us
    ppermute x4, starting transfers between devices, sent_back(): return lax.ppermute(value, 'tm', [(1, 0)])  5.35 us
    pallas_call x2, Pallas kernels, last(): pl.pallas_call(last_inner_kernel if inner else last_outer_kernel, out_sha...  4.93 us
    ppermute x8, waiting for transfers between devices, exchanged(): return lax.ppermute(value, axis, pairs + [(j, i) for i, j in pairs])  3.53 us
  transfers between devices with their start and end apart: 12, of which 7 were waited for; matrix products, arithmetic and copies ran while one was open for 0% of the time, Pallas kernels for 41%

profile of v2, /device:TPU:41, one launch (start us, length us, event | category | flops | bytes accessed | tf_op | source)
XLA Modules:
  0.0 73.7 jit_solution(805398812063827449)
XLA Ops:
  0.7 0.1 pad_add_fusion.info
  0.8 1.9 %faces.1 = (f32[4,256,128]{2,1,0:T(8,128)S(1)}, f32[4,256,128]{2,1,0:T(8,128)S(1)}, f32[4,8,16,128]{3,2,1,0:T(8,128)S(1)}, f32[4,8,16,128]{3,2,1,0:T(8,128)S(1)}) custom-call(s32[4]{0:T(128)S(1)} %pad_add_fusion.info, f32[4,8,256,128]{3,2,1,0:T(8,128)} %bitcast.8), custom_call_target="tpu_custom_call" | custom-call | flops 2000000000 | tf_op jit(solution)/shard_map/faces/pallas_call | solution.py:91
  2.7 0.8 %collective-permute-start.2 = (f32[4,256,128]{2,1,0:T(8,128)S(1)}, f32[4,256,128]{2,1,0:T(8,128)S(1)}, u32[]{:S(2)}, u32[]{:S(2)}) collective-permute-start(f32[4,256,128]{2,1,0:T(8,128)S(1)} %get-tuple-element.53), channel_id=1, source_target_pairs={{0,4},{8,12},{16,20},{24,28},{32,36},{40,44},{48,52},{56,60},{64,6... | collective-permute-start | bytes 1572872 | tf_op jit(solution)/shard_map/ppermute | solution.py:505
  3.5 4.6 %collective-permute-start.3 = (f32[4,256,128]{2,1,0:T(8,128)S(1)}, f32[4,256,128]{2,1,0:T(8,128)S(1)}, u32[]{:S(2)}, u32[]{:S(2)}) collective-permute-start(f32[4,256,128]{2,1,0:T(8,128)S(1)} %get-tuple-element.54), channel_id=1, source_target_pairs={{4,8},{12,16},{20,24},{28,32},{36,40},{44,48},{52,56},{60,64},{68,... | collective-permute-start | bytes 1572872 | tf_op jit(solution)/shard_map/ppermute | solution.py:505
  8.1 0.3 collective-permute-start
  8.3 4.0 %collective-permute-start.1 = (f32[4,8,16,128]{3,2,1,0:T(8,128)S(1)}, f32[4,8,16,128]{3,2,1,0:T(8,128)S(1)}, u32[]{:S(2)}, u32[]{:S(2)}) collective-permute-start(f32[4,8,16,128]{3,2,1,0:T(8,128)S(1)} %get-tuple-element.46), channel_id=1, source_target_pairs={{1,2},{2,1},{5,6},{6,5},{9,10},{10,9},{13,14},{14,13},{17,18},{18,... | collective-permute-start | bytes 786440 | tf_op jit(solution)/shard_map/ppermute | solution.py:505
  12.4 9.9 %first_inner.1 = (f32[4,8,256,128]{3,2,1,0:T(8,128)S(1)}, f32[4,8,256,128]{3,2,1,0:T(8,128)S(1)}, f32[4,8,256,128]{3,2,1,0:T(8,128)S(1)}, f32[4,8,256,128]{3,2,1...) custom-call(s32[4]{0:T(128)S(1)} %pad_add_fusion.info, ...), custom_call_target="tpu_custom_call" | custom-call | flops 10000000 | tf_op jit(solution)/shard_map/first_inner/pallas_call | solution.py:249
  22.3 0.0 collective-permute-done.y_near.refs_13_
  22.3 0.8 %inner_halos.2 = (f32[4,8,256,128]{3,2,1,0:T(8,128)S(1)}, f32[640,128]{1,0:T(8,128)S(1)}) custom-call(s32[4]{0:T(128)S(1)} %pad_add_fusion.info, f32[4,8,256,128]{3,2,1,0:T(8,128)S(1)} %get-tuple-element.41.pred, f32[4,8,256,128]{3,2,1,0:T(8,128)S(1)} %get-tuple-element.42.relaxed.refs_6_, ...), custom_call_target="tpu_custom_call", output_to_operand_aliasing={{0}: (1, {})} | custom-call | flops 2000000000 | tf_op jit(solution)/shard_map/inner_halos/pallas_call | solution.py:356
  23.1 1.5 %collective-permute-start.4 = (f32[640,128]{1,0:T(8,128)S(1)}, f32[640,128]{1,0:T(8,128)S(1)}, u32[]{:S(2)}, u32[]{:S(2)}) collective-permute-start(f32[640,128]{1,0:T(8,128)S(1)} %get-tuple-element.57), channel_id=1, source_target_pairs={{128,0},{129,1},{130,2},{131,3},{132,4},{133,5},{134,6},{135,7},{1... | collective-permute-start | bytes 983048 | tf_op jit(solution)/shard_map/ppermute | solution.py:509
  24.6 4.5 %first_outer.1 = (f32[4,8,256,128]{3,2,1,0:T(8,128)S(1)}, bf16[10,4,288,128]{3,2,1,0:T(8,128)(2,1)S(1)}, bf16[10,4,288,128]{3,2,1,0:T(8,128)(2,1)S(1)}, f32[4,8,...) custom-call(s32[4]{0:T(128)S(1)} %pad_add_fusion.info, ...), custom_call_target="tpu_custom_call", output_to_operand_aliasing={{0}: (3, {}), {1}: (4, {}), {2}: (5, {}), {3}: (6, {}), {4}... | custom-call | flops 7000000000 | tf_op jit(solution)/shard_map/first_outer/pallas_call | solution.py:404
  29.1 1.3 %collective-permute-start.5 = (f32[384,128]{1,0:T(8,128)S(1)}, f32[384,128]{1,0:T(8,128)S(1)}, u32[]{:S(2)}, u32[]{:S(2)}) collective-permute-start(f32[384,128]{1,0:T(8,128)S(1)} %get-tuple-element.58), channel_id=1, source_target_pairs={{128,0},{129,1},{130,2},{131,3},{132,4},{133,5},{134,6},{135,7},{1... | collective-permute-start | bytes 589832 | tf_op jit(solution)/shard_map/ppermute | solution.py:509
  30.4 3.3 %collective-permute-done.4.trace = f32[640,128]{1,0:T(8,128)S(1)} collective-permute-done((f32[640,128]{1,0:T(8,128)S(1)}, f32[640,128]{1,0:T(8,128)S(1)}, u32[]{:S(2)}, u32[]{:S(2)}) %collective-permute-start.4) | collective-permute-done | bytes 327712 | tf_op jit(solution)/shard_map/ppermute | solution.py:509
  33.7 1.7 %late_inner.1.field = f32[4,8,256,128]{3,2,1,0:T(8,128)S(1)} custom-call(s32[4]{0:T(128)S(1)} %pad_add_fusion.info, f32[4,8,256,128]{3,2,1,0:T(8,128)S(1)} %get-tuple-element.55.field, f32[4,8,256,128]{3,2,1,0:T(8,128)S(1)} %get-tuple-element.56.relaxed.refs_12_, ...), custom_call_target="tpu_custom_call", output_to_operand_aliasing={{}: (1, {})} | custom-call | flops 2000000000 | tf_op jit(solution)/shard_map/late_inner/pallas_call | solution.py:439
  35.4 2.8 %collective-permute-done.5.trace = f32[384,128]{1,0:T(8,128)S(1)} collective-permute-done((f32[384,128]{1,0:T(8,128)S(1)}, f32[384,128]{1,0:T(8,128)S(1)}, u32[]{:S(2)}, u32[]{:S(2)}) %collective-permute-start.5) | collective-permute-done | bytes 196640 | tf_op jit(solution)/shard_map/ppermute | solution.py:509
  38.2 1.4 %late_outer.1 = (f32[4,8,256,128]{3,2,1,0:T(8,128)S(1)}, f32[4,256,128]{2,1,0:T(8,128)S(1)}, f32[4,256,128]{2,1,0:T(8,128)S(1)}, f32[4,8,16,128]{3,2,1,0:T(8,128)S(1)}, f32[4,8,16,128]{3,2,1,0:T(8,128)S(1)}) custom-call(s32[4]{0:T(128)S(1)} %pad_add_fusion.info, f32[4,8,256,128]{3,2,1,0:T(8,128)S(1)} %late_inner.1.field, ...), custom_call_target="tpu_custom_call", output_to_operand_aliasing={{0}: (1, {})} | custom-call | flops 2000000000 | tf_op jit(solution)/shard_map/late_outer/pallas_call | solution.py:439
  39.7 1.2 %collective-permute-start.8 = (f32[4,256,128]{2,1,0:T(8,128)S(1)}, f32[4,256,128]{2,1,0:T(8,128)S(1)}, u32[]{:S(2)}, u32[]{:S(2)}) collective-permute-start(f32[4,256,128]{2,1,0:T(8,128)S(1)} %get-tuple-element.67), channel_id=1, source_target_pairs={{0,4},{8,12},{16,20},{24,28},{32,36},{40,44},{48,52},{56,60},{64,6... | collective-permute-start | bytes 1572872 | tf_op jit(solution)/shard_map/ppermute | solution.py:505
  40.9 4.0 %collective-permute-start.9 = (f32[4,256,128]{2,1,0:T(8,128)S(1)}, f32[4,256,128]{2,1,0:T(8,128)S(1)}, u32[]{:S(2)}, u32[]{:S(2)}) collective-permute-start(f32[4,256,128]{2,1,0:T(8,128)S(1)} %get-tuple-element.68), channel_id=1, source_target_pairs={{4,8},{12,16},{20,24},{28,32},{36,40},{44,48},{52,56},{60,64},{68,... | collective-permute-start | bytes 1572872 | tf_op jit(solution)/shard_map/ppermute | solution.py:505
  44.8 0.1 collective-permute-start.6
  44.9 2.1 %collective-permute-start.7 = (f32[4,8,16,128]{3,2,1,0:T(8,128)S(1)}, f32[4,8,16,128]{3,2,1,0:T(8,128)S(1)}, u32[]{:S(2)}, u32[]{:S(2)}) collective-permute-start(f32[4,8,16,128]{3,2,1,0:T(8,128)S(1)} %get-tuple-element.63), channel_id=1, source_target_pairs={{1,2},{2,1},{5,6},{6,5},{9,10},{10,9},{13,14},{14,13},{17,18},{18,... | collective-permute-start | bytes 786440 | tf_op jit(solution)/shard_map/ppermute | solution.py:505
  47.1 5.7 %next_inner.1 = (f32[4,8,256,128]{3,2,1,0:T(8,128)S(1)}, bf16[10,4,288,128]{3,2,1,0:T(8,128)(2,1)S(1)}, bf16[10,4,288,128]{3,2,1,0:T(8,128)(2,1)S(1)}) custom-call(f32[4,8,256,128]{3,2,1,0:T(8,128)S(1)} %get-tuple-element.59.adjoint.refs_3_, f32[4,8,256,128]{3,2,1,0:T(8,128)S(1)} %get-tuple-element.60.loads.refs_11_, ...), custom_call_target="tpu_custom_call" | custom-call | flops 10000000 | tf_op jit(solution)/shard_map/next_inner/pallas_call | solution.py:281
  52.8 0.1 collective-permute-done.6.y_near.refs_9_
  53.0 1.9 %collective-permute-done.7.y_far.refs_10_ = f32[4,8,16,128]{3,2,1,0:T(8,128)S(1)} collective-permute-done((f32[4,8,16,128]{3,2,1,0:T(8,128)S(1)}, f32[4,8,16,128]{3,2,1,0:T(8,128)S(1)}, u32[]{:S(2)}, u32[]{:S(2)}) %collective-permute-start.7) | collective-permute-done | bytes 262176 | tf_op jit(solution)/shard_map/ppermute | solution.py:505
  54.9 0.8 %inner_halos.3 = (f32[4,8,256,128]{3,2,1,0:T(8,128)S(1)}, f32[640,128]{1,0:T(8,128)S(1)}) custom-call(s32[4]{0:T(128)S(1)} %pad_add_fusion.info, f32[4,8,256,128]{3,2,1,0:T(8,128)S(1)} %get-tuple-element.61.pred, f32[4,8,256,128]{3,2,1,0:T(8,128)S(1)} %get-tuple-element.56.relaxed.refs_12_, ...), custom_call_target="tpu_custom_call", output_to_operand_aliasing={{0}: (1, {})} | custom-call | flops 2000000000 | tf_op jit(solution)/shard_map/inner_halos/pallas_call | solution.py:356
  55.7 1.3 %collective-permute-start.10 = (f32[640,128]{1,0:T(8,128)S(1)}, f32[640,128]{1,0:T(8,128)S(1)}, u32[]{:S(2)}, u32[]{:S(2)}) collective-permute-start(f32[640,128]{1,0:T(8,128)S(1)} %get-tuple-element.70), channel_id=1, source_target_pairs={{128,0},{129,1},{130,2},{131,3},{132,4},{133,5},{134,6},{135,7},{1... | collective-permute-start | bytes 983048 | tf_op jit(solution)/shard_map/ppermute | solution.py:509
  57.0 1.5 %collective-permute-done.9.refs_8_ = f32[4,256,128]{2,1,0:T(8,128)S(1)} collective-permute-done((f32[4,256,128]{2,1,0:T(8,128)S(1)}, f32[4,256,128]{2,1,0:T(8,128)S(1)}, u32[]{:S(2)}, u32[]{:S(2)}) %collective-permute-start.9) | collective-permute-done | bytes 524320 | tf_op jit(solution)/shard_map/ppermute | solution.py:505
  58.5 4.0 %next_outer.1 = (f32[4,8,256,128]{3,2,1,0:T(8,128)S(1)}, bf16[10,4,288,128]{3,2,1,0:T(8,128)(2,1)S(1)}, bf16[10,4,288,128]{3,2,1,0:T(8,128)(2,1)S(1)}, f32[384,128]{1,0:T(8,128)S(1)}) custom-call(s32[4]{0:T(128)S(1)} %pad_add_fusion.info, ...), custom_call_target="tpu_custom_call", output_to_operand_aliasing={{0}: (1, {}), {1}: (2, {}), {2}: (3, {})} | custom-call | flops 7000000000 | tf_op jit(solution)/shard_map/next_outer/pallas_call | solution.py:404
  62.4 1.3 %collective-permute-start.11 = (f32[384,128]{1,0:T(8,128)S(1)}, f32[384,128]{1,0:T(8,128)S(1)}, u32[]{:S(2)}, u32[]{:S(2)}) collective-permute-start(f32[384,128]{1,0:T(8,128)S(1)} %get-tuple-element.72), channel_id=1, source_target_pairs={{128,0},{129,1},{130,2},{131,3},{132,4},{133,5},{134,6},{135,7},{1... | collective-permute-start | bytes 589832 | tf_op jit(solution)/shard_map/ppermute | solution.py:509
  63.7 2.4 %collective-permute-done.10.trace = f32[640,128]{1,0:T(8,128)S(1)} collective-permute-done((f32[640,128]{1,0:T(8,128)S(1)}, f32[640,128]{1,0:T(8,128)S(1)}, u32[]{:S(2)}, u32[]{:S(2)}) %collective-permute-start.10) | collective-permute-done | bytes 327712 | tf_op jit(solution)/shard_map/ppermute | solution.py:509
  66.2 2.7 %last_inner.1 = (f32[4,8,256,128]{3,2,1,0:T(8,128)S(1)}, f32[4,8,256,128]{3,2,1,0:T(8,128)}) custom-call(s32[4]{0:T(128)S(1)} %pad_add_fusion.info, f32[4,8,256,128]{3,2,1,0:T(8,128)S(1)} %get-tuple-element.69.field, f32[4,8,256,128]{3,2,1,0:T(8,128)S(1)} %get-tuple-element.56.relaxed.refs_12_, ...), custom_call_target="tpu_custom_call", output_to_operand_aliasing={{0}: (1, {})} | custom-call | flops 3000000000 | tf_op jit(solution)/shard_map/last_inner/pallas_call | solution.py:489
  68.9 2.4 %collective-permute-done.11.trace = f32[384,128]{1,0:T(8,128)S(1)} collective-permute-done((f32[384,128]{1,0:T(8,128)S(1)}, f32[384,128]{1,0:T(8,128)S(1)}, u32[]{:S(2)}, u32[]{:S(2)}) %collective-permute-start.11) | collective-permute-done | bytes 196640 | tf_op jit(solution)/shard_map/ppermute | solution.py:509
  71.3 2.2 %last_outer.1 = (f32[4,8,256,128]{3,2,1,0:T(8,128)S(1)}, f32[4,8,256,128]{3,2,1,0:T(8,128)}) custom-call(s32[4]{0:T(128)S(1)} %pad_add_fusion.info, f32[4,8,256,128]{3,2,1,0:T(8,128)S(1)} %get-tuple-element.71.field, f32[4,8,256,128]{3,2,1,0:T(8,128)S(1)} %get-tuple-element.56.relaxed.refs_12_, ...), custom_call_target="tpu_custom_call", output_to_operand_aliasing={{0}: (1, {}), {1}: (5, {})} | custom-call | flops 3000000000 | tf_op jit(solution)/shard_map/last_outer/pallas_call | solution.py:489
  (6 shorter events, 0.0 us)
Async XLA Ops:
  0.0 12.3 %copy-start = (f32[4,8,16,16]{3,2,1,0:T(8,128)S(1)}, f32[4,8,16,16]{3,2,1,0:T(8,128)}, u32[]{:S(2)}) copy-start(f32[4,8,16,16]{3,2,1,0:T(8,128)} %refs_0_.1) | copy-start | bytes 98308
  2.7 21.9 %collective-permute-start.2 = (f32[4,256,128]{2,1,0:T(8,128)S(1)}, f32[4,256,128]{2,1,0:T(8,128)S(1)}, u32[]{:S(2)}, u32[]{:S(2)}) collective-permute-start(f32[4,256,128]{2,1,0:T(8,128)S(1)} %get-tuple-element.53), channel_id=1, source_target_pairs={{0,4},{8,12},{16,20},{24,28},{32,36},{40,44},{48,52},{56,60},{64,6... | collective-permute-start | bytes 1572872 | tf_op jit(solution)/shard_map/ppermute | solution.py:505
  3.5 21.1 %collective-permute-start.3 = (f32[4,256,128]{2,1,0:T(8,128)S(1)}, f32[4,256,128]{2,1,0:T(8,128)S(1)}, u32[]{:S(2)}, u32[]{:S(2)}) collective-permute-start(f32[4,256,128]{2,1,0:T(8,128)S(1)} %get-tuple-element.54), channel_id=1, source_target_pairs={{4,8},{12,16},{20,24},{28,32},{36,40},{44,48},{52,56},{60,64},{68,... | collective-permute-start | bytes 1572872 | tf_op jit(solution)/shard_map/ppermute | solution.py:505
  8.1 14.2 %collective-permute-start = (f32[4,8,16,128]{3,2,1,0:T(8,128)S(1)}, f32[4,8,16,128]{3,2,1,0:T(8,128)S(1)}, u32[]{:S(2)}, u32[]{:S(2)}) collective-permute-start(f32[4,8,16,128]{3,2,1,0:T(8,128)S(1)} %get-tuple-element.45), channel_id=1, source_target_pairs={{0,1},{2,3},{1,0},{3,2},{4,5},{6,7},{5,4},{7,6},{8,9},{10,11},{9,8... | collective-permute-start | bytes 786440 | tf_op jit(solution)/shard_map/ppermute | solution.py:505
  8.3 14.0 %collective-permute-start.1 = (f32[4,8,16,128]{3,2,1,0:T(8,128)S(1)}, f32[4,8,16,128]{3,2,1,0:T(8,128)S(1)}, u32[]{:S(2)}, u32[]{:S(2)}) collective-permute-start(f32[4,8,16,128]{3,2,1,0:T(8,128)S(1)} %get-tuple-element.46), channel_id=1, source_target_pairs={{1,2},{2,1},{5,6},{6,5},{9,10},{10,9},{13,14},{14,13},{17,18},{18,... | collective-permute-start | bytes 786440 | tf_op jit(solution)/shard_map/ppermute | solution.py:505
  23.1 10.6 %collective-permute-start.4 = (f32[640,128]{1,0:T(8,128)S(1)}, f32[640,128]{1,0:T(8,128)S(1)}, u32[]{:S(2)}, u32[]{:S(2)}) collective-permute-start(f32[640,128]{1,0:T(8,128)S(1)} %get-tuple-element.57), channel_id=1, source_target_pairs={{128,0},{129,1},{130,2},{131,3},{132,4},{133,5},{134,6},{135,7},{1... | collective-permute-start | bytes 983048 | tf_op jit(solution)/shard_map/ppermute | solution.py:509
  29.1 9.1 %collective-permute-start.5 = (f32[384,128]{1,0:T(8,128)S(1)}, f32[384,128]{1,0:T(8,128)S(1)}, u32[]{:S(2)}, u32[]{:S(2)}) collective-permute-start(f32[384,128]{1,0:T(8,128)S(1)} %get-tuple-element.58), channel_id=1, source_target_pairs={{128,0},{129,1},{130,2},{131,3},{132,4},{133,5},{134,6},{135,7},{1... | collective-permute-start | bytes 589832 | tf_op jit(solution)/shard_map/ppermute | solution.py:509
  39.7 17.4 %collective-permute-start.8 = (f32[4,256,128]{2,1,0:T(8,128)S(1)}, f32[4,256,128]{2,1,0:T(8,128)S(1)}, u32[]{:S(2)}, u32[]{:S(2)}) collective-permute-start(f32[4,256,128]{2,1,0:T(8,128)S(1)} %get-tuple-element.67), channel_id=1, source_target_pairs={{0,4},{8,12},{16,20},{24,28},{32,36},{40,44},{48,52},{56,60},{64,6... | collective-permute-start | bytes 1572872 | tf_op jit(solution)/shard_map/ppermute | solution.py:505
  40.9 17.6 %collective-permute-start.9 = (f32[4,256,128]{2,1,0:T(8,128)S(1)}, f32[4,256,128]{2,1,0:T(8,128)S(1)}, u32[]{:S(2)}, u32[]{:S(2)}) collective-permute-start(f32[4,256,128]{2,1,0:T(8,128)S(1)} %get-tuple-element.68), channel_id=1, source_target_pairs={{4,8},{12,16},{20,24},{28,32},{36,40},{44,48},{52,56},{60,64},{68,... | collective-permute-start | bytes 1572872 | tf_op jit(solution)/shard_map/ppermute | solution.py:505
  44.8 8.1 %collective-permute-start.6 = (f32[4,8,16,128]{3,2,1,0:T(8,128)S(1)}, f32[4,8,16,128]{3,2,1,0:T(8,128)S(1)}, u32[]{:S(2)}, u32[]{:S(2)}) collective-permute-start(f32[4,8,16,128]{3,2,1,0:T(8,128)S(1)} %get-tuple-element.62), channel_id=1, source_target_pairs={{0,1},{2,3},{1,0},{3,2},{4,5},{6,7},{5,4},{7,6},{8,9},{10,11},{9,8... | collective-permute-start | bytes 786440 | tf_op jit(solution)/shard_map/ppermute | solution.py:505
  44.9 9.9 %collective-permute-start.7 = (f32[4,8,16,128]{3,2,1,0:T(8,128)S(1)}, f32[4,8,16,128]{3,2,1,0:T(8,128)S(1)}, u32[]{:S(2)}, u32[]{:S(2)}) collective-permute-start(f32[4,8,16,128]{3,2,1,0:T(8,128)S(1)} %get-tuple-element.63), channel_id=1, source_target_pairs={{1,2},{2,1},{5,6},{6,5},{9,10},{10,9},{13,14},{14,13},{17,18},{18,... | collective-permute-start | bytes 786440 | tf_op jit(solution)/shard_map/ppermute | solution.py:505
  55.7 10.5 %collective-permute-start.10 = (f32[640,128]{1,0:T(8,128)S(1)}, f32[640,128]{1,0:T(8,128)S(1)}, u32[]{:S(2)}, u32[]{:S(2)}) collective-permute-start(f32[640,128]{1,0:T(8,128)S(1)} %get-tuple-element.70), channel_id=1, source_target_pairs={{128,0},{129,1},{130,2},{131,3},{132,4},{133,5},{134,6},{135,7},{1... | collective-permute-start | bytes 983048 | tf_op jit(solution)/shard_map/ppermute | solution.py:509
  62.4 8.9 %collective-permute-start.11 = (f32[384,128]{1,0:T(8,128)S(1)}, f32[384,128]{1,0:T(8,128)S(1)}, u32[]{:S(2)}, u32[]{:S(2)}) collective-permute-start(f32[384,128]{1,0:T(8,128)S(1)} %get-tuple-element.72), channel_id=1, source_target_pairs={{128,0},{129,1},{130,2},{131,3},{132,4},{133,5},{134,6},{135,7},{1... | collective-permute-start | bytes 589832 | tf_op jit(solution)/shard_map/ppermute | solution.py:509

commit v3 on v2

--- a/solution.py
+++ b/solution.py
@@ -335,6 +335,10 @@
     def _():
         trace[...] = packed(chain(info, field, relaxed, carry, runs, None))
 
+    @pl.when(info[1] == 0)
+    def _():
+        trace[...] = jnp.zeros(trace.shape, F32)
+
 
 def face_matrix(lateral, d):
     top, bottom = pl.multiple_of(d * BLOCK, BLOCK), pl.multiple_of((d + 4) * BLOCK, BLOCK)
@@ -343,9 +347,9 @@
 
 def inner_kernel(info, pred, relaxed, lateral, carry, y_near, y_far, field, trace):
     ((first, count),) = INNER
-    for halo, at in ((y_near, near(info, 1)), (y_far, far(info, 1))):
+    for halo, at, has in ((y_near, near(info, 1), 1), (y_far, far(info, 1), info[5])):
         matrix = face_matrix(lateral, 2 + (at > 0).astype(jnp.int32))
-        values = halo[:, first : first + count].reshape(NTD * count * EZ, BLOCK)
+        values = jnp.where(has > 0, halo[:, first : first + count].reshape(NTD * count * EZ, BLOCK), 0.0)
         term = folded(both(values), matrix).reshape(NTD, count, EZ, BLOCK)
         area = (slice(None), pl.ds(first, count), pl.ds(at, EZ))
         field[area] = field[area] - relaxed[area] * term
@@ -374,15 +378,15 @@
         conductance = given = None
         (_, _, _, adjoint, lateral, central, carry, x_near, x_far, y_near, y_far, loads, relaxed,
          field, high, low, trace) = refs
-    for halo, x in ((x_near, near(info, 0)), (x_far, far(info, 0))):
-        h, l = split(halo[...])
+    for halo, x, has in ((x_near, near(info, 0), 1), (x_far, far(info, 0), info[4])):
+        h, l = split(jnp.where(has > 0, halo[...], 0.0))
         place = jnp.where(x > 0, EX + 1, 0)
         high[place, :, pl.ds(EZ, LAYER)] = h
         low[place, :, pl.ds(EZ, LAYER)] = l
-    for halo, y in ((y_near, near(info, 1)), (y_far, far(info, 1))):
+    for halo, y, has in ((y_near, near(info, 1), 1), (y_far, far(info, 1), info[5])):
         place = pl.multiple_of(jnp.where(y > 0, LAYER + EZ, 0), EZ)
         for x in layers(OUTER):
-            h, l = split(halo[:, x])
+            h, l = split(jnp.where(has > 0, halo[:, x], 0.0))
             high[x + 1, :, pl.ds(place, EZ)] = h
             low[x + 1, :, pl.ds(place, EZ)] = l
     for x in layers(OUTER):
@@ -499,14 +503,24 @@
     )(*args)
 
 
+def both_ways(pairs):
+    return pairs + [(j, i) for i, j in pairs]
+
+
 def exchanged(value, axis, first):
     count = lax.axis_size(axis)
-    pairs = [(i, i + 1) for i in range(first, count - 1, 2)]
-    return lax.ppermute(value, axis, pairs + [(j, i) for i, j in pairs])
+    return lax.ppermute(value, axis, both_ways([(i, (i + 1) % count) for i in range(first, count, 2)]))
+
+
+def exchanged_far_x(value):
+    count, lines = lax.axis_size("sx"), lax.axis_size("sy")
+    pairs = [(i * lines + k, (i + 1) * lines + k) for i in range(1, count - 1, 2) for k in range(lines)]
+    pairs += [(i * lines + k, i * lines + k + 1) for i in (0, count - 1) for k in range(0, lines, 2)]
+    return lax.ppermute(value, ("sx", "sy"), both_ways(pairs))
 
 
 def sent_back(value):
-    return lax.ppermute(value, "tm", [(1, 0)])
+    return lax.ppermute(value, "tm", [(1, 0), (0, 1)])
 
 
 def body(forcing, initial, conductance, counts, block_matrix, precond, face_coupling, time_coupling):
@@ -518,13 +532,19 @@
     )
     even_x = 1 - lax.rem(lax.axis_index("sx"), 2).astype(jnp.int32)
     even_y = 1 - lax.rem(lax.axis_index("sy"), 2).astype(jnp.int32)
+    at_x, at_y = lax.axis_index("sx"), lax.axis_index("sy")
+    has_x = jnp.logical_and(at_x > 0, at_x < lax.axis_size("sx") - 1).astype(jnp.int32)
+    has_y = jnp.logical_and(at_y > 0, at_y < lax.axis_size("sy") - 1).astype(jnp.int32)
     info = jnp.stack(
-        [counts[0, 0], lax.axis_index("tm").astype(jnp.int32), even_x * (EX - 1), even_y * (LAYER - EZ)]
+        [
+            counts[0, 0], lax.axis_index("tm").astype(jnp.int32),
+            even_x * (EX - 1), even_y * (LAYER - EZ), has_x, has_y,
+        ]
     )
 
     def halos_of(x_near, x_far, y_near, y_far):
         return (
-            exchanged(x_near, "sx", 0), exchanged(x_far, "sx", 1),
+            exchanged(x_near, "sx", 0), exchanged_far_x(x_far),
             exchanged(y_near, "sy", 0), exchanged(y_far, "sy", 1),
         )
 

time: 74 us -> 65.5 us (0.89)
  the two profiles are of different devices: /device:TPU:41 before, /device:TPU:64 now
where the time goes in v3:
time: 65.5 us; the launch traced here: 65.1 us
  Pallas kernels  35.8 us (55%)
  starting transfers between devices  16.3 us (25%)
  waiting for transfers between devices  12 us (18%)
  between operations  1 us (2%)
    pallas_call x1, Pallas kernels, first_prediction(): pl.pallas_call(first_kernel, out_shape=[VMEM(STACK, F32)] * 4 + [VMEM(PAD...  9.88 us
    ppermute x4, waiting for transfers between devices, sent_back(): return lax.ppermute(value, 'tm', [(1, 0), (0, 1)])  8.53 us
    pallas_call x2, Pallas kernels, outer_prediction(): pl.pallas_call(functools.partial(outer_kernel, first_sweep), out_shape=ou...  8.5 us
    ppermute x4, starting transfers between devices, sent_back(): return lax.ppermute(value, 'tm', [(1, 0), (0, 1)])  6 us
    pallas_call x1, Pallas kernels, next_prediction(): pl.pallas_call(next_kernel, out_shape=[VMEM(STACK, F32), VMEM(PADDED, BF1...  5.73 us
    ppermute x6, starting transfers between devices, exchanged(): lax.ppermute(value, axis, both_ways([(i, (i + 1) % count) for i in range(...  5.18 us
    ppermute x2, starting transfers between devices, exchanged_far_x(): return lax.ppermute(value, ('sx', 'sy'), both_ways(pairs))  5.08 us
    pallas_call x2, Pallas kernels, last(): pl.pallas_call(last_inner_kernel if inner else last_outer_kernel, out_sha...  4.93 us
  transfers between devices with their start and end apart: 12, of which 6 were waited for; matrix products, arithmetic and copies ran while one was open for 0% of the time, Pallas kernels for 46%

profile of v3, /device:TPU:64, one launch (start us, length us, event | category | flops | bytes accessed | tf_op | source)
XLA Modules:
  0.0 65.1 jit_solution(62168498365528925)
XLA Ops:
  0.7 0.1 stack.31.info
  0.8 1.9 %faces.1 = (f32[4,256,128]{2,1,0:T(8,128)S(1)}, f32[4,256,128]{2,1,0:T(8,128)S(1)}, f32[4,8,16,128]{3,2,1,0:T(8,128)S(1)}, f32[4,8,16,128]{3,2,1,0:T(8,128)S(1)}) custom-call(s32[6]{0:T(128)S(1)} %stack.31.info, f32[4,8,256,128]{3,2,1,0:T(8,128)} %bitcast.10), custom_call_target="tpu_custom_call" | custom-call | flops 2000000000 | tf_op jit(solution)/shard_map/faces/pallas_call | solution.py:91
  2.7 0.1 collective-permute-start.2
  2.8 2.7 %collective-permute-start.3 = (f32[4,256,128]{2,1,0:T(8,128)S(1)}, f32[4,256,128]{2,1,0:T(8,128)S(1)}, u32[]{:S(2)}, u32[]{:S(2)}) collective-permute-start(f32[4,256,128]{2,1,0:T(8,128)S(1)} %get-tuple-element.54), channel_id=1, source_target_pairs={{4,8},{5,9},{6,10},{7,11},{12,16},{13,17},{14,18},{15,19},{20,24},... | collective-permute-start | bytes 1572872 | tf_op jit(solution)/shard_map/ppermute | solution.py:519
  5.5 1.6 %collective-permute-start = (f32[4,8,16,128]{3,2,1,0:T(8,128)S(1)}, f32[4,8,16,128]{3,2,1,0:T(8,128)S(1)}, u32[]{:S(2)}, u32[]{:S(2)}) collective-permute-start(f32[4,8,16,128]{3,2,1,0:T(8,128)S(1)} %get-tuple-element.45), channel_id=1, source_target_pairs={{0,1},{2,3},{1,0},{3,2},{4,5},{6,7},{5,4},{7,6},{8,9},{10,11},{9,8... | collective-permute-start | bytes 786440 | tf_op jit(solution)/shard_map/ppermute | solution.py:512
  7.1 2.2 %collective-permute-start.1 = (f32[4,8,16,128]{3,2,1,0:T(8,128)S(1)}, f32[4,8,16,128]{3,2,1,0:T(8,128)S(1)}, u32[]{:S(2)}, u32[]{:S(2)}) collective-permute-start(f32[4,8,16,128]{3,2,1,0:T(8,128)S(1)} %get-tuple-element.46), channel_id=1, source_target_pairs={{1,2},{3,0},{2,1},{0,3},{5,6},{7,4},{6,5},{4,7},{9,10},{11,8},{10,... | collective-permute-start | bytes 786440 | tf_op jit(solution)/shard_map/ppermute | solution.py:512
  9.3 9.9 %first_inner.1 = (f32[4,8,256,128]{3,2,1,0:T(8,128)S(1)}, f32[4,8,256,128]{3,2,1,0:T(8,128)S(1)}, f32[4,8,256,128]{3,2,1,0:T(8,128)S(1)}, f32[4,8,256,128]{3,2,1...) custom-call(s32[6]{0:T(128)S(1)} %stack.31.info, ...), custom_call_target="tpu_custom_call" | custom-call | flops 10000000 | tf_op jit(solution)/shard_map/first_inner/pallas_call | solution.py:249
  19.2 0.0 collective-permute-done.y_near.refs_13_
  19.2 0.8 %inner_halos.2 = (f32[4,8,256,128]{3,2,1,0:T(8,128)S(1)}, f32[640,128]{1,0:T(8,128)S(1)}) custom-call(s32[6]{0:T(128)S(1)} %stack.31.info, f32[4,8,256,128]{3,2,1,0:T(8,128)S(1)} %get-tuple-element.41.pred, f32[4,8,256,128]{3,2,1,0:T(8,128)S(1)} %get-tuple-element.42.relaxed.refs_6_, ...), custom_call_target="tpu_custom_call", output_to_operand_aliasing={{0}: (1, {})} | custom-call | flops 2000000000 | tf_op jit(solution)/shard_map/inner_halos/pallas_call | solution.py:360
  20.0 1.9 %collective-permute-start.4 = (f32[640,128]{1,0:T(8,128)S(1)}, f32[640,128]{1,0:T(8,128)S(1)}, u32[]{:S(2)}, u32[]{:S(2)}) collective-permute-start(f32[640,128]{1,0:T(8,128)S(1)} %get-tuple-element.57), channel_id=1, source_target_pairs={{128,0},{0,128},{129,1},{1,129},{130,2},{2,130},{131,3},{3,131},{1... | collective-permute-start | bytes 983048 | tf_op jit(solution)/shard_map/ppermute | solution.py:523
  21.9 0.0 collective-permute-done.3.refs_12_
  21.9 4.5 %first_outer.1 = (f32[4,8,256,128]{3,2,1,0:T(8,128)S(1)}, bf16[10,4,288,128]{3,2,1,0:T(8,128)(2,1)S(1)}, bf16[10,4,288,128]{3,2,1,0:T(8,128)(2,1)S(1)}, f32[4,8,...) custom-call(s32[6]{0:T(128)S(1)} %stack.31.info, ...), custom_call_target="tpu_custom_call", output_to_operand_aliasing={{0}: (3, {}), {1}: (4, {}), {2}: (5, {}), {3}: (6, {}), {4}... | custom-call | flops 7000000000 | tf_op jit(solution)/shard_map/first_outer/pallas_call | solution.py:408
  26.4 1.2 %collective-permute-start.5 = (f32[384,128]{1,0:T(8,128)S(1)}, f32[384,128]{1,0:T(8,128)S(1)}, u32[]{:S(2)}, u32[]{:S(2)}) collective-permute-start(f32[384,128]{1,0:T(8,128)S(1)} %get-tuple-element.58), channel_id=1, source_target_pairs={{128,0},{0,128},{129,1},{1,129},{130,2},{2,130},{131,3},{3,131},{1... | collective-permute-start | bytes 589832 | tf_op jit(solution)/shard_map/ppermute | solution.py:523
  27.6 3.2 %collective-permute-done.4.trace = f32[640,128]{1,0:T(8,128)S(1)} collective-permute-done((f32[640,128]{1,0:T(8,128)S(1)}, f32[640,128]{1,0:T(8,128)S(1)}, u32[]{:S(2)}, u32[]{:S(2)}) %collective-permute-start.4) | collective-permute-done | bytes 327712 | tf_op jit(solution)/shard_map/ppermute | solution.py:523
  30.9 1.7 %late_inner.1.field = f32[4,8,256,128]{3,2,1,0:T(8,128)S(1)} custom-call(s32[6]{0:T(128)S(1)} %stack.31.info, f32[4,8,256,128]{3,2,1,0:T(8,128)S(1)} %get-tuple-element.55.field, f32[4,8,256,128]{3,2,1,0:T(8,128)S(1)} %get-tuple-element.56.relaxed.refs_12_, ...), custom_call_target="tpu_custom_call", output_to_operand_aliasing={{}: (1, {})} | custom-call | flops 2000000000 | tf_op jit(solution)/shard_map/late_inner/pallas_call | solution.py:443
  32.6 1.6 %collective-permute-done.5.trace = f32[384,128]{1,0:T(8,128)S(1)} collective-permute-done((f32[384,128]{1,0:T(8,128)S(1)}, f32[384,128]{1,0:T(8,128)S(1)}, u32[]{:S(2)}, u32[]{:S(2)}) %collective-permute-start.5) | collective-permute-done | bytes 196640 | tf_op jit(solution)/shard_map/ppermute | solution.py:523
  34.1 1.4 %late_outer.1 = (f32[4,8,256,128]{3,2,1,0:T(8,128)S(1)}, f32[4,256,128]{2,1,0:T(8,128)S(1)}, f32[4,256,128]{2,1,0:T(8,128)S(1)}, f32[4,8,16,128]{3,2,1,0:T(8,128)S(1)}, f32[4,8,16,128]{3,2,1,0:T(8,128)S(1)}) custom-call(s32[6]{0:T(128)S(1)} %stack.31.info, f32[4,8,256,128]{3,2,1,0:T(8,128)S(1)} %late_inner.1.field, ...), custom_call_target="tpu_custom_call", output_to_operand_aliasing={{0}: (1, {})} | custom-call | flops 2000000000 | tf_op jit(solution)/shard_map/late_outer/pallas_call | solution.py:443
  35.6 0.1 collective-permute-start.8
  35.7 2.4 %collective-permute-start.9 = (f32[4,256,128]{2,1,0:T(8,128)S(1)}, f32[4,256,128]{2,1,0:T(8,128)S(1)}, u32[]{:S(2)}, u32[]{:S(2)}) collective-permute-start(f32[4,256,128]{2,1,0:T(8,128)S(1)} %get-tuple-element.68), channel_id=1, source_target_pairs={{4,8},{5,9},{6,10},{7,11},{12,16},{13,17},{14,18},{15,19},{20,24},... | collective-permute-start | bytes 1572872 | tf_op jit(solution)/shard_map/ppermute | solution.py:519
  38.1 0.7 %collective-permute-start.6 = (f32[4,8,16,128]{3,2,1,0:T(8,128)S(1)}, f32[4,8,16,128]{3,2,1,0:T(8,128)S(1)}, u32[]{:S(2)}, u32[]{:S(2)}) collective-permute-start(f32[4,8,16,128]{3,2,1,0:T(8,128)S(1)} %get-tuple-element.62), channel_id=1, source_target_pairs={{0,1},{2,3},{1,0},{3,2},{4,5},{6,7},{5,4},{7,6},{8,9},{10,11},{9,8... | collective-permute-start | bytes 786440 | tf_op jit(solution)/shard_map/ppermute | solution.py:512
  38.8 0.5 collective-permute-start.7
  39.3 5.7 %next_inner.1 = (f32[4,8,256,128]{3,2,1,0:T(8,128)S(1)}, bf16[10,4,288,128]{3,2,1,0:T(8,128)(2,1)S(1)}, bf16[10,4,288,128]{3,2,1,0:T(8,128)(2,1)S(1)}) custom-call(f32[4,8,256,128]{3,2,1,0:T(8,128)S(1)} %get-tuple-element.59.adjoint.refs_3_, f32[4,8,256,128]{3,2,1,0:T(8,128)S(1)} %get-tuple-element.60.loads.refs_11_, ...), custom_call_target="tpu_custom_call" | custom-call | flops 10000000 | tf_op jit(solution)/shard_map/next_inner/pallas_call | solution.py:281
  45.0 1.9 %collective-permute-done.6.y_near.refs_9_ = f32[4,8,16,128]{3,2,1,0:T(8,128)S(1)} collective-permute-done((f32[4,8,16,128]{3,2,1,0:T(8,128)S(1)}, f32[4,8,16,128]{3,2,1,0:T(8,128)S(1)}, u32[]{:S(2)}, u32[]{:S(2)}) %collective-permute-start.6) | collective-permute-done | bytes 262176 | tf_op jit(solution)/shard_map/ppermute | solution.py:512
  46.9 1.6 %collective-permute-done.7.y_far.refs_10_ = f32[4,8,16,128]{3,2,1,0:T(8,128)S(1)} collective-permute-done((f32[4,8,16,128]{3,2,1,0:T(8,128)S(1)}, f32[4,8,16,128]{3,2,1,0:T(8,128)S(1)}, u32[]{:S(2)}, u32[]{:S(2)}) %collective-permute-start.7) | collective-permute-done | bytes 262176 | tf_op jit(solution)/shard_map/ppermute | solution.py:512
  48.5 0.8 %inner_halos.3 = (f32[4,8,256,128]{3,2,1,0:T(8,128)S(1)}, f32[640,128]{1,0:T(8,128)S(1)}) custom-call(s32[6]{0:T(128)S(1)} %stack.31.info, f32[4,8,256,128]{3,2,1,0:T(8,128)S(1)} %get-tuple-element.61.pred, f32[4,8,256,128]{3,2,1,0:T(8,128)S(1)} %get-tuple-element.56.relaxed.refs_12_, ...), custom_call_target="tpu_custom_call", output_to_operand_aliasing={{0}: (1, {})} | custom-call | flops 2000000000 | tf_op jit(solution)/shard_map/inner_halos/pallas_call | solution.py:360
  49.4 1.8 %collective-permute-start.10 = (f32[640,128]{1,0:T(8,128)S(1)}, f32[640,128]{1,0:T(8,128)S(1)}, u32[]{:S(2)}, u32[]{:S(2)}) collective-permute-start(f32[640,128]{1,0:T(8,128)S(1)} %get-tuple-element.70), channel_id=1, source_target_pairs={{128,0},{0,128},{129,1},{1,129},{130,2},{2,130},{131,3},{3,131},{1... | collective-permute-start | bytes 983048 | tf_op jit(solution)/shard_map/ppermute | solution.py:523
  51.2 4.0 %next_outer.1 = (f32[4,8,256,128]{3,2,1,0:T(8,128)S(1)}, bf16[10,4,288,128]{3,2,1,0:T(8,128)(2,1)S(1)}, bf16[10,4,288,128]{3,2,1,0:T(8,128)(2,1)S(1)}, f32[384,128]{1,0:T(8,128)S(1)}) custom-call(s32[6]{0:T(128)S(1)} %stack.31.info, f32[4,8,256,128]{3,2,1,0:T(8,128)S(1)} %get-tuple-element.64.refs_0_, ...), custom_call_target="tpu_custom_call", output_to_operand_aliasing={{0}: (1, {}), {1}: (2, {}), {2}: (3, {})} | custom-call | flops 7000000000 | tf_op jit(solution)/shard_map/next_outer/pallas_call | solution.py:408
  55.2 1.1 %collective-permute-start.11 = (f32[384,128]{1,0:T(8,128)S(1)}, f32[384,128]{1,0:T(8,128)S(1)}, u32[]{:S(2)}, u32[]{:S(2)}) collective-permute-start(f32[384,128]{1,0:T(8,128)S(1)} %get-tuple-element.72), channel_id=1, source_target_pairs={{128,0},{0,128},{129,1},{1,129},{130,2},{2,130},{131,3},{3,131},{1... | collective-permute-start | bytes 589832 | tf_op jit(solution)/shard_map/ppermute | solution.py:523
  56.3 2.3 %collective-permute-done.10.trace = f32[640,128]{1,0:T(8,128)S(1)} collective-permute-done((f32[640,128]{1,0:T(8,128)S(1)}, f32[640,128]{1,0:T(8,128)S(1)}, u32[]{:S(2)}, u32[]{:S(2)}) %collective-permute-start.10) | collective-permute-done | bytes 327712 | tf_op jit(solution)/shard_map/ppermute | solution.py:523
  58.5 2.7 %last_inner.1 = (f32[4,8,256,128]{3,2,1,0:T(8,128)S(1)}, f32[4,8,256,128]{3,2,1,0:T(8,128)}) custom-call(s32[6]{0:T(128)S(1)} %stack.31.info, f32[4,8,256,128]{3,2,1,0:T(8,128)S(1)} %get-tuple-element.69.field, f32[4,8,256,128]{3,2,1,0:T(8,128)S(1)} %get-tuple-element.56.relaxed.refs_12_, ...), custom_call_target="tpu_custom_call", output_to_operand_aliasing={{0}: (1, {})} | custom-call | flops 3000000000 | tf_op jit(solution)/shard_map/last_inner/pallas_call | solution.py:493
  61.3 1.5 %collective-permute-done.11.trace = f32[384,128]{1,0:T(8,128)S(1)} collective-permute-done((f32[384,128]{1,0:T(8,128)S(1)}, f32[384,128]{1,0:T(8,128)S(1)}, u32[]{:S(2)}, u32[]{:S(2)}) %collective-permute-start.11) | collective-permute-done | bytes 196640 | tf_op jit(solution)/shard_map/ppermute | solution.py:523
  62.8 2.2 %last_outer.1 = (f32[4,8,256,128]{3,2,1,0:T(8,128)S(1)}, f32[4,8,256,128]{3,2,1,0:T(8,128)}) custom-call(s32[6]{0:T(128)S(1)} %stack.31.info, f32[4,8,256,128]{3,2,1,0:T(8,128)S(1)} %get-tuple-element.71.field, f32[4,8,256,128]{3,2,1,0:T(8,128)S(1)} %get-tuple-element.56.relaxed.refs_12_, ...), custom_call_target="tpu_custom_call", output_to_operand_aliasing={{0}: (1, {}), {1}: (5, {})} | custom-call | flops 3000000000 | tf_op jit(solution)/shard_map/last_outer/pallas_call | solution.py:493
  (6 shorter events, 0.0 us)
Async XLA Ops:
  0.0 9.3 %copy-start = (f32[4,8,16,16]{3,2,1,0:T(8,128)S(1)}, f32[4,8,16,16]{3,2,1,0:T(8,128)}, u32[]{:S(2)}) copy-start(f32[4,8,16,16]{3,2,1,0:T(8,128)} %refs_0_.1) | copy-start | bytes 98308
  2.7 19.1 %collective-permute-start.2 = (f32[4,256,128]{2,1,0:T(8,128)S(1)}, f32[4,256,128]{2,1,0:T(8,128)S(1)}, u32[]{:S(2)}, u32[]{:S(2)}) collective-permute-start(f32[4,256,128]{2,1,0:T(8,128)S(1)} %get-tuple-element.53), channel_id=1, source_target_pairs={{0,4},{8,12},{16,20},{24,28},{32,36},{40,44},{48,52},{56,60},{64,6... | collective-permute-start | bytes 1572872 | tf_op jit(solution)/shard_map/ppermute | solution.py:512
  2.8 19.0 %collective-permute-start.3 = (f32[4,256,128]{2,1,0:T(8,128)S(1)}, f32[4,256,128]{2,1,0:T(8,128)S(1)}, u32[]{:S(2)}, u32[]{:S(2)}) collective-permute-start(f32[4,256,128]{2,1,0:T(8,128)S(1)} %get-tuple-element.54), channel_id=1, source_target_pairs={{4,8},{5,9},{6,10},{7,11},{12,16},{13,17},{14,18},{15,19},{20,24},... | collective-permute-start | bytes 1572872 | tf_op jit(solution)/shard_map/ppermute | solution.py:519
  5.5 13.7 %collective-permute-start = (f32[4,8,16,128]{3,2,1,0:T(8,128)S(1)}, f32[4,8,16,128]{3,2,1,0:T(8,128)S(1)}, u32[]{:S(2)}, u32[]{:S(2)}) collective-permute-start(f32[4,8,16,128]{3,2,1,0:T(8,128)S(1)} %get-tuple-element.45), channel_id=1, source_target_pairs={{0,1},{2,3},{1,0},{3,2},{4,5},{6,7},{5,4},{7,6},{8,9},{10,11},{9,8... | collective-permute-start | bytes 786440 | tf_op jit(solution)/shard_map/ppermute | solution.py:512
  7.1 12.1 %collective-permute-start.1 = (f32[4,8,16,128]{3,2,1,0:T(8,128)S(1)}, f32[4,8,16,128]{3,2,1,0:T(8,128)S(1)}, u32[]{:S(2)}, u32[]{:S(2)}) collective-permute-start(f32[4,8,16,128]{3,2,1,0:T(8,128)S(1)} %get-tuple-element.46), channel_id=1, source_target_pairs={{1,2},{3,0},{2,1},{0,3},{5,6},{7,4},{6,5},{4,7},{9,10},{11,8},{10,... | collective-permute-start | bytes 786440 | tf_op jit(solution)/shard_map/ppermute | solution.py:512
  20.0 10.8 %collective-permute-start.4 = (f32[640,128]{1,0:T(8,128)S(1)}, f32[640,128]{1,0:T(8,128)S(1)}, u32[]{:S(2)}, u32[]{:S(2)}) collective-permute-start(f32[640,128]{1,0:T(8,128)S(1)} %get-tuple-element.57), channel_id=1, source_target_pairs={{128,0},{0,128},{129,1},{1,129},{130,2},{2,130},{131,3},{3,131},{1... | collective-permute-start | bytes 983048 | tf_op jit(solution)/shard_map/ppermute | solution.py:523
  26.4 7.7 %collective-permute-start.5 = (f32[384,128]{1,0:T(8,128)S(1)}, f32[384,128]{1,0:T(8,128)S(1)}, u32[]{:S(2)}, u32[]{:S(2)}) collective-permute-start(f32[384,128]{1,0:T(8,128)S(1)} %get-tuple-element.58), channel_id=1, source_target_pairs={{128,0},{0,128},{129,1},{1,129},{130,2},{2,130},{131,3},{3,131},{1... | collective-permute-start | bytes 589832 | tf_op jit(solution)/shard_map/ppermute | solution.py:523
  35.6 15.6 %collective-permute-start.8 = (f32[4,256,128]{2,1,0:T(8,128)S(1)}, f32[4,256,128]{2,1,0:T(8,128)S(1)}, u32[]{:S(2)}, u32[]{:S(2)}) collective-permute-start(f32[4,256,128]{2,1,0:T(8,128)S(1)} %get-tuple-element.67), channel_id=1, source_target_pairs={{0,4},{8,12},{16,20},{24,28},{32,36},{40,44},{48,52},{56,60},{64,6... | collective-permute-start | bytes 1572872 | tf_op jit(solution)/shard_map/ppermute | solution.py:512
  35.7 15.5 %collective-permute-start.9 = (f32[4,256,128]{2,1,0:T(8,128)S(1)}, f32[4,256,128]{2,1,0:T(8,128)S(1)}, u32[]{:S(2)}, u32[]{:S(2)}) collective-permute-start(f32[4,256,128]{2,1,0:T(8,128)S(1)} %get-tuple-element.68), channel_id=1, source_target_pairs={{4,8},{5,9},{6,10},{7,11},{12,16},{13,17},{14,18},{15,19},{20,24},... | collective-permute-start | bytes 1572872 | tf_op jit(solution)/shard_map/ppermute | solution.py:519
  38.1 8.8 %collective-permute-start.6 = (f32[4,8,16,128]{3,2,1,0:T(8,128)S(1)}, f32[4,8,16,128]{3,2,1,0:T(8,128)S(1)}, u32[]{:S(2)}, u32[]{:S(2)}) collective-permute-start(f32[4,8,16,128]{3,2,1,0:T(8,128)S(1)} %get-tuple-element.62), channel_id=1, source_target_pairs={{0,1},{2,3},{1,0},{3,2},{4,5},{6,7},{5,4},{7,6},{8,9},{10,11},{9,8... | collective-permute-start | bytes 786440 | tf_op jit(solution)/shard_map/ppermute | solution.py:512
  38.8 9.7 %collective-permute-start.7 = (f32[4,8,16,128]{3,2,1,0:T(8,128)S(1)}, f32[4,8,16,128]{3,2,1,0:T(8,128)S(1)}, u32[]{:S(2)}, u32[]{:S(2)}) collective-permute-start(f32[4,8,16,128]{3,2,1,0:T(8,128)S(1)} %get-tuple-element.63), channel_id=1, source_target_pairs={{1,2},{3,0},{2,1},{0,3},{5,6},{7,4},{6,5},{4,7},{9,10},{11,8},{10,... | collective-permute-start | bytes 786440 | tf_op jit(solution)/shard_map/ppermute | solution.py:512
  49.4 9.2 %collective-permute-start.10 = (f32[640,128]{1,0:T(8,128)S(1)}, f32[640,128]{1,0:T(8,128)S(1)}, u32[]{:S(2)}, u32[]{:S(2)}) collective-permute-start(f32[640,128]{1,0:T(8,128)S(1)} %get-tuple-element.70), channel_id=1, source_target_pairs={{128,0},{0,128},{129,1},{1,129},{130,2},{2,130},{131,3},{3,131},{1... | collective-permute-start | bytes 983048 | tf_op jit(solution)/shard_map/ppermute | solution.py:523
  55.2 7.6 %collective-permute-start.11 = (f32[384,128]{1,0:T(8,128)S(1)}, f32[384,128]{1,0:T(8,128)S(1)}, u32[]{:S(2)}, u32[]{:S(2)}) collective-permute-start(f32[384,128]{1,0:T(8,128)S(1)} %get-tuple-element.72), channel_id=1, source_target_pairs={{128,0},{0,128},{129,1},{1,129},{130,2},{2,130},{131,3},{3,131},{1... | collective-permute-start | bytes 589832 | tf_op jit(solution)/shard_map/ppermute | solution.py:523

commit v4 on v3

--- a/solution.py
+++ b/solution.py
@@ -166,41 +166,25 @@
     return jnp.concatenate(factor, axis=0)
 
 
-def predict(x, field, adjoint, loads, relaxed, high, low, lateral, central, given=None, conductance=None):
+def predict(x, field, adjoint, loads, relaxed, high, low, lateral, central, given=None, conductance=None, forcing=None):
     if given is None:
         factor, rest = flat(relaxed[:, x]), flat(loads[:, x])
     else:
         factor = row_factors(conductance, x, relaxed)
-        rest = factor * folded(both(flat(loads[:, x])), given[...])
+        rest = factor * folded(both(flat(forcing[:, x])), given[...])
         loads[:, x] = rest.reshape(NTD, LAYER, BLOCK)
     own, around = stencil_layer(x, flat(adjoint[:, x]), high, low, lateral, central)
     field[:, x] = (own + rest - factor * around).reshape(NTD, LAYER, BLOCK)
 
 
 def first_kernel(
-    info, initial, forcing, conductance, block_matrix_hbm, precond_hbm, faces_hbm, coupling_hbm,
-    field, adjoint, loads, relaxed, high, low, lateral, central, carry, given,
-    block_matrix, precond, faces, coupling, sems, small_sems,
+    info, initial, forcing, conductance, block_matrix, precond, faces, coupling,
+    field, adjoint, loads, relaxed, high, low, lateral, central, carry, given, sems,
 ):
-    small = [
-        pltpu.make_async_copy(source, target, small_sems.at[k])
-        for k, (source, target) in enumerate(
-            [(precond_hbm, precond), (faces_hbm, faces), (block_matrix_hbm, block_matrix), (coupling_hbm, coupling)]
-        )
-    ]
-    for copy in small:
-        copy.start()
-
-    def fetch(x, which):
-        source, target = ((initial, adjoint), (forcing, loads))[which]
-        return pltpu.make_async_copy(source.at[:, x], target.at[:, x], sems.at[which, x])
-
+    fetched = [pltpu.make_async_copy(initial.at[:, x], adjoint.at[:, x], sems.at[x]) for x in range(EX)]
     for x in range(3):
-        fetch(x, 0).start()
-    fetch(1, 1).start()
+        fetched[x].start()
     stencil_setup(high, low)
-    for copy in small:
-        copy.wait()
 
     zero = jnp.zeros((BLOCK, BLOCK), BF16)
     h, l = split(precond[...])
@@ -223,26 +207,21 @@
     )
 
     def enter(x):
-        fetch(x, 0).wait()
         position = lax.broadcasted_iota(jnp.int32, (NTD, LAYER, BLOCK), 1) + x * LAYER
+        fetched[x].wait()
+        if x + 3 < EX:
+            fetched[x + 3].start()
         value = jnp.where(position < info[0], adjoint[:, x], 0.0)
         adjoint[:, x] = value
         stencil_split(x, value, high, low)
 
     enter(0)
     enter(1)
-    later = {x: [(x + 2, 0), (x + 1, 1)] for x in layers(INNER)}
-    later[2] += [(0, 1)]
-    later[3] += [(EX - 1, 1)]
     for x in layers(INNER):
-        for piece in later[x]:
-            fetch(*piece).start()
         enter(x + 1)
-        fetch(x, 1).wait()
-        predict(x, field, adjoint, loads, relaxed, high, low, lateral, central, given, conductance)
-    enter(EX - 1)
-    for x in layers(OUTER):
-        fetch(x, 1).wait()
+        predict(x, field, adjoint, loads, relaxed, high, low, lateral, central, given, conductance, forcing)
+    for x in range(INNER[0][0] + INNER[0][1] + 1, EX):
+        enter(x)
 
 
 def first_prediction(info, initial, forcing, conductance, block_matrix, precond, faces, coupling):
@@ -251,16 +230,9 @@
         out_shape=[VMEM(STACK, F32)] * 4
         + [VMEM(PADDED, BF16)] * 2
         + [VMEM(LATERAL, BF16), VMEM(CENTRAL, BF16), VMEM(SQUARE, BF16), VMEM(SQUARE, BF16)],
-        in_specs=[INS, INH, INH, INV] + [INH] * 4,
+        in_specs=[INS, INH] + [INV] * 6,
         out_specs=[INV] * 10,
-        scratch_shapes=[
-            pltpu.VMEM((BLOCK, BLOCK), F32),
-            pltpu.VMEM((BLOCK, BLOCK), F32),
-            pltpu.VMEM((6, BLOCK, BLOCK), F32),
-            pltpu.VMEM((SPACE, BLOCK), F32),
-            pltpu.SemaphoreType.DMA((2, EX)),
-            pltpu.SemaphoreType.DMA((4,)),
-        ],
+        scratch_shapes=[pltpu.SemaphoreType.DMA((EX,))],
         compiler_params=params(16),
         cost_estimate=cost(0.01),
         name="first_inner",
@@ -274,7 +246,8 @@
     for x in layers(INNER):
         stencil_split(x + 1, adjoint[:, x + 1], high, low)
         predict(x, field, adjoint, loads, relaxed, high, low, lateral, central)
-    stencil_split(EX - 1, adjoint[:, EX - 1], high, low)
+    for x in range(INNER[0][0] + INNER[0][1] + 1, EX):
+        stencil_split(x, adjoint[:, x], high, low)
 
 
 def next_prediction(adjoint, loads, relaxed, lateral, central):
@@ -371,11 +344,11 @@
 
 def outer_kernel(first_sweep, info, *refs):
     if first_sweep:
-        conductance, given, *refs = refs
+        conductance, given, forcing, *refs = refs
         (_, _, _, _, _, adjoint, lateral, central, carry, x_near, x_far, y_near, y_far,
          field, high, low, loads, relaxed, trace) = refs
     else:
-        conductance = given = None
+        conductance = given = forcing = None
         (_, _, _, adjoint, lateral, central, carry, x_near, x_far, y_near, y_far, loads, relaxed,
          field, high, low, trace) = refs
     for halo, x, has in ((x_near, near(info, 0), 1), (x_far, far(info, 0), info[4])):
@@ -390,16 +363,16 @@
             high[x + 1, :, pl.ds(place, EZ)] = h
             low[x + 1, :, pl.ds(place, EZ)] = l
     for x in layers(OUTER):
-        predict(x, field, adjoint, loads, relaxed, high, low, lateral, central, given, conductance)
+        predict(x, field, adjoint, loads, relaxed, high, low, lateral, central, given, conductance, forcing)
     early_chain(info, field, relaxed, carry, OUTER, trace)
 
 
-def outer_prediction(info, field, high, low, adjoint, lateral, central, carry, halos, loads, relaxed, given, conductance):
+def outer_prediction(info, field, high, low, adjoint, lateral, central, carry, halos, loads, relaxed, given, conductance, forcing):
     first_sweep = given is not None
     if first_sweep:
-        args = [info, conductance, given, field, high, low, loads, relaxed, adjoint, lateral, central, carry, *halos]
+        args = [info, conductance, given, forcing, field, high, low, loads, relaxed, adjoint, lateral, central, carry, *halos]
         outs = [VMEM(STACK, F32), VMEM(PADDED, BF16), VMEM(PADDED, BF16), VMEM(STACK, F32), VMEM(STACK, F32)]
-        aliases = {k + 3: k for k in range(5)}
+        aliases = {k + 4: k for k in range(5)}
     else:
         args = [info, field, high, low, adjoint, lateral, central, carry, *halos, loads, relaxed]
         outs = [VMEM(STACK, F32), VMEM(PADDED, BF16), VMEM(PADDED, BF16)]
@@ -526,10 +499,7 @@
 def body(forcing, initial, conductance, counts, block_matrix, precond, face_coupling, time_coupling):
     shape = forcing.shape
     in_hbm = functools.partial(pltpu.with_memory_space_constraint, memory_space=pltpu.HBM)
-    forcing, initial = in_hbm(forcing.reshape(STACK)), in_hbm(initial.reshape(STACK))
-    block_matrix, precond, face_coupling, time_coupling = map(
-        in_hbm, (block_matrix, precond, face_coupling, time_coupling)
-    )
+    forcing, initial = forcing.reshape(STACK), in_hbm(initial.reshape(STACK))
     even_x = 1 - lax.rem(lax.axis_index("sx"), 2).astype(jnp.int32)
     even_y = 1 - lax.rem(lax.axis_index("sy"), 2).astype(jnp.int32)
     at_x, at_y = lax.axis_index("sx"), lax.axis_index("sy")
@@ -559,7 +529,7 @@
         field, inner = inner_halos(info, field, relaxed, lateral, carry, halos[2:])
         inner = sent_back(inner)
         field, outer, loads, relaxed = outer_prediction(
-            info, field, high, low, adjoint, lateral, central, carry, halos, loads, relaxed, given, conductance
+            info, field, high, low, adjoint, lateral, central, carry, halos, loads, relaxed, given, conductance, forcing
         )
         outer = sent_back(outer)
         if sweep < SWEEPS - 1:

time: 65.5 us -> 65 us (level)
    pallas_call x1, Pallas kernels: 9.88 us -> 9.06 us  [first_prediction(): pl.pallas_call(first_kernel, out_shape=[VMEM(STACK, F32)] * 4 + [VMEM(PAD...]
  transfers between devices with their start and end apart: 12 -> 12, of which waited for: 6 -> 6; matrix products, arithmetic and copies ran while one was open for 0% -> 0% of each run, Pallas kernels for 46% -> 45%
where the time goes in v4:
time: 65 us; the launch traced here: 64.7 us
  Pallas kernels  35.2 us (54%)
  starting transfers between devices  16.6 us (26%)
  waiting for transfers between devices  11.7 us (18%)
  between operations  1.07 us (2%)
    pallas_call x1, Pallas kernels, first_prediction(): pl.pallas_call(first_kernel, out_shape=[VMEM(STACK, F32)] * 4 + [VMEM(PAD...  9.06 us
    ppermute x4, waiting for transfers between devices, sent_back(): return lax.ppermute(value, 'tm', [(1, 0), (0, 1)])  8.55 us
    pallas_call x2, Pallas kernels, outer_prediction(): pl.pallas_call(functools.partial(outer_kernel, first_sweep), out_shape=ou...  8.5 us
    ppermute x4, starting transfers between devices, sent_back(): return lax.ppermute(value, 'tm', [(1, 0), (0, 1)])  6 us
    pallas_call x1, Pallas kernels, next_prediction(): pl.pallas_call(next_kernel, out_shape=[VMEM(STACK, F32), VMEM(PADDED, BF1...  5.73 us
    ppermute x6, starting transfers between devices, exchanged(): lax.ppermute(value, axis, both_ways([(i, (i + 1) % count) for i in range(...  5.45 us
    ppermute x2, starting transfers between devices, exchanged_far_x(): return lax.ppermute(value, ('sx', 'sy'), both_ways(pairs))  5.12 us
    pallas_call x2, Pallas kernels, last(): pl.pallas_call(last_inner_kernel if inner else last_outer_kernel, out_sha...  4.93 us
  transfers between devices with their start and end apart: 12, of which 6 were waited for; matrix products, arithmetic and copies ran while one was open for 0% of the time, Pallas kernels for 45%

profile of v4, /device:TPU:64, one launch (start us, length us, event | category | flops | bytes accessed | tf_op | source)
XLA Modules:
  0.0 64.7 jit_solution(17500681707460717181)
XLA Ops:
  0.8 0.1 stack.31.info
  0.8 2.2 %faces.3 = (f32[4,256,128]{2,1,0:T(8,128)S(1)}, f32[4,256,128]{2,1,0:T(8,128)S(1)}, f32[4,8,16,128]{3,2,1,0:T(8,128)S(1)}, f32[4,8,16,128]{3,2,1,0:T(8,128)S(1)}) custom-call(s32[6]{0:T(128)S(1)} %stack.31.info, f32[4,8,256,128]{3,2,1,0:T(8,128)} %bitcast.12), custom_call_target="tpu_custom_call" | custom-call | flops 2000000000 | tf_op jit(solution)/shard_map/faces/pallas_call | solution.py:91
  3.1 0.1 collective-permute-start.2
  3.2 2.7 %collective-permute-start.3 = (f32[4,256,128]{2,1,0:T(8,128)S(1)}, f32[4,256,128]{2,1,0:T(8,128)S(1)}, u32[]{:S(2)}, u32[]{:S(2)}) collective-permute-start(f32[4,256,128]{2,1,0:T(8,128)S(1)} %get-tuple-element.54), channel_id=1, source_target_pairs={{4,8},{5,9},{6,10},{7,11},{12,16},{13,17},{14,18},{15,19},{20,24},... | collective-permute-start | bytes 1572872 | tf_op jit(solution)/shard_map/ppermute | solution.py:492
  5.8 1.6 %collective-permute-start = (f32[4,8,16,128]{3,2,1,0:T(8,128)S(1)}, f32[4,8,16,128]{3,2,1,0:T(8,128)S(1)}, u32[]{:S(2)}, u32[]{:S(2)}) collective-permute-start(f32[4,8,16,128]{3,2,1,0:T(8,128)S(1)} %get-tuple-element.45), channel_id=1, source_target_pairs={{0,1},{2,3},{1,0},{3,2},{4,5},{6,7},{5,4},{7,6},{8,9},{10,11},{9,8... | collective-permute-start | bytes 786440 | tf_op jit(solution)/shard_map/ppermute | solution.py:485
  7.4 2.2 %collective-permute-start.1 = (f32[4,8,16,128]{3,2,1,0:T(8,128)S(1)}, f32[4,8,16,128]{3,2,1,0:T(8,128)S(1)}, u32[]{:S(2)}, u32[]{:S(2)}) collective-permute-start(f32[4,8,16,128]{3,2,1,0:T(8,128)S(1)} %get-tuple-element.46), channel_id=1, source_target_pairs={{1,2},{3,0},{2,1},{0,3},{5,6},{7,4},{6,5},{4,7},{9,10},{11,8},{10,... | collective-permute-start | bytes 786440 | tf_op jit(solution)/shard_map/ppermute | solution.py:485
  9.6 9.1 %first_inner.1 = (f32[4,8,256,128]{3,2,1,0:T(8,128)S(1)}, f32[4,8,256,128]{3,2,1,0:T(8,128)S(1)}, f32[4,8,256,128]{3,2,1,0:T(8,128)S(1)}, f32[4,8,256,128]{3,2,1...) custom-call(s32[6]{0:T(128)S(1)} %stack.31.info, ...), custom_call_target="tpu_custom_call" | custom-call | flops 10000000 | tf_op jit(solution)/shard_map/first_inner/pallas_call | solution.py:228
  18.7 0.0 collective-permute-done.y_near.refs_14_
  18.7 0.0 collective-permute-done.1.y_far.refs_15_
  18.7 0.8 %inner_halos.2 = (f32[4,8,256,128]{3,2,1,0:T(8,128)S(1)}, f32[640,128]{1,0:T(8,128)S(1)}) custom-call(s32[6]{0:T(128)S(1)} %stack.31.info, f32[4,8,256,128]{3,2,1,0:T(8,128)S(1)} %get-tuple-element.41.pred, f32[4,8,256,128]{3,2,1,0:T(8,128)S(1)} %get-tuple-element.42.relaxed.refs_7_, ...), custom_call_target="tpu_custom_call", output_to_operand_aliasing={{0}: (1, {})} | custom-call | flops 2000000000 | tf_op jit(solution)/shard_map/inner_halos/pallas_call | solution.py:333
  19.6 1.9 %collective-permute-start.4 = (f32[640,128]{1,0:T(8,128)S(1)}, f32[640,128]{1,0:T(8,128)S(1)}, u32[]{:S(2)}, u32[]{:S(2)}) collective-permute-start(f32[640,128]{1,0:T(8,128)S(1)} %get-tuple-element.57), channel_id=1, source_target_pairs={{128,0},{0,128},{129,1},{1,129},{130,2},{2,130},{131,3},{3,131},{1... | collective-permute-start | bytes 983048 | tf_op jit(solution)/shard_map/ppermute | solution.py:496
  21.4 4.5 %first_outer.1 = (f32[4,8,256,128]{3,2,1,0:T(8,128)S(1)}, bf16[10,4,288,128]{3,2,1,0:T(8,128)(2,1)S(1)}, bf16[10,4,288,128]{3,2,1,0:T(8,128)(2,1)S(1)}, f32[4,8,...) custom-call(s32[6]{0:T(128)S(1)} %stack.31.info, ...), custom_call_target="tpu_custom_call", output_to_operand_aliasing={{0}: (4, {}), {1}: (5, {}), {2}: (6, {}), {3}: (7, {}), {4}... | custom-call | flops 7000000000 | tf_op jit(solution)/shard_map/first_outer/pallas_call | solution.py:381
  26.0 1.2 %collective-permute-start.5 = (f32[384,128]{1,0:T(8,128)S(1)}, f32[384,128]{1,0:T(8,128)S(1)}, u32[]{:S(2)}, u32[]{:S(2)}) collective-permute-start(f32[384,128]{1,0:T(8,128)S(1)} %get-tuple-element.58), channel_id=1, source_target_pairs={{128,0},{0,128},{129,1},{1,129},{130,2},{2,130},{131,3},{3,131},{1... | collective-permute-start | bytes 589832 | tf_op jit(solution)/shard_map/ppermute | solution.py:496
  27.2 3.2 %collective-permute-done.4.trace = f32[640,128]{1,0:T(8,128)S(1)} collective-permute-done((f32[640,128]{1,0:T(8,128)S(1)}, f32[640,128]{1,0:T(8,128)S(1)}, u32[]{:S(2)}, u32[]{:S(2)}) %collective-permute-start.4) | collective-permute-done | bytes 327712 | tf_op jit(solution)/shard_map/ppermute | solution.py:496
  30.4 1.7 %late_inner.1.field = f32[4,8,256,128]{3,2,1,0:T(8,128)S(1)} custom-call(s32[6]{0:T(128)S(1)} %stack.31.info, f32[4,8,256,128]{3,2,1,0:T(8,128)S(1)} %get-tuple-element.55.field, f32[4,8,256,128]{3,2,1,0:T(8,128)S(1)} %get-tuple-element.56.relaxed.refs_12_, ...), custom_call_target="tpu_custom_call", output_to_operand_aliasing={{}: (1, {})} | custom-call | flops 2000000000 | tf_op jit(solution)/shard_map/late_inner/pallas_call | solution.py:416
  32.1 1.6 %collective-permute-done.5.trace = f32[384,128]{1,0:T(8,128)S(1)} collective-permute-done((f32[384,128]{1,0:T(8,128)S(1)}, f32[384,128]{1,0:T(8,128)S(1)}, u32[]{:S(2)}, u32[]{:S(2)}) %collective-permute-start.5) | collective-permute-done | bytes 196640 | tf_op jit(solution)/shard_map/ppermute | solution.py:496
  33.7 1.4 %late_outer.1 = (f32[4,8,256,128]{3,2,1,0:T(8,128)S(1)}, f32[4,256,128]{2,1,0:T(8,128)S(1)}, f32[4,256,128]{2,1,0:T(8,128)S(1)}, f32[4,8,16,128]{3,2,1,0:T(8,128)S(1)}, f32[4,8,16,128]{3,2,1,0:T(8,128)S(1)}) custom-call(s32[6]{0:T(128)S(1)} %stack.31.info, f32[4,8,256,128]{3,2,1,0:T(8,128)S(1)} %late_inner.1.field, ...), custom_call_target="tpu_custom_call", output_to_operand_aliasing={{0}: (1, {})} | custom-call | flops 2000000000 | tf_op jit(solution)/shard_map/late_outer/pallas_call | solution.py:416
  35.1 0.1 collective-permute-start.8
  35.2 2.4 %collective-permute-start.9 = (f32[4,256,128]{2,1,0:T(8,128)S(1)}, f32[4,256,128]{2,1,0:T(8,128)S(1)}, u32[]{:S(2)}, u32[]{:S(2)}) collective-permute-start(f32[4,256,128]{2,1,0:T(8,128)S(1)} %get-tuple-element.68), channel_id=1, source_target_pairs={{4,8},{5,9},{6,10},{7,11},{12,16},{13,17},{14,18},{15,19},{20,24},... | collective-permute-start | bytes 1572872 | tf_op jit(solution)/shard_map/ppermute | solution.py:492
  37.7 0.7 %collective-permute-start.6 = (f32[4,8,16,128]{3,2,1,0:T(8,128)S(1)}, f32[4,8,16,128]{3,2,1,0:T(8,128)S(1)}, u32[]{:S(2)}, u32[]{:S(2)}) collective-permute-start(f32[4,8,16,128]{3,2,1,0:T(8,128)S(1)} %get-tuple-element.62), channel_id=1, source_target_pairs={{0,1},{2,3},{1,0},{3,2},{4,5},{6,7},{5,4},{7,6},{8,9},{10,11},{9,8... | collective-permute-start | bytes 786440 | tf_op jit(solution)/shard_map/ppermute | solution.py:485
  38.3 0.8 %collective-permute-start.7 = (f32[4,8,16,128]{3,2,1,0:T(8,128)S(1)}, f32[4,8,16,128]{3,2,1,0:T(8,128)S(1)}, u32[]{:S(2)}, u32[]{:S(2)}) collective-permute-start(f32[4,8,16,128]{3,2,1,0:T(8,128)S(1)} %get-tuple-element.63), channel_id=1, source_target_pairs={{1,2},{3,0},{2,1},{0,3},{5,6},{7,4},{6,5},{4,7},{9,10},{11,8},{10,... | collective-permute-start | bytes 786440 | tf_op jit(solution)/shard_map/ppermute | solution.py:485
  39.2 5.7 %next_inner.1 = (f32[4,8,256,128]{3,2,1,0:T(8,128)S(1)}, bf16[10,4,288,128]{3,2,1,0:T(8,128)(2,1)S(1)}, bf16[10,4,288,128]{3,2,1,0:T(8,128)(2,1)S(1)}) custom-call(f32[4,8,256,128]{3,2,1,0:T(8,128)S(1)} %get-tuple-element.59.adjoint.refs_3_, f32[4,8,256,128]{3,2,1,0:T(8,128)S(1)} %get-tuple-element.60.loads.refs_11_, ...), custom_call_target="tpu_custom_call" | custom-call | flops 10000000 | tf_op jit(solution)/shard_map/next_inner/pallas_call | solution.py:254
  44.9 1.5 %collective-permute-done.6.y_near.refs_9_ = f32[4,8,16,128]{3,2,1,0:T(8,128)S(1)} collective-permute-done((f32[4,8,16,128]{3,2,1,0:T(8,128)S(1)}, f32[4,8,16,128]{3,2,1,0:T(8,128)S(1)}, u32[]{:S(2)}, u32[]{:S(2)}) %collective-permute-start.6) | collective-permute-done | bytes 262176 | tf_op jit(solution)/shard_map/ppermute | solution.py:485
  46.4 1.6 %collective-permute-done.7.y_far.refs_10_ = f32[4,8,16,128]{3,2,1,0:T(8,128)S(1)} collective-permute-done((f32[4,8,16,128]{3,2,1,0:T(8,128)S(1)}, f32[4,8,16,128]{3,2,1,0:T(8,128)S(1)}, u32[]{:S(2)}, u32[]{:S(2)}) %collective-permute-start.7) | collective-permute-done | bytes 262176 | tf_op jit(solution)/shard_map/ppermute | solution.py:485
  48.1 0.8 %inner_halos.3 = (f32[4,8,256,128]{3,2,1,0:T(8,128)S(1)}, f32[640,128]{1,0:T(8,128)S(1)}) custom-call(s32[6]{0:T(128)S(1)} %stack.31.info, f32[4,8,256,128]{3,2,1,0:T(8,128)S(1)} %get-tuple-element.61.pred, f32[4,8,256,128]{3,2,1,0:T(8,128)S(1)} %get-tuple-element.56.relaxed.refs_12_, ...), custom_call_target="tpu_custom_call", output_to_operand_aliasing={{0}: (1, {})} | custom-call | flops 2000000000 | tf_op jit(solution)/shard_map/inner_halos/pallas_call | solution.py:333
  48.9 1.8 %collective-permute-start.10 = (f32[640,128]{1,0:T(8,128)S(1)}, f32[640,128]{1,0:T(8,128)S(1)}, u32[]{:S(2)}, u32[]{:S(2)}) collective-permute-start(f32[640,128]{1,0:T(8,128)S(1)} %get-tuple-element.70), channel_id=1, source_target_pairs={{128,0},{0,128},{129,1},{1,129},{130,2},{2,130},{131,3},{3,131},{1... | collective-permute-start | bytes 983048 | tf_op jit(solution)/shard_map/ppermute | solution.py:496
  50.7 4.0 %next_outer.1 = (f32[4,8,256,128]{3,2,1,0:T(8,128)S(1)}, bf16[10,4,288,128]{3,2,1,0:T(8,128)(2,1)S(1)}, bf16[10,4,288,128]{3,2,1,0:T(8,128)(2,1)S(1)}, f32[384,128]{1,0:T(8,128)S(1)}) custom-call(s32[6]{0:T(128)S(1)} %stack.31.info, f32[4,8,256,128]{3,2,1,0:T(8,128)S(1)} %get-tuple-element.64.refs_0_, ...), custom_call_target="tpu_custom_call", output_to_operand_aliasing={{0}: (1, {}), {1}: (2, {}), {2}: (3, {})} | custom-call | flops 7000000000 | tf_op jit(solution)/shard_map/next_outer/pallas_call | solution.py:381
  54.7 1.1 %collective-permute-start.11 = (f32[384,128]{1,0:T(8,128)S(1)}, f32[384,128]{1,0:T(8,128)S(1)}, u32[]{:S(2)}, u32[]{:S(2)}) collective-permute-start(f32[384,128]{1,0:T(8,128)S(1)} %get-tuple-element.72), channel_id=1, source_target_pairs={{128,0},{0,128},{129,1},{1,129},{130,2},{2,130},{131,3},{3,131},{1... | collective-permute-start | bytes 589832 | tf_op jit(solution)/shard_map/ppermute | solution.py:496
  55.8 2.3 %collective-permute-done.10.trace = f32[640,128]{1,0:T(8,128)S(1)} collective-permute-done((f32[640,128]{1,0:T(8,128)S(1)}, f32[640,128]{1,0:T(8,128)S(1)}, u32[]{:S(2)}, u32[]{:S(2)}) %collective-permute-start.10) | collective-permute-done | bytes 327712 | tf_op jit(solution)/shard_map/ppermute | solution.py:496
  58.1 2.7 %last_inner.1 = (f32[4,8,256,128]{3,2,1,0:T(8,128)S(1)}, f32[4,8,256,128]{3,2,1,0:T(8,128)}) custom-call(s32[6]{0:T(128)S(1)} %stack.31.info, f32[4,8,256,128]{3,2,1,0:T(8,128)S(1)} %get-tuple-element.69.field, f32[4,8,256,128]{3,2,1,0:T(8,128)S(1)} %get-tuple-element.56.relaxed.refs_12_, ...), custom_call_target="tpu_custom_call", output_to_operand_aliasing={{0}: (1, {})} | custom-call | flops 3000000000 | tf_op jit(solution)/shard_map/last_inner/pallas_call | solution.py:466
  60.9 1.5 %collective-permute-done.11.trace = f32[384,128]{1,0:T(8,128)S(1)} collective-permute-done((f32[384,128]{1,0:T(8,128)S(1)}, f32[384,128]{1,0:T(8,128)S(1)}, u32[]{:S(2)}, u32[]{:S(2)}) %collective-permute-start.11) | collective-permute-done | bytes 196640 | tf_op jit(solution)/shard_map/ppermute | solution.py:496
  62.3 2.2 %last_outer.1 = (f32[4,8,256,128]{3,2,1,0:T(8,128)S(1)}, f32[4,8,256,128]{3,2,1,0:T(8,128)}) custom-call(s32[6]{0:T(128)S(1)} %stack.31.info, f32[4,8,256,128]{3,2,1,0:T(8,128)S(1)} %get-tuple-element.71.field, f32[4,8,256,128]{3,2,1,0:T(8,128)S(1)} %get-tuple-element.56.relaxed.refs_12_, ...), custom_call_target="tpu_custom_call", output_to_operand_aliasing={{0}: (1, {}), {1}: (5, {})} | custom-call | flops 3000000000 | tf_op jit(solution)/shard_map/last_outer/pallas_call | solution.py:466
  (16 shorter events, 0.0 us)
Async XLA Ops:
  0.0 9.6 %copy-start.1 = (f32[4,8,16,16]{3,2,1,0:T(8,128)S(1)}, f32[4,8,16,16]{3,2,1,0:T(8,128)}, u32[]{:S(2)}) copy-start(f32[4,8,16,16]{3,2,1,0:T(8,128)} %refs_0_.1) | copy-start | bytes 98308
  0.0 9.6 %copy-start.5 = (f32[64,128]{1,0:T(8,128)S(1)}, f32[64,128]{1,0:T(8,128)}, u32[]{:S(2)}) copy-start(f32[64,128]{1,0:T(8,128)} %coupling.1) | copy-start | bytes 98308
  0.0 9.6 %copy-start.2 = (f32[6,128,128]{2,1,0:T(8,128)S(1)}, f32[6,128,128]{2,1,0:T(8,128)}, u32[]{:S(2)}) copy-start(f32[6,128,128]{2,1,0:T(8,128)} %faces.2) | copy-start | bytes 1179652
  0.0 9.6 %copy-start.4 = (f32[128,128]{1,0:T(8,128)S(1)}, f32[128,128]{1,0:T(8,128)}, u32[]{:S(2)}) copy-start(f32[128,128]{1,0:T(8,128)} %precond.1) | copy-start | bytes 196612
  0.0 9.6 %copy-start.3 = (f32[128,128]{1,0:T(8,128)S(1)}, f32[128,128]{1,0:T(8,128)}, u32[]{:S(2)}) copy-start(f32[128,128]{1,0:T(8,128)} %block_matrix.1) | copy-start | bytes 196612
  0.8 8.8 %copy-start = (f32[4,8,16,16,128]{4,3,2,1,0:T(8,128)S(1)}, f32[4,8,16,16,128]{4,3,2,1,0:T(8,128)}, u32[]{:S(2)}) copy-start(f32[4,8,16,16,128]{4,3,2,1,0:T(8,128)} %param.8) | copy-start | bytes 12582916
  3.1 18.4 %collective-permute-start.2 = (f32[4,256,128]{2,1,0:T(8,128)S(1)}, f32[4,256,128]{2,1,0:T(8,128)S(1)}, u32[]{:S(2)}, u32[]{:S(2)}) collective-permute-start(f32[4,256,128]{2,1,0:T(8,128)S(1)} %get-tuple-element.53), channel_id=1, source_target_pairs={{0,4},{8,12},{16,20},{24,28},{32,36},{40,44},{48,52},{56,60},{64,6... | collective-permute-start | bytes 1572872 | tf_op jit(solution)/shard_map/ppermute | solution.py:485
  3.2 18.3 %collective-permute-start.3 = (f32[4,256,128]{2,1,0:T(8,128)S(1)}, f32[4,256,128]{2,1,0:T(8,128)S(1)}, u32[]{:S(2)}, u32[]{:S(2)}) collective-permute-start(f32[4,256,128]{2,1,0:T(8,128)S(1)} %get-tuple-element.54), channel_id=1, source_target_pairs={{4,8},{5,9},{6,10},{7,11},{12,16},{13,17},{14,18},{15,19},{20,24},... | collective-permute-start | bytes 1572872 | tf_op jit(solution)/shard_map/ppermute | solution.py:492
  5.8 12.9 %collective-permute-start = (f32[4,8,16,128]{3,2,1,0:T(8,128)S(1)}, f32[4,8,16,128]{3,2,1,0:T(8,128)S(1)}, u32[]{:S(2)}, u32[]{:S(2)}) collective-permute-start(f32[4,8,16,128]{3,2,1,0:T(8,128)S(1)} %get-tuple-element.45), channel_id=1, source_target_pairs={{0,1},{2,3},{1,0},{3,2},{4,5},{6,7},{5,4},{7,6},{8,9},{10,11},{9,8... | collective-permute-start | bytes 786440 | tf_op jit(solution)/shard_map/ppermute | solution.py:485
  7.4 11.3 %collective-permute-start.1 = (f32[4,8,16,128]{3,2,1,0:T(8,128)S(1)}, f32[4,8,16,128]{3,2,1,0:T(8,128)S(1)}, u32[]{:S(2)}, u32[]{:S(2)}) collective-permute-start(f32[4,8,16,128]{3,2,1,0:T(8,128)S(1)} %get-tuple-element.46), channel_id=1, source_target_pairs={{1,2},{3,0},{2,1},{0,3},{5,6},{7,4},{6,5},{4,7},{9,10},{11,8},{10,... | collective-permute-start | bytes 786440 | tf_op jit(solution)/shard_map/ppermute | solution.py:485
  19.6 10.8 %collective-permute-start.4 = (f32[640,128]{1,0:T(8,128)S(1)}, f32[640,128]{1,0:T(8,128)S(1)}, u32[]{:S(2)}, u32[]{:S(2)}) collective-permute-start(f32[640,128]{1,0:T(8,128)S(1)} %get-tuple-element.57), channel_id=1, source_target_pairs={{128,0},{0,128},{129,1},{1,129},{130,2},{2,130},{131,3},{3,131},{1... | collective-permute-start | bytes 983048 | tf_op jit(solution)/shard_map/ppermute | solution.py:496
  26.0 7.7 %collective-permute-start.5 = (f32[384,128]{1,0:T(8,128)S(1)}, f32[384,128]{1,0:T(8,128)S(1)}, u32[]{:S(2)}, u32[]{:S(2)}) collective-permute-start(f32[384,128]{1,0:T(8,128)S(1)} %get-tuple-element.58), channel_id=1, source_target_pairs={{128,0},{0,128},{129,1},{1,129},{130,2},{2,130},{131,3},{3,131},{1... | collective-permute-start | bytes 589832 | tf_op jit(solution)/shard_map/ppermute | solution.py:496
  35.1 15.6 %collective-permute-start.8 = (f32[4,256,128]{2,1,0:T(8,128)S(1)}, f32[4,256,128]{2,1,0:T(8,128)S(1)}, u32[]{:S(2)}, u32[]{:S(2)}) collective-permute-start(f32[4,256,128]{2,1,0:T(8,128)S(1)} %get-tuple-element.67), channel_id=1, source_target_pairs={{0,4},{8,12},{16,20},{24,28},{32,36},{40,44},{48,52},{56,60},{64,6... | collective-permute-start | bytes 1572872 | tf_op jit(solution)/shard_map/ppermute | solution.py:485
  35.2 15.5 %collective-permute-start.9 = (f32[4,256,128]{2,1,0:T(8,128)S(1)}, f32[4,256,128]{2,1,0:T(8,128)S(1)}, u32[]{:S(2)}, u32[]{:S(2)}) collective-permute-start(f32[4,256,128]{2,1,0:T(8,128)S(1)} %get-tuple-element.68), channel_id=1, source_target_pairs={{4,8},{5,9},{6,10},{7,11},{12,16},{13,17},{14,18},{15,19},{20,24},... | collective-permute-start | bytes 1572872 | tf_op jit(solution)/shard_map/ppermute | solution.py:492
  37.7 8.8 %collective-permute-start.6 = (f32[4,8,16,128]{3,2,1,0:T(8,128)S(1)}, f32[4,8,16,128]{3,2,1,0:T(8,128)S(1)}, u32[]{:S(2)}, u32[]{:S(2)}) collective-permute-start(f32[4,8,16,128]{3,2,1,0:T(8,128)S(1)} %get-tuple-element.62), channel_id=1, source_target_pairs={{0,1},{2,3},{1,0},{3,2},{4,5},{6,7},{5,4},{7,6},{8,9},{10,11},{9,8... | collective-permute-start | bytes 786440 | tf_op jit(solution)/shard_map/ppermute | solution.py:485
  38.3 9.7 %collective-permute-start.7 = (f32[4,8,16,128]{3,2,1,0:T(8,128)S(1)}, f32[4,8,16,128]{3,2,1,0:T(8,128)S(1)}, u32[]{:S(2)}, u32[]{:S(2)}) collective-permute-start(f32[4,8,16,128]{3,2,1,0:T(8,128)S(1)} %get-tuple-element.63), channel_id=1, source_target_pairs={{1,2},{3,0},{2,1},{0,3},{5,6},{7,4},{6,5},{4,7},{9,10},{11,8},{10,... | collective-permute-start | bytes 786440 | tf_op jit(solution)/shard_map/ppermute | solution.py:485
  48.9 9.2 %collective-permute-start.10 = (f32[640,128]{1,0:T(8,128)S(1)}, f32[640,128]{1,0:T(8,128)S(1)}, u32[]{:S(2)}, u32[]{:S(2)}) collective-permute-start(f32[640,128]{1,0:T(8,128)S(1)} %get-tuple-element.70), channel_id=1, source_target_pairs={{128,0},{0,128},{129,1},{1,129},{130,2},{2,130},{131,3},{3,131},{1... | collective-permute-start | bytes 983048 | tf_op jit(solution)/shard_map/ppermute | solution.py:496
  54.7 7.6 %collective-permute-start.11 = (f32[384,128]{1,0:T(8,128)S(1)}, f32[384,128]{1,0:T(8,128)S(1)}, u32[]{:S(2)}, u32[]{:S(2)}) collective-permute-start(f32[384,128]{1,0:T(8,128)S(1)} %get-tuple-element.72), channel_id=1, source_target_pairs={{128,0},{0,128},{129,1},{1,129},{130,2},{2,130},{131,3},{3,131},{1... | collective-permute-start | bytes 589832 | tf_op jit(solution)/shard_map/ppermute | solution.py:496

commit v5 on v4

--- a/solution.py
+++ b/solution.py
@@ -17,9 +17,10 @@
 ANY = pl.BlockSpec(memory_space=pl.ANY)
 INH = pl.BlockSpec(memory_space=pltpu.HBM)
 INV = pl.BlockSpec(memory_space=VMEM)
-INS = pl.BlockSpec(memory_space=pltpu.SMEM)
 INNER = ((1, 5),)
 OUTER = ((0, 1), (6, 2))
+NEXT_INNER = ((1, 6),)
+NEXT_OUTER = ((0, 1), (7, 1))
 
 
 def params(mib):
@@ -54,6 +55,18 @@
     return position < info[0]
 
 
+def facts(count):
+    at_x, at_y = lax.axis_index("sx"), lax.axis_index("sy")
+    return (
+        count[0:1, :],
+        lax.axis_index("tm"),
+        jnp.where(lax.rem(at_x, 2) == 0, EX - 1, 0),
+        jnp.where(lax.rem(at_y, 2) == 0, LAYER - EZ, 0),
+        jnp.logical_and(at_x > 0, at_x < lax.axis_size("sx") - 1).astype(jnp.int32),
+        jnp.logical_and(at_y > 0, at_y < lax.axis_size("sy") - 1).astype(jnp.int32),
+    )
+
+
 def near(info, dim):
     return pl.multiple_of(info[3], EZ) if dim else info[2]
 
@@ -63,6 +76,7 @@
 
 
 def faces_kernel(info, initial, x_near, x_far, y_near, y_far, sems):
+    info = facts(info)
     places = (near(info, 0), far(info, 0), near(info, 1), far(info, 1))
     refs = (x_near, x_far, y_near, y_far)
     copies = [
@@ -91,7 +105,7 @@
     return pl.pallas_call(
         faces_kernel,
         out_shape=FACES,
-        in_specs=[INS, INH],
+        in_specs=[INV, INH],
         out_specs=[INV] * 4,
         scratch_shapes=[pltpu.SemaphoreType.DMA((4,))],
         compiler_params=params(4),
@@ -181,6 +195,7 @@
     info, initial, forcing, conductance, block_matrix, precond, faces, coupling,
     field, adjoint, loads, relaxed, high, low, lateral, central, carry, given, sems,
 ):
+    info = facts(info)
     fetched = [pltpu.make_async_copy(initial.at[:, x], adjoint.at[:, x], sems.at[x]) for x in range(EX)]
     for x in range(3):
         fetched[x].start()
@@ -230,7 +245,7 @@
         out_shape=[VMEM(STACK, F32)] * 4
         + [VMEM(PADDED, BF16)] * 2
         + [VMEM(LATERAL, BF16), VMEM(CENTRAL, BF16), VMEM(SQUARE, BF16), VMEM(SQUARE, BF16)],
-        in_specs=[INS, INH] + [INV] * 6,
+        in_specs=[INV, INH] + [INV] * 6,
         out_specs=[INV] * 10,
         scratch_shapes=[pltpu.SemaphoreType.DMA((EX,))],
         compiler_params=params(16),
@@ -243,11 +258,9 @@
     stencil_setup(high, low)
     for x in range(2):
         stencil_split(x, adjoint[:, x], high, low)
-    for x in layers(INNER):
+    for x in layers(NEXT_INNER):
         stencil_split(x + 1, adjoint[:, x + 1], high, low)
         predict(x, field, adjoint, loads, relaxed, high, low, lateral, central)
-    for x in range(INNER[0][0] + INNER[0][1] + 1, EX):
-        stencil_split(x, adjoint[:, x], high, low)
 
 
 def next_prediction(adjoint, loads, relaxed, lateral, central):
@@ -318,8 +331,9 @@
     return jnp.concatenate([lateral[pl.ds(top, BLOCK), :], lateral[pl.ds(bottom, BLOCK), :]], axis=0)
 
 
-def inner_kernel(info, pred, relaxed, lateral, carry, y_near, y_far, field, trace):
-    ((first, count),) = INNER
+def inner_kernel(predicted, info, pred, relaxed, lateral, carry, y_near, y_far, field, trace):
+    info = facts(info)
+    ((first, count),) = predicted
     for halo, at, has in ((y_near, near(info, 1), 1), (y_far, far(info, 1), info[5])):
         matrix = face_matrix(lateral, 2 + (at > 0).astype(jnp.int32))
         values = jnp.where(has > 0, halo[:, first : first + count].reshape(NTD * count * EZ, BLOCK), 0.0)
@@ -329,11 +343,11 @@
     early_chain(info, field, relaxed, carry, INNER, trace)
 
 
-def inner_halos(info, field, relaxed, lateral, carry, y_halos):
+def inner_halos(info, field, relaxed, lateral, carry, y_halos, predicted):
     return pl.pallas_call(
-        inner_kernel,
+        functools.partial(inner_kernel, predicted),
         out_shape=[VMEM(STACK, F32), trace_shape(INNER)],
-        in_specs=[INS] + [INV] * 6,
+        in_specs=[INV] + [INV] * 6,
         out_specs=[INV, INV],
         input_output_aliases={1: 0},
         compiler_params=params(8),
@@ -343,6 +357,8 @@
 
 
 def outer_kernel(first_sweep, info, *refs):
+    info = facts(info)
+    predicted = OUTER if first_sweep else NEXT_OUTER
     if first_sweep:
         conductance, given, forcing, *refs = refs
         (_, _, _, _, _, adjoint, lateral, central, carry, x_near, x_far, y_near, y_far,
@@ -358,11 +374,11 @@
         low[place, :, pl.ds(EZ, LAYER)] = l
     for halo, y, has in ((y_near, near(info, 1), 1), (y_far, far(info, 1), info[5])):
         place = pl.multiple_of(jnp.where(y > 0, LAYER + EZ, 0), EZ)
-        for x in layers(OUTER):
+        for x in layers(predicted):
             h, l = split(jnp.where(has > 0, halo[:, x], 0.0))
             high[x + 1, :, pl.ds(place, EZ)] = h
             low[x + 1, :, pl.ds(place, EZ)] = l
-    for x in layers(OUTER):
+    for x in layers(predicted):
         predict(x, field, adjoint, loads, relaxed, high, low, lateral, central, given, conductance, forcing)
     early_chain(info, field, relaxed, carry, OUTER, trace)
 
@@ -381,7 +397,7 @@
     out = pl.pallas_call(
         functools.partial(outer_kernel, first_sweep),
         out_shape=outs,
-        in_specs=[INS] + [INV] * (len(args) - 1),
+        in_specs=[INV] + [INV] * (len(args) - 1),
         out_specs=[INV] * len(outs),
         input_output_aliases=aliases,
         compiler_params=params(16),
@@ -400,10 +416,12 @@
 
 
 def late_inner_kernel(info, field, relaxed, carry, trace, out):
+    info = facts(info)
     late_chain(info, out, relaxed, carry, trace, INNER)
 
 
 def late_outer_kernel(info, field, relaxed, carry, trace, out, x_near, x_far, y_near, y_far):
+    info = facts(info)
     late_chain(info, out, relaxed, carry, trace, OUTER)
     x_near[...] = out[:, near(info, 0)]
     x_far[...] = out[:, far(info, 0)]
@@ -416,7 +434,7 @@
     return pl.pallas_call(
         late_inner_kernel if inner else late_outer_kernel,
         out_shape=outs,
-        in_specs=[INS] + [INV] * 4,
+        in_specs=[INV] + [INV] * 4,
         out_specs=[INV] * len(outs),
         input_output_aliases={1: 0},
         compiler_params=params(8),
@@ -453,10 +471,12 @@
 
 
 def last_inner_kernel(info, field, relaxed, carry, trace, kept, out, sems):
+    info = facts(info)
     last_chain(info, relaxed, carry, trace, kept, out, sems, INNER)
 
 
 def last_outer_kernel(info, field, relaxed, carry, trace, given, kept, out, sems):
+    info = facts(info)
     last_chain(info, relaxed, carry, trace, kept, out, sems, OUTER)
 
 
@@ -466,7 +486,7 @@
     return pl.pallas_call(
         last_inner_kernel if inner else last_outer_kernel,
         out_shape=[VMEM(STACK, F32), pltpu.HBM(STACK, F32)],
-        in_specs=[INS] + [INV] * 4 + ([] if inner else [INH]),
+        in_specs=[INV] + [INV] * 4 + ([] if inner else [INH]),
         out_specs=[INV, INH],
         input_output_aliases={1: 0} if inner else {1: 0, 5: 1},
         scratch_shapes=[pltpu.SemaphoreType.DMA((NTD, 2))],
@@ -500,17 +520,7 @@
     shape = forcing.shape
     in_hbm = functools.partial(pltpu.with_memory_space_constraint, memory_space=pltpu.HBM)
     forcing, initial = forcing.reshape(STACK), in_hbm(initial.reshape(STACK))
-    even_x = 1 - lax.rem(lax.axis_index("sx"), 2).astype(jnp.int32)
-    even_y = 1 - lax.rem(lax.axis_index("sy"), 2).astype(jnp.int32)
-    at_x, at_y = lax.axis_index("sx"), lax.axis_index("sy")
-    has_x = jnp.logical_and(at_x > 0, at_x < lax.axis_size("sx") - 1).astype(jnp.int32)
-    has_y = jnp.logical_and(at_y > 0, at_y < lax.axis_size("sy") - 1).astype(jnp.int32)
-    info = jnp.stack(
-        [
-            counts[0, 0], lax.axis_index("tm").astype(jnp.int32),
-            even_x * (EX - 1), even_y * (LAYER - EZ), has_x, has_y,
-        ]
-    )
+    info = jnp.full((8, BLOCK), counts[0, 0])
 
     def halos_of(x_near, x_far, y_near, y_far):
         return (
@@ -526,7 +536,9 @@
         if sweep:
             adjoint, given = field, None
             field, high, low = next_prediction(adjoint, loads, relaxed, lateral, central)
-        field, inner = inner_halos(info, field, relaxed, lateral, carry, halos[2:])
+        field, inner = inner_halos(
+            info, field, relaxed, lateral, carry, halos[2:], NEXT_INNER if sweep else INNER
+        )
         inner = sent_back(inner)
         field, outer, loads, relaxed = outer_prediction(
             info, field, high, low, adjoint, lateral, central, carry, halos, loads, relaxed, given, conductance, forcing

time: 65 us -> 62.2 us (0.957)
  Pallas kernels: 35.2 us -> 29.9 us
  waiting for transfers between devices: 11.7 us -> 14 us
    ppermute x4, waiting for transfers between devices: 8.55 us -> 12.2 us  [sent_back(): return lax.ppermute(value, 'tm', [(1, 0), (0, 1)])]
    pallas_call x2, Pallas kernels: 8.5 us -> 6.38 us  [outer_prediction(): pl.pallas_call(functools.partial(outer_kernel, first_sweep), out_shape=ou...]
    ppermute x6, waiting for transfers between devices: 3.16 us -> 1.78 us  [exchanged(): lax.ppermute(value, axis, both_ways([(i, (i + 1) % count) for i in range(...]
    pallas_call x3, Pallas kernels: 3.88 us -> 2.53 us  [the longest x1 1.85 us: faces_of_initial(): pl.pallas_call(faces_kernel, out_shape=FACES, in_specs=[INV, INH], out_sp...]
    pallas_call x2, Pallas kernels: 3.12 us -> 2.02 us  [after_trace(): pl.pallas_call(late_inner_kernel if inner else late_outer_kernel, out_sha...]
    pallas_call x2, Pallas kernels: 4.93 us -> 3.84 us  [last(): pl.pallas_call(last_inner_kernel if inner else last_outer_kernel, out_sha...]
    pallas_call x1, Pallas kernels: 5.73 us -> 6.65 us  [next_prediction(): pl.pallas_call(next_kernel, out_shape=[VMEM(STACK, F32), VMEM(PADDED, BF1...]
  transfers between devices with their start and end apart: 12 -> 12, of which waited for: 6 -> 6; matrix products, arithmetic and copies ran while one was open for 0% -> 0% of each run, Pallas kernels for 45% -> 41%
where the time goes in v5:
time: 62.2 us; the launch traced here: 62.1 us
  Pallas kernels  29.9 us (48%)
  starting transfers between devices  17.1 us (27%)
  waiting for transfers between devices  14 us (23%)
  between operations  1.15 us (2%)
    ppermute x4, waiting for transfers between devices, sent_back(): return lax.ppermute(value, 'tm', [(1, 0), (0, 1)])  12.2 us
    pallas_call x1, Pallas kernels, first_prediction(): pl.pallas_call(first_kernel, out_shape=[VMEM(STACK, F32)] * 4 + [VMEM(PAD...  8.42 us
    pallas_call x1, Pallas kernels, next_prediction(): pl.pallas_call(next_kernel, out_shape=[VMEM(STACK, F32), VMEM(PADDED, BF1...  6.65 us
    pallas_call x2, Pallas kernels, outer_prediction(): pl.pallas_call(functools.partial(outer_kernel, first_sweep), out_shape=ou...  6.38 us
    ppermute x4, starting transfers between devices, sent_back(): return lax.ppermute(value, 'tm', [(1, 0), (0, 1)])  6.03 us
    ppermute x6, starting transfers between devices, exchanged(): lax.ppermute(value, axis, both_ways([(i, (i + 1) % count) for i in range(...  5.9 us
    ppermute x2, starting transfers between devices, exchanged_far_x(): return lax.ppermute(value, ('sx', 'sy'), both_ways(pairs))  5.13 us
    pallas_call x2, Pallas kernels, last(): pl.pallas_call(last_inner_kernel if inner else last_outer_kernel, out_sha...  3.84 us
  transfers between devices with their start and end apart: 12, of which 6 were waited for; matrix products, arithmetic and copies ran while one was open for 0% of the time, Pallas kernels for 41%

profile of v5, /device:TPU:64, one launch (start us, length us, event | category | flops | bytes accessed | tf_op | source)
XLA Modules:
  0.0 62.1 jit_solution(9688299987105102820)
XLA Ops:
  0.8 1.9 %faces.3 = (f32[4,256,128]{2,1,0:T(8,128)S(1)}, f32[4,256,128]{2,1,0:T(8,128)S(1)}, f32[4,8,16,128]{3,2,1,0:T(8,128)S(1)}, f32[4,8,16,128]{3,2,1,0:T(8,128)S(1)}) custom-call(s32[8,128]{1,0:T(8,128)S(1)} %broadcast_in_dim.3.info, f32[4,8,256,128]{3,2,1,0:T(8,128)} %bitcast.7), custom_call_target="tpu_custom_call" | custom-call | flops 2000000000 | tf_op jit(solution)/shard_map/faces/pallas_call | solution.py:105
  2.7 0.1 collective-permute-start.2
  2.8 2.7 %collective-permute-start.3 = (f32[4,256,128]{2,1,0:T(8,128)S(1)}, f32[4,256,128]{2,1,0:T(8,128)S(1)}, u32[]{:S(2)}, u32[]{:S(2)}) collective-permute-start(f32[4,256,128]{2,1,0:T(8,128)S(1)} %get-tuple-element.54), channel_id=1, source_target_pairs={{4,8},{5,9},{6,10},{7,11},{12,16},{13,17},{14,18},{15,19},{20,24},... | collective-permute-start | bytes 1572872 | tf_op jit(solution)/shard_map/ppermute | solution.py:512
  5.5 1.6 %collective-permute-start = (f32[4,8,16,128]{3,2,1,0:T(8,128)S(1)}, f32[4,8,16,128]{3,2,1,0:T(8,128)S(1)}, u32[]{:S(2)}, u32[]{:S(2)}) collective-permute-start(f32[4,8,16,128]{3,2,1,0:T(8,128)S(1)} %get-tuple-element.45), channel_id=1, source_target_pairs={{0,1},{2,3},{1,0},{3,2},{4,5},{6,7},{5,4},{7,6},{8,9},{10,11},{9,8... | collective-permute-start | bytes 786440 | tf_op jit(solution)/shard_map/ppermute | solution.py:505
  7.1 2.2 %collective-permute-start.1 = (f32[4,8,16,128]{3,2,1,0:T(8,128)S(1)}, f32[4,8,16,128]{3,2,1,0:T(8,128)S(1)}, u32[]{:S(2)}, u32[]{:S(2)}) collective-permute-start(f32[4,8,16,128]{3,2,1,0:T(8,128)S(1)} %get-tuple-element.46), channel_id=1, source_target_pairs={{1,2},{3,0},{2,1},{0,3},{5,6},{7,4},{6,5},{4,7},{9,10},{11,8},{10,... | collective-permute-start | bytes 786440 | tf_op jit(solution)/shard_map/ppermute | solution.py:505
  9.3 8.4 %first_inner.1 = (f32[4,8,256,128]{3,2,1,0:T(8,128)S(1)}, f32[4,8,256,128]{3,2,1,0:T(8,128)S(1)}, f32[4,8,256,128]{3,2,1,0:T(8,128)S(1)}, f32[4,8,256,128]{3,2,1...) custom-call(s32[8,128]{1,0:T(8,128)S(1)} %broadcast_in_dim.3.info, ...), custom_call_target="tpu_custom_call" | custom-call | flops 10000000 | tf_op jit(solution)/shard_map/first_inner/pallas_call | solution.py:243
  17.7 0.3 inner_halos.2
  18.1 1.9 %collective-permute-start.4 = (f32[640,128]{1,0:T(8,128)S(1)}, f32[640,128]{1,0:T(8,128)S(1)}, u32[]{:S(2)}, u32[]{:S(2)}) collective-permute-start(f32[640,128]{1,0:T(8,128)S(1)} %get-tuple-element.57), channel_id=1, source_target_pairs={{128,0},{0,128},{129,1},{1,129},{130,2},{2,130},{131,3},{3,131},{1... | collective-permute-start | bytes 983048 | tf_op jit(solution)/shard_map/ppermute | solution.py:516
  19.9 0.0 collective-permute-done.2.refs_12_
  19.9 0.0 collective-permute-done.3.refs_13_
  19.9 4.0 %first_outer.1 = (f32[4,8,256,128]{3,2,1,0:T(8,128)S(1)}, bf16[10,4,288,128]{3,2,1,0:T(8,128)(2,1)S(1)}, bf16[10,4,288,128]{3,2,1,0:T(8,128)(2,1)S(1)}, f32[4,8,...) custom-call(s32[8,128]{1,0:T(8,128)S(1)} %broadcast_in_dim.3.info, ...), custom_call_target="tpu_custom_call", output_to_operand_aliasing={{0}: (4, {}), {1}: (5, {}), {2}: (6, {}), {3}: (7, {}), {4}... | custom-call | flops 7000000000 | tf_op jit(solution)/shard_map/first_outer/pallas_call | solution.py:397
  24.0 1.2 %collective-permute-start.5 = (f32[384,128]{1,0:T(8,128)S(1)}, f32[384,128]{1,0:T(8,128)S(1)}, u32[]{:S(2)}, u32[]{:S(2)}) collective-permute-start(f32[384,128]{1,0:T(8,128)S(1)} %get-tuple-element.58), channel_id=1, source_target_pairs={{128,0},{0,128},{129,1},{1,129},{130,2},{2,130},{131,3},{3,131},{1... | collective-permute-start | bytes 589832 | tf_op jit(solution)/shard_map/ppermute | solution.py:516
  25.2 3.7 %collective-permute-done.4.trace = f32[640,128]{1,0:T(8,128)S(1)} collective-permute-done((f32[640,128]{1,0:T(8,128)S(1)}, f32[640,128]{1,0:T(8,128)S(1)}, u32[]{:S(2)}, u32[]{:S(2)}) %collective-permute-start.4) | collective-permute-done | bytes 327712 | tf_op jit(solution)/shard_map/ppermute | solution.py:516
  28.9 1.1 %late_inner.1.field = f32[4,8,256,128]{3,2,1,0:T(8,128)S(1)} custom-call(s32[8,128]{1,0:T(8,128)S(1)} %broadcast_in_dim.3.info, f32[4,8,256,128]{3,2,1,0:T(8,128)S(1)} %get-tuple-element.55.field, f32[4,8,256,128]{3,2,1,0:T(8,128)S(1)} %get-tuple-element.56.relaxed.refs_12_, ...), custom_call_target="tpu_custom_call", output_to_operand_aliasing={{}: (1, {})} | custom-call | flops 2000000000 | tf_op jit(solution)/shard_map/late_inner/pallas_call | solution.py:434
  30.0 2.1 %collective-permute-done.5.trace = f32[384,128]{1,0:T(8,128)S(1)} collective-permute-done((f32[384,128]{1,0:T(8,128)S(1)}, f32[384,128]{1,0:T(8,128)S(1)}, u32[]{:S(2)}, u32[]{:S(2)}) %collective-permute-start.5) | collective-permute-done | bytes 196640 | tf_op jit(solution)/shard_map/ppermute | solution.py:516
  32.2 0.9 %late_outer.1 = (f32[4,8,256,128]{3,2,1,0:T(8,128)S(1)}, f32[4,256,128]{2,1,0:T(8,128)S(1)}, f32[4,256,128]{2,1,0:T(8,128)S(1)}, f32[4,8,16,128]{3,2,1,0:T(8,128)S(1)}, f32[4,8,16,128]{3,2,1,0:T(8,128)S(1)}) custom-call(s32[8,128]{1,0:T(8,128)S(1)} %broadcast_in_dim.3.info, f32[4,8,256,128]{3,2,1,0:T(8,128)S(1)} %late_inner.1.field, ...), custom_call_target="tpu_custom_call", output_to_operand_aliasing={{0}: (1, {})} | custom-call | flops 2000000000 | tf_op jit(solution)/shard_map/late_outer/pallas_call | solution.py:434
  33.0 0.1 collective-permute-start.8
  33.1 2.5 %collective-permute-start.9 = (f32[4,256,128]{2,1,0:T(8,128)S(1)}, f32[4,256,128]{2,1,0:T(8,128)S(1)}, u32[]{:S(2)}, u32[]{:S(2)}) collective-permute-start(f32[4,256,128]{2,1,0:T(8,128)S(1)} %get-tuple-element.68), channel_id=1, source_target_pairs={{4,8},{5,9},{6,10},{7,11},{12,16},{13,17},{14,18},{15,19},{20,24},... | collective-permute-start | bytes 1572872 | tf_op jit(solution)/shard_map/ppermute | solution.py:512
  35.6 0.7 %collective-permute-start.6 = (f32[4,8,16,128]{3,2,1,0:T(8,128)S(1)}, f32[4,8,16,128]{3,2,1,0:T(8,128)S(1)}, u32[]{:S(2)}, u32[]{:S(2)}) collective-permute-start(f32[4,8,16,128]{3,2,1,0:T(8,128)S(1)} %get-tuple-element.62), channel_id=1, source_target_pairs={{0,1},{2,3},{1,0},{3,2},{4,5},{6,7},{5,4},{7,6},{8,9},{10,11},{9,8... | collective-permute-start | bytes 786440 | tf_op jit(solution)/shard_map/ppermute | solution.py:505
  36.3 1.3 %collective-permute-start.7 = (f32[4,8,16,128]{3,2,1,0:T(8,128)S(1)}, f32[4,8,16,128]{3,2,1,0:T(8,128)S(1)}, u32[]{:S(2)}, u32[]{:S(2)}) collective-permute-start(f32[4,8,16,128]{3,2,1,0:T(8,128)S(1)} %get-tuple-element.63), channel_id=1, source_target_pairs={{1,2},{3,0},{2,1},{0,3},{5,6},{7,4},{6,5},{4,7},{9,10},{11,8},{10,... | collective-permute-start | bytes 786440 | tf_op jit(solution)/shard_map/ppermute | solution.py:505
  37.6 6.7 %next_inner.1 = (f32[4,8,256,128]{3,2,1,0:T(8,128)S(1)}, bf16[10,4,288,128]{3,2,1,0:T(8,128)(2,1)S(1)}, bf16[10,4,288,128]{3,2,1,0:T(8,128)(2,1)S(1)}) custom-call(f32[4,8,256,128]{3,2,1,0:T(8,128)S(1)} %get-tuple-element.59.adjoint.refs_3_, f32[4,8,256,128]{3,2,1,0:T(8,128)S(1)} %get-tuple-element.60.loads.refs_11_, ...), custom_call_target="tpu_custom_call" | custom-call | flops 10000000 | tf_op jit(solution)/shard_map/next_inner/pallas_call | solution.py:267
  44.2 0.1 collective-permute-done.6.y_near.refs_9_
  44.4 1.6 %collective-permute-done.7.y_far.refs_10_ = f32[4,8,16,128]{3,2,1,0:T(8,128)S(1)} collective-permute-done((f32[4,8,16,128]{3,2,1,0:T(8,128)S(1)}, f32[4,8,16,128]{3,2,1,0:T(8,128)S(1)}, u32[]{:S(2)}, u32[]{:S(2)}) %collective-permute-start.7) | collective-permute-done | bytes 262176 | tf_op jit(solution)/shard_map/ppermute | solution.py:505
  46.0 0.3 inner_halos.3
  46.3 1.8 %collective-permute-start.10 = (f32[640,128]{1,0:T(8,128)S(1)}, f32[640,128]{1,0:T(8,128)S(1)}, u32[]{:S(2)}, u32[]{:S(2)}) collective-permute-start(f32[640,128]{1,0:T(8,128)S(1)} %get-tuple-element.70), channel_id=1, source_target_pairs={{128,0},{0,128},{129,1},{1,129},{130,2},{2,130},{131,3},{3,131},{1... | collective-permute-start | bytes 983048 | tf_op jit(solution)/shard_map/ppermute | solution.py:516
  48.2 0.0 collective-permute-done.8.refs_7_
  48.2 2.4 %next_outer.1 = (f32[4,8,256,128]{3,2,1,0:T(8,128)S(1)}, bf16[10,4,288,128]{3,2,1,0:T(8,128)(2,1)S(1)}, bf16[10,4,288,128]{3,2,1,0:T(8,128)(2,1)S(1)}, f32[384,128]{1,0:T(8,128)S(1)}) custom-call(s32[8,128]{1,0:T(8,128)S(1)} %broadcast_in_dim.3.info, ...), custom_call_target="tpu_custom_call", output_to_operand_aliasing={{0}: (1, {}), {1}: (2, {}), {2}: (3, {})} | custom-call | flops 7000000000 | tf_op jit(solution)/shard_map/next_outer/pallas_call | solution.py:397
  50.6 1.1 %collective-permute-start.11 = (f32[384,128]{1,0:T(8,128)S(1)}, f32[384,128]{1,0:T(8,128)S(1)}, u32[]{:S(2)}, u32[]{:S(2)}) collective-permute-start(f32[384,128]{1,0:T(8,128)S(1)} %get-tuple-element.72), channel_id=1, source_target_pairs={{128,0},{0,128},{129,1},{1,129},{130,2},{2,130},{131,3},{3,131},{1... | collective-permute-start | bytes 589832 | tf_op jit(solution)/shard_map/ppermute | solution.py:516
  51.6 5.4 %collective-permute-done.10.trace = f32[640,128]{1,0:T(8,128)S(1)} collective-permute-done((f32[640,128]{1,0:T(8,128)S(1)}, f32[640,128]{1,0:T(8,128)S(1)}, u32[]{:S(2)}, u32[]{:S(2)}) %collective-permute-start.10) | collective-permute-done | bytes 327712 | tf_op jit(solution)/shard_map/ppermute | solution.py:516
  57.1 2.2 %last_inner.1 = (f32[4,8,256,128]{3,2,1,0:T(8,128)S(1)}, f32[4,8,256,128]{3,2,1,0:T(8,128)}) custom-call(s32[8,128]{1,0:T(8,128)S(1)} %broadcast_in_dim.3.info, f32[4,8,256,128]{3,2,1,0:T(8,128)S(1)} %get-tuple-element.69.field, f32[4,8,256,128]{3,2,1,0:T(8,128)S(1)} %get-tuple-element.56.relaxed.refs_12_, ...), custom_call_target="tpu_custom_call", output_to_operand_aliasing={{0}: (1, {})} | custom-call | flops 3000000000 | tf_op jit(solution)/shard_map/last_inner/pallas_call | solution.py:486
  59.3 0.9 %collective-permute-done.11.trace = f32[384,128]{1,0:T(8,128)S(1)} collective-permute-done((f32[384,128]{1,0:T(8,128)S(1)}, f32[384,128]{1,0:T(8,128)S(1)}, u32[]{:S(2)}, u32[]{:S(2)}) %collective-permute-start.11) | collective-permute-done | bytes 196640 | tf_op jit(solution)/shard_map/ppermute | solution.py:516
  60.2 1.6 %last_outer.1 = (f32[4,8,256,128]{3,2,1,0:T(8,128)S(1)}, f32[4,8,256,128]{3,2,1,0:T(8,128)}) custom-call(s32[8,128]{1,0:T(8,128)S(1)} %broadcast_in_dim.3.info, f32[4,8,256,128]{3,2,1,0:T(8,128)S(1)} %get-tuple-element.71.field, f32[4,8,256,128]{3,2,1,0:T(8,128)S(1)} %get-tuple-element.56.relaxed.refs_12_, ...), custom_call_target="tpu_custom_call", output_to_operand_aliasing={{0}: (1, {}), {1}: (5, {})} | custom-call | flops 3000000000 | tf_op jit(solution)/shard_map/last_outer/pallas_call | solution.py:486
  (16 shorter events, 0.0 us)
Async XLA Ops:
  0.0 9.2 %copy-start.1 = (f32[4,8,16,16]{3,2,1,0:T(8,128)S(1)}, f32[4,8,16,16]{3,2,1,0:T(8,128)}, u32[]{:S(2)}) copy-start(f32[4,8,16,16]{3,2,1,0:T(8,128)} %refs_0_.1) | copy-start | bytes 98308
  0.0 9.2 %copy-start.5 = (f32[64,128]{1,0:T(8,128)S(1)}, f32[64,128]{1,0:T(8,128)}, u32[]{:S(2)}) copy-start(f32[64,128]{1,0:T(8,128)} %coupling.1) | copy-start | bytes 98308
  0.0 9.2 %copy-start.2 = (f32[6,128,128]{2,1,0:T(8,128)S(1)}, f32[6,128,128]{2,1,0:T(8,128)}, u32[]{:S(2)}) copy-start(f32[6,128,128]{2,1,0:T(8,128)} %faces.2) | copy-start | bytes 1179652
  0.0 9.2 %copy-start.4 = (f32[128,128]{1,0:T(8,128)S(1)}, f32[128,128]{1,0:T(8,128)}, u32[]{:S(2)}) copy-start(f32[128,128]{1,0:T(8,128)} %precond.1) | copy-start | bytes 196612
  0.0 9.2 %copy-start.3 = (f32[128,128]{1,0:T(8,128)S(1)}, f32[128,128]{1,0:T(8,128)}, u32[]{:S(2)}) copy-start(f32[128,128]{1,0:T(8,128)} %block_matrix.1) | copy-start | bytes 196612
  0.0 9.2 %copy-start = (f32[4,8,16,16,128]{4,3,2,1,0:T(8,128)S(1)}, f32[4,8,16,16,128]{4,3,2,1,0:T(8,128)}, u32[]{:S(2)}) copy-start(f32[4,8,16,16,128]{4,3,2,1,0:T(8,128)} %param.8) | copy-start | bytes 12582916
  2.7 17.2 %collective-permute-start.2 = (f32[4,256,128]{2,1,0:T(8,128)S(1)}, f32[4,256,128]{2,1,0:T(8,128)S(1)}, u32[]{:S(2)}, u32[]{:S(2)}) collective-permute-start(f32[4,256,128]{2,1,0:T(8,128)S(1)} %get-tuple-element.53), channel_id=1, source_target_pairs={{0,4},{8,12},{16,20},{24,28},{32,36},{40,44},{48,52},{56,60},{64,6... | collective-permute-start | bytes 1572872 | tf_op jit(solution)/shard_map/ppermute | solution.py:505
  2.8 17.1 %collective-permute-start.3 = (f32[4,256,128]{2,1,0:T(8,128)S(1)}, f32[4,256,128]{2,1,0:T(8,128)S(1)}, u32[]{:S(2)}, u32[]{:S(2)}) collective-permute-start(f32[4,256,128]{2,1,0:T(8,128)S(1)} %get-tuple-element.54), channel_id=1, source_target_pairs={{4,8},{5,9},{6,10},{7,11},{12,16},{13,17},{14,18},{15,19},{20,24},... | collective-permute-start | bytes 1572872 | tf_op jit(solution)/shard_map/ppermute | solution.py:512
  5.5 12.2 %collective-permute-start = (f32[4,8,16,128]{3,2,1,0:T(8,128)S(1)}, f32[4,8,16,128]{3,2,1,0:T(8,128)S(1)}, u32[]{:S(2)}, u32[]{:S(2)}) collective-permute-start(f32[4,8,16,128]{3,2,1,0:T(8,128)S(1)} %get-tuple-element.45), channel_id=1, source_target_pairs={{0,1},{2,3},{1,0},{3,2},{4,5},{6,7},{5,4},{7,6},{8,9},{10,11},{9,8... | collective-permute-start | bytes 786440 | tf_op jit(solution)/shard_map/ppermute | solution.py:505
  7.1 10.7 %collective-permute-start.1 = (f32[4,8,16,128]{3,2,1,0:T(8,128)S(1)}, f32[4,8,16,128]{3,2,1,0:T(8,128)S(1)}, u32[]{:S(2)}, u32[]{:S(2)}) collective-permute-start(f32[4,8,16,128]{3,2,1,0:T(8,128)S(1)} %get-tuple-element.46), channel_id=1, source_target_pairs={{1,2},{3,0},{2,1},{0,3},{5,6},{7,4},{6,5},{4,7},{9,10},{11,8},{10,... | collective-permute-start | bytes 786440 | tf_op jit(solution)/shard_map/ppermute | solution.py:505
  18.1 10.8 %collective-permute-start.4 = (f32[640,128]{1,0:T(8,128)S(1)}, f32[640,128]{1,0:T(8,128)S(1)}, u32[]{:S(2)}, u32[]{:S(2)}) collective-permute-start(f32[640,128]{1,0:T(8,128)S(1)} %get-tuple-element.57), channel_id=1, source_target_pairs={{128,0},{0,128},{129,1},{1,129},{130,2},{2,130},{131,3},{3,131},{1... | collective-permute-start | bytes 983048 | tf_op jit(solution)/shard_map/ppermute | solution.py:516
  24.0 8.2 %collective-permute-start.5 = (f32[384,128]{1,0:T(8,128)S(1)}, f32[384,128]{1,0:T(8,128)S(1)}, u32[]{:S(2)}, u32[]{:S(2)}) collective-permute-start(f32[384,128]{1,0:T(8,128)S(1)} %get-tuple-element.58), channel_id=1, source_target_pairs={{128,0},{0,128},{129,1},{1,129},{130,2},{2,130},{131,3},{3,131},{1... | collective-permute-start | bytes 589832 | tf_op jit(solution)/shard_map/ppermute | solution.py:516
  33.0 15.1 %collective-permute-start.8 = (f32[4,256,128]{2,1,0:T(8,128)S(1)}, f32[4,256,128]{2,1,0:T(8,128)S(1)}, u32[]{:S(2)}, u32[]{:S(2)}) collective-permute-start(f32[4,256,128]{2,1,0:T(8,128)S(1)} %get-tuple-element.67), channel_id=1, source_target_pairs={{0,4},{8,12},{16,20},{24,28},{32,36},{40,44},{48,52},{56,60},{64,6... | collective-permute-start | bytes 1572872 | tf_op jit(solution)/shard_map/ppermute | solution.py:505
  33.1 15.0 %collective-permute-start.9 = (f32[4,256,128]{2,1,0:T(8,128)S(1)}, f32[4,256,128]{2,1,0:T(8,128)S(1)}, u32[]{:S(2)}, u32[]{:S(2)}) collective-permute-start(f32[4,256,128]{2,1,0:T(8,128)S(1)} %get-tuple-element.68), channel_id=1, source_target_pairs={{4,8},{5,9},{6,10},{7,11},{12,16},{13,17},{14,18},{15,19},{20,24},... | collective-permute-start | bytes 1572872 | tf_op jit(solution)/shard_map/ppermute | solution.py:512
  35.6 8.8 %collective-permute-start.6 = (f32[4,8,16,128]{3,2,1,0:T(8,128)S(1)}, f32[4,8,16,128]{3,2,1,0:T(8,128)S(1)}, u32[]{:S(2)}, u32[]{:S(2)}) collective-permute-start(f32[4,8,16,128]{3,2,1,0:T(8,128)S(1)} %get-tuple-element.62), channel_id=1, source_target_pairs={{0,1},{2,3},{1,0},{3,2},{4,5},{6,7},{5,4},{7,6},{8,9},{10,11},{9,8... | collective-permute-start | bytes 786440 | tf_op jit(solution)/shard_map/ppermute | solution.py:505
  36.3 9.7 %collective-permute-start.7 = (f32[4,8,16,128]{3,2,1,0:T(8,128)S(1)}, f32[4,8,16,128]{3,2,1,0:T(8,128)S(1)}, u32[]{:S(2)}, u32[]{:S(2)}) collective-permute-start(f32[4,8,16,128]{3,2,1,0:T(8,128)S(1)} %get-tuple-element.63), channel_id=1, source_target_pairs={{1,2},{3,0},{2,1},{0,3},{5,6},{7,4},{6,5},{4,7},{9,10},{11,8},{10,... | collective-permute-start | bytes 786440 | tf_op jit(solution)/shard_map/ppermute | solution.py:505
  46.3 10.7 %collective-permute-start.10 = (f32[640,128]{1,0:T(8,128)S(1)}, f32[640,128]{1,0:T(8,128)S(1)}, u32[]{:S(2)}, u32[]{:S(2)}) collective-permute-start(f32[640,128]{1,0:T(8,128)S(1)} %get-tuple-element.70), channel_id=1, source_target_pairs={{128,0},{0,128},{129,1},{1,129},{130,2},{2,130},{131,3},{3,131},{1... | collective-permute-start | bytes 983048 | tf_op jit(solution)/shard_map/ppermute | solution.py:516
  50.6 9.7 %collective-permute-start.11 = (f32[384,128]{1,0:T(8,128)S(1)}, f32[384,128]{1,0:T(8,128)S(1)}, u32[]{:S(2)}, u32[]{:S(2)}) collective-permute-start(f32[384,128]{1,0:T(8,128)S(1)} %get-tuple-element.72), channel_id=1, source_target_pairs={{128,0},{0,128},{129,1},{1,129},{130,2},{2,130},{131,3},{3,131},{1... | collective-permute-start | bytes 589832 | tf_op jit(solution)/shard_map/ppermute | solution.py:516

commit v6 on v5

--- a/solution.py
+++ b/solution.py
@@ -523,10 +523,9 @@
     info = jnp.full((8, BLOCK), counts[0, 0])
 
     def halos_of(x_near, x_far, y_near, y_far):
-        return (
-            exchanged(x_near, "sx", 0), exchanged_far_x(x_far),
-            exchanged(y_near, "sy", 0), exchanged(y_far, "sy", 1),
-        )
+        x_far = exchanged_far_x(x_far)
+        y_near, y_far = exchanged(y_near, "sy", 0), exchanged(y_far, "sy", 1)
+        return exchanged(x_near, "sx", 0), x_far, y_near, y_far
 
     halos = halos_of(*faces_of_initial(info, initial))
     field, adjoint, loads, relaxed, high, low, lateral, central, carry, given = first_prediction(

time: 62.2 us -> 62.2 us (level)
  no operation moved by 1% of the time
where the time goes in v6:
time: 62.2 us; the launch traced here: 62.1 us
  Pallas kernels  29.9 us (48%)
  starting transfers between devices  17.1 us (27%)
  waiting for transfers between devices  14 us (23%)
  between operations  1.15 us (2%)
    ppermute x4, waiting for transfers between devices, sent_back(): return lax.ppermute(value, 'tm', [(1, 0), (0, 1)])  12.2 us
    pallas_call x1, Pallas kernels, first_prediction(): pl.pallas_call(first_kernel, out_shape=[VMEM(STACK, F32)] * 4 + [VMEM(PAD...  8.42 us
    pallas_call x1, Pallas kernels, next_prediction(): pl.pallas_call(next_kernel, out_shape=[VMEM(STACK, F32), VMEM(PADDED, BF1...  6.65 us
    pallas_call x2, Pallas kernels, outer_prediction(): pl.pallas_call(functools.partial(outer_kernel, first_sweep), out_shape=ou...  6.38 us
    ppermute x4, starting transfers between devices, sent_back(): return lax.ppermute(value, 'tm', [(1, 0), (0, 1)])  6.03 us
    ppermute x6, starting transfers between devices, exchanged(): lax.ppermute(value, axis, both_ways([(i, (i + 1) % count) for i in range(...  5.9 us
    ppermute x2, starting transfers between devices, exchanged_far_x(): return lax.ppermute(value, ('sx', 'sy'), both_ways(pairs))  5.13 us
    pallas_call x2, Pallas kernels, last(): pl.pallas_call(last_inner_kernel if inner else last_outer_kernel, out_sha...  3.84 us
  transfers between devices with their start and end apart: 12, of which 6 were waited for; matrix products, arithmetic and copies ran while one was open for 0% of the time, Pallas kernels for 41%

profile of v6, /device:TPU:64, one launch (start us, length us, event | category | flops | bytes accessed | tf_op | source)
XLA Modules:
  0.0 62.1 jit_solution(9688299987105102820)
XLA Ops:
  0.8 1.9 %faces.3 = (f32[4,256,128]{2,1,0:T(8,128)S(1)}, f32[4,256,128]{2,1,0:T(8,128)S(1)}, f32[4,8,16,128]{3,2,1,0:T(8,128)S(1)}, f32[4,8,16,128]{3,2,1,0:T(8,128)S(1)}) custom-call(s32[8,128]{1,0:T(8,128)S(1)} %broadcast_in_dim.3.info, f32[4,8,256,128]{3,2,1,0:T(8,128)} %bitcast.7), custom_call_target="tpu_custom_call" | custom-call | flops 2000000000 | tf_op jit(solution)/shard_map/faces/pallas_call | solution.py:105
  2.7 0.1 collective-permute-start.2
  2.8 2.7 %collective-permute-start.3 = (f32[4,256,128]{2,1,0:T(8,128)S(1)}, f32[4,256,128]{2,1,0:T(8,128)S(1)}, u32[]{:S(2)}, u32[]{:S(2)}) collective-permute-start(f32[4,256,128]{2,1,0:T(8,128)S(1)} %get-tuple-element.54), channel_id=1, source_target_pairs={{4,8},{5,9},{6,10},{7,11},{12,16},{13,17},{14,18},{15,19},{20,24},... | collective-permute-start | bytes 1572872 | tf_op jit(solution)/shard_map/ppermute | solution.py:512
  5.5 1.6 %collective-permute-start = (f32[4,8,16,128]{3,2,1,0:T(8,128)S(1)}, f32[4,8,16,128]{3,2,1,0:T(8,128)S(1)}, u32[]{:S(2)}, u32[]{:S(2)}) collective-permute-start(f32[4,8,16,128]{3,2,1,0:T(8,128)S(1)} %get-tuple-element.45), channel_id=1, source_target_pairs={{0,1},{2,3},{1,0},{3,2},{4,5},{6,7},{5,4},{7,6},{8,9},{10,11},{9,8... | collective-permute-start | bytes 786440 | tf_op jit(solution)/shard_map/ppermute | solution.py:505
  7.1 2.2 %collective-permute-start.1 = (f32[4,8,16,128]{3,2,1,0:T(8,128)S(1)}, f32[4,8,16,128]{3,2,1,0:T(8,128)S(1)}, u32[]{:S(2)}, u32[]{:S(2)}) collective-permute-start(f32[4,8,16,128]{3,2,1,0:T(8,128)S(1)} %get-tuple-element.46), channel_id=1, source_target_pairs={{1,2},{3,0},{2,1},{0,3},{5,6},{7,4},{6,5},{4,7},{9,10},{11,8},{10,... | collective-permute-start | bytes 786440 | tf_op jit(solution)/shard_map/ppermute | solution.py:505
  9.3 8.4 %first_inner.1 = (f32[4,8,256,128]{3,2,1,0:T(8,128)S(1)}, f32[4,8,256,128]{3,2,1,0:T(8,128)S(1)}, f32[4,8,256,128]{3,2,1,0:T(8,128)S(1)}, f32[4,8,256,128]{3,2,1...) custom-call(s32[8,128]{1,0:T(8,128)S(1)} %broadcast_in_dim.3.info, ...), custom_call_target="tpu_custom_call" | custom-call | flops 10000000 | tf_op jit(solution)/shard_map/first_inner/pallas_call | solution.py:243
  17.7 0.3 inner_halos.2
  18.1 1.9 %collective-permute-start.4 = (f32[640,128]{1,0:T(8,128)S(1)}, f32[640,128]{1,0:T(8,128)S(1)}, u32[]{:S(2)}, u32[]{:S(2)}) collective-permute-start(f32[640,128]{1,0:T(8,128)S(1)} %get-tuple-element.57), channel_id=1, source_target_pairs={{128,0},{0,128},{129,1},{1,129},{130,2},{2,130},{131,3},{3,131},{1... | collective-permute-start | bytes 983048 | tf_op jit(solution)/shard_map/ppermute | solution.py:516
  19.9 0.0 collective-permute-done.2.refs_12_
  19.9 0.0 collective-permute-done.3.refs_13_
  19.9 4.0 %first_outer.1 = (f32[4,8,256,128]{3,2,1,0:T(8,128)S(1)}, bf16[10,4,288,128]{3,2,1,0:T(8,128)(2,1)S(1)}, bf16[10,4,288,128]{3,2,1,0:T(8,128)(2,1)S(1)}, f32[4,8,...) custom-call(s32[8,128]{1,0:T(8,128)S(1)} %broadcast_in_dim.3.info, ...), custom_call_target="tpu_custom_call", output_to_operand_aliasing={{0}: (4, {}), {1}: (5, {}), {2}: (6, {}), {3}: (7, {}), {4}... | custom-call | flops 7000000000 | tf_op jit(solution)/shard_map/first_outer/pallas_call | solution.py:397
  24.0 1.2 %collective-permute-start.5 = (f32[384,128]{1,0:T(8,128)S(1)}, f32[384,128]{1,0:T(8,128)S(1)}, u32[]{:S(2)}, u32[]{:S(2)}) collective-permute-start(f32[384,128]{1,0:T(8,128)S(1)} %get-tuple-element.58), channel_id=1, source_target_pairs={{128,0},{0,128},{129,1},{1,129},{130,2},{2,130},{131,3},{3,131},{1... | collective-permute-start | bytes 589832 | tf_op jit(solution)/shard_map/ppermute | solution.py:516
  25.2 3.7 %collective-permute-done.4.trace = f32[640,128]{1,0:T(8,128)S(1)} collective-permute-done((f32[640,128]{1,0:T(8,128)S(1)}, f32[640,128]{1,0:T(8,128)S(1)}, u32[]{:S(2)}, u32[]{:S(2)}) %collective-permute-start.4) | collective-permute-done | bytes 327712 | tf_op jit(solution)/shard_map/ppermute | solution.py:516
  28.9 1.1 %late_inner.1.field = f32[4,8,256,128]{3,2,1,0:T(8,128)S(1)} custom-call(s32[8,128]{1,0:T(8,128)S(1)} %broadcast_in_dim.3.info, f32[4,8,256,128]{3,2,1,0:T(8,128)S(1)} %get-tuple-element.55.field, f32[4,8,256,128]{3,2,1,0:T(8,128)S(1)} %get-tuple-element.56.relaxed.refs_12_, ...), custom_call_target="tpu_custom_call", output_to_operand_aliasing={{}: (1, {})} | custom-call | flops 2000000000 | tf_op jit(solution)/shard_map/late_inner/pallas_call | solution.py:434
  30.0 2.1 %collective-permute-done.5.trace = f32[384,128]{1,0:T(8,128)S(1)} collective-permute-done((f32[384,128]{1,0:T(8,128)S(1)}, f32[384,128]{1,0:T(8,128)S(1)}, u32[]{:S(2)}, u32[]{:S(2)}) %collective-permute-start.5) | collective-permute-done | bytes 196640 | tf_op jit(solution)/shard_map/ppermute | solution.py:516
  32.2 0.9 %late_outer.1 = (f32[4,8,256,128]{3,2,1,0:T(8,128)S(1)}, f32[4,256,128]{2,1,0:T(8,128)S(1)}, f32[4,256,128]{2,1,0:T(8,128)S(1)}, f32[4,8,16,128]{3,2,1,0:T(8,128)S(1)}, f32[4,8,16,128]{3,2,1,0:T(8,128)S(1)}) custom-call(s32[8,128]{1,0:T(8,128)S(1)} %broadcast_in_dim.3.info, f32[4,8,256,128]{3,2,1,0:T(8,128)S(1)} %late_inner.1.field, ...), custom_call_target="tpu_custom_call", output_to_operand_aliasing={{0}: (1, {})} | custom-call | flops 2000000000 | tf_op jit(solution)/shard_map/late_outer/pallas_call | solution.py:434
  33.0 0.1 collective-permute-start.8
  33.1 2.5 %collective-permute-start.9 = (f32[4,256,128]{2,1,0:T(8,128)S(1)}, f32[4,256,128]{2,1,0:T(8,128)S(1)}, u32[]{:S(2)}, u32[]{:S(2)}) collective-permute-start(f32[4,256,128]{2,1,0:T(8,128)S(1)} %get-tuple-element.68), channel_id=1, source_target_pairs={{4,8},{5,9},{6,10},{7,11},{12,16},{13,17},{14,18},{15,19},{20,24},... | collective-permute-start | bytes 1572872 | tf_op jit(solution)/shard_map/ppermute | solution.py:512
  35.6 0.7 %collective-permute-start.6 = (f32[4,8,16,128]{3,2,1,0:T(8,128)S(1)}, f32[4,8,16,128]{3,2,1,0:T(8,128)S(1)}, u32[]{:S(2)}, u32[]{:S(2)}) collective-permute-start(f32[4,8,16,128]{3,2,1,0:T(8,128)S(1)} %get-tuple-element.62), channel_id=1, source_target_pairs={{0,1},{2,3},{1,0},{3,2},{4,5},{6,7},{5,4},{7,6},{8,9},{10,11},{9,8... | collective-permute-start | bytes 786440 | tf_op jit(solution)/shard_map/ppermute | solution.py:505
  36.3 1.3 %collective-permute-start.7 = (f32[4,8,16,128]{3,2,1,0:T(8,128)S(1)}, f32[4,8,16,128]{3,2,1,0:T(8,128)S(1)}, u32[]{:S(2)}, u32[]{:S(2)}) collective-permute-start(f32[4,8,16,128]{3,2,1,0:T(8,128)S(1)} %get-tuple-element.63), channel_id=1, source_target_pairs={{1,2},{3,0},{2,1},{0,3},{5,6},{7,4},{6,5},{4,7},{9,10},{11,8},{10,... | collective-permute-start | bytes 786440 | tf_op jit(solution)/shard_map/ppermute | solution.py:505
  37.6 6.7 %next_inner.1 = (f32[4,8,256,128]{3,2,1,0:T(8,128)S(1)}, bf16[10,4,288,128]{3,2,1,0:T(8,128)(2,1)S(1)}, bf16[10,4,288,128]{3,2,1,0:T(8,128)(2,1)S(1)}) custom-call(f32[4,8,256,128]{3,2,1,0:T(8,128)S(1)} %get-tuple-element.59.adjoint.refs_3_, f32[4,8,256,128]{3,2,1,0:T(8,128)S(1)} %get-tuple-element.60.loads.refs_11_, ...), custom_call_target="tpu_custom_call" | custom-call | flops 10000000 | tf_op jit(solution)/shard_map/next_inner/pallas_call | solution.py:267
  44.2 0.1 collective-permute-done.6.y_near.refs_9_
  44.4 1.6 %collective-permute-done.7.y_far.refs_10_ = f32[4,8,16,128]{3,2,1,0:T(8,128)S(1)} collective-permute-done((f32[4,8,16,128]{3,2,1,0:T(8,128)S(1)}, f32[4,8,16,128]{3,2,1,0:T(8,128)S(1)}, u32[]{:S(2)}, u32[]{:S(2)}) %collective-permute-start.7) | collective-permute-done | bytes 262176 | tf_op jit(solution)/shard_map/ppermute | solution.py:505
  46.0 0.3 inner_halos.3
  46.3 1.8 %collective-permute-start.10 = (f32[640,128]{1,0:T(8,128)S(1)}, f32[640,128]{1,0:T(8,128)S(1)}, u32[]{:S(2)}, u32[]{:S(2)}) collective-permute-start(f32[640,128]{1,0:T(8,128)S(1)} %get-tuple-element.70), channel_id=1, source_target_pairs={{128,0},{0,128},{129,1},{1,129},{130,2},{2,130},{131,3},{3,131},{1... | collective-permute-start | bytes 983048 | tf_op jit(solution)/shard_map/ppermute | solution.py:516
  48.2 0.0 collective-permute-done.8.refs_7_
  48.2 2.4 %next_outer.1 = (f32[4,8,256,128]{3,2,1,0:T(8,128)S(1)}, bf16[10,4,288,128]{3,2,1,0:T(8,128)(2,1)S(1)}, bf16[10,4,288,128]{3,2,1,0:T(8,128)(2,1)S(1)}, f32[384,128]{1,0:T(8,128)S(1)}) custom-call(s32[8,128]{1,0:T(8,128)S(1)} %broadcast_in_dim.3.info, ...), custom_call_target="tpu_custom_call", output_to_operand_aliasing={{0}: (1, {}), {1}: (2, {}), {2}: (3, {})} | custom-call | flops 7000000000 | tf_op jit(solution)/shard_map/next_outer/pallas_call | solution.py:397
  50.6 1.1 %collective-permute-start.11 = (f32[384,128]{1,0:T(8,128)S(1)}, f32[384,128]{1,0:T(8,128)S(1)}, u32[]{:S(2)}, u32[]{:S(2)}) collective-permute-start(f32[384,128]{1,0:T(8,128)S(1)} %get-tuple-element.72), channel_id=1, source_target_pairs={{128,0},{0,128},{129,1},{1,129},{130,2},{2,130},{131,3},{3,131},{1... | collective-permute-start | bytes 589832 | tf_op jit(solution)/shard_map/ppermute | solution.py:516
  51.6 5.4 %collective-permute-done.10.trace = f32[640,128]{1,0:T(8,128)S(1)} collective-permute-done((f32[640,128]{1,0:T(8,128)S(1)}, f32[640,128]{1,0:T(8,128)S(1)}, u32[]{:S(2)}, u32[]{:S(2)}) %collective-permute-start.10) | collective-permute-done | bytes 327712 | tf_op jit(solution)/shard_map/ppermute | solution.py:516
  57.1 2.2 %last_inner.1 = (f32[4,8,256,128]{3,2,1,0:T(8,128)S(1)}, f32[4,8,256,128]{3,2,1,0:T(8,128)}) custom-call(s32[8,128]{1,0:T(8,128)S(1)} %broadcast_in_dim.3.info, f32[4,8,256,128]{3,2,1,0:T(8,128)S(1)} %get-tuple-element.69.field, f32[4,8,256,128]{3,2,1,0:T(8,128)S(1)} %get-tuple-element.56.relaxed.refs_12_, ...), custom_call_target="tpu_custom_call", output_to_operand_aliasing={{0}: (1, {})} | custom-call | flops 3000000000 | tf_op jit(solution)/shard_map/last_inner/pallas_call | solution.py:486
  59.3 0.9 %collective-permute-done.11.trace = f32[384,128]{1,0:T(8,128)S(1)} collective-permute-done((f32[384,128]{1,0:T(8,128)S(1)}, f32[384,128]{1,0:T(8,128)S(1)}, u32[]{:S(2)}, u32[]{:S(2)}) %collective-permute-start.11) | collective-permute-done | bytes 196640 | tf_op jit(solution)/shard_map/ppermute | solution.py:516
  60.2 1.6 %last_outer.1 = (f32[4,8,256,128]{3,2,1,0:T(8,128)S(1)}, f32[4,8,256,128]{3,2,1,0:T(8,128)}) custom-call(s32[8,128]{1,0:T(8,128)S(1)} %broadcast_in_dim.3.info, f32[4,8,256,128]{3,2,1,0:T(8,128)S(1)} %get-tuple-element.71.field, f32[4,8,256,128]{3,2,1,0:T(8,128)S(1)} %get-tuple-element.56.relaxed.refs_12_, ...), custom_call_target="tpu_custom_call", output_to_operand_aliasing={{0}: (1, {}), {1}: (5, {})} | custom-call | flops 3000000000 | tf_op jit(solution)/shard_map/last_outer/pallas_call | solution.py:486
  (16 shorter events, 0.0 us)
Async XLA Ops:
  0.0 9.2 %copy-start.1 = (f32[4,8,16,16]{3,2,1,0:T(8,128)S(1)}, f32[4,8,16,16]{3,2,1,0:T(8,128)}, u32[]{:S(2)}) copy-start(f32[4,8,16,16]{3,2,1,0:T(8,128)} %refs_0_.1) | copy-start | bytes 98308
  0.0 9.2 %copy-start.5 = (f32[64,128]{1,0:T(8,128)S(1)}, f32[64,128]{1,0:T(8,128)}, u32[]{:S(2)}) copy-start(f32[64,128]{1,0:T(8,128)} %coupling.1) | copy-start | bytes 98308
  0.0 9.2 %copy-start.2 = (f32[6,128,128]{2,1,0:T(8,128)S(1)}, f32[6,128,128]{2,1,0:T(8,128)}, u32[]{:S(2)}) copy-start(f32[6,128,128]{2,1,0:T(8,128)} %faces.2) | copy-start | bytes 1179652
  0.0 9.2 %copy-start.4 = (f32[128,128]{1,0:T(8,128)S(1)}, f32[128,128]{1,0:T(8,128)}, u32[]{:S(2)}) copy-start(f32[128,128]{1,0:T(8,128)} %precond.1) | copy-start | bytes 196612
  0.0 9.2 %copy-start.3 = (f32[128,128]{1,0:T(8,128)S(1)}, f32[128,128]{1,0:T(8,128)}, u32[]{:S(2)}) copy-start(f32[128,128]{1,0:T(8,128)} %block_matrix.1) | copy-start | bytes 196612
  0.0 9.2 %copy-start = (f32[4,8,16,16,128]{4,3,2,1,0:T(8,128)S(1)}, f32[4,8,16,16,128]{4,3,2,1,0:T(8,128)}, u32[]{:S(2)}) copy-start(f32[4,8,16,16,128]{4,3,2,1,0:T(8,128)} %param.8) | copy-start | bytes 12582916
  2.7 17.2 %collective-permute-start.2 = (f32[4,256,128]{2,1,0:T(8,128)S(1)}, f32[4,256,128]{2,1,0:T(8,128)S(1)}, u32[]{:S(2)}, u32[]{:S(2)}) collective-permute-start(f32[4,256,128]{2,1,0:T(8,128)S(1)} %get-tuple-element.53), channel_id=1, source_target_pairs={{0,4},{8,12},{16,20},{24,28},{32,36},{40,44},{48,52},{56,60},{64,6... | collective-permute-start | bytes 1572872 | tf_op jit(solution)/shard_map/ppermute | solution.py:505
  2.8 17.1 %collective-permute-start.3 = (f32[4,256,128]{2,1,0:T(8,128)S(1)}, f32[4,256,128]{2,1,0:T(8,128)S(1)}, u32[]{:S(2)}, u32[]{:S(2)}) collective-permute-start(f32[4,256,128]{2,1,0:T(8,128)S(1)} %get-tuple-element.54), channel_id=1, source_target_pairs={{4,8},{5,9},{6,10},{7,11},{12,16},{13,17},{14,18},{15,19},{20,24},... | collective-permute-start | bytes 1572872 | tf_op jit(solution)/shard_map/ppermute | solution.py:512
  5.5 12.2 %collective-permute-start = (f32[4,8,16,128]{3,2,1,0:T(8,128)S(1)}, f32[4,8,16,128]{3,2,1,0:T(8,128)S(1)}, u32[]{:S(2)}, u32[]{:S(2)}) collective-permute-start(f32[4,8,16,128]{3,2,1,0:T(8,128)S(1)} %get-tuple-element.45), channel_id=1, source_target_pairs={{0,1},{2,3},{1,0},{3,2},{4,5},{6,7},{5,4},{7,6},{8,9},{10,11},{9,8... | collective-permute-start | bytes 786440 | tf_op jit(solution)/shard_map/ppermute | solution.py:505
  7.1 10.7 %collective-permute-start.1 = (f32[4,8,16,128]{3,2,1,0:T(8,128)S(1)}, f32[4,8,16,128]{3,2,1,0:T(8,128)S(1)}, u32[]{:S(2)}, u32[]{:S(2)}) collective-permute-start(f32[4,8,16,128]{3,2,1,0:T(8,128)S(1)} %get-tuple-element.46), channel_id=1, source_target_pairs={{1,2},{3,0},{2,1},{0,3},{5,6},{7,4},{6,5},{4,7},{9,10},{11,8},{10,... | collective-permute-start | bytes 786440 | tf_op jit(solution)/shard_map/ppermute | solution.py:505
  18.1 10.8 %collective-permute-start.4 = (f32[640,128]{1,0:T(8,128)S(1)}, f32[640,128]{1,0:T(8,128)S(1)}, u32[]{:S(2)}, u32[]{:S(2)}) collective-permute-start(f32[640,128]{1,0:T(8,128)S(1)} %get-tuple-element.57), channel_id=1, source_target_pairs={{128,0},{0,128},{129,1},{1,129},{130,2},{2,130},{131,3},{3,131},{1... | collective-permute-start | bytes 983048 | tf_op jit(solution)/shard_map/ppermute | solution.py:516
  24.0 8.2 %collective-permute-start.5 = (f32[384,128]{1,0:T(8,128)S(1)}, f32[384,128]{1,0:T(8,128)S(1)}, u32[]{:S(2)}, u32[]{:S(2)}) collective-permute-start(f32[384,128]{1,0:T(8,128)S(1)} %get-tuple-element.58), channel_id=1, source_target_pairs={{128,0},{0,128},{129,1},{1,129},{130,2},{2,130},{131,3},{3,131},{1... | collective-permute-start | bytes 589832 | tf_op jit(solution)/shard_map/ppermute | solution.py:516
  33.0 15.1 %collective-permute-start.8 = (f32[4,256,128]{2,1,0:T(8,128)S(1)}, f32[4,256,128]{2,1,0:T(8,128)S(1)}, u32[]{:S(2)}, u32[]{:S(2)}) collective-permute-start(f32[4,256,128]{2,1,0:T(8,128)S(1)} %get-tuple-element.67), channel_id=1, source_target_pairs={{0,4},{8,12},{16,20},{24,28},{32,36},{40,44},{48,52},{56,60},{64,6... | collective-permute-start | bytes 1572872 | tf_op jit(solution)/shard_map/ppermute | solution.py:505
  33.1 15.0 %collective-permute-start.9 = (f32[4,256,128]{2,1,0:T(8,128)S(1)}, f32[4,256,128]{2,1,0:T(8,128)S(1)}, u32[]{:S(2)}, u32[]{:S(2)}) collective-permute-start(f32[4,256,128]{2,1,0:T(8,128)S(1)} %get-tuple-element.68), channel_id=1, source_target_pairs={{4,8},{5,9},{6,10},{7,11},{12,16},{13,17},{14,18},{15,19},{20,24},... | collective-permute-start | bytes 1572872 | tf_op jit(solution)/shard_map/ppermute | solution.py:512
  35.6 8.8 %collective-permute-start.6 = (f32[4,8,16,128]{3,2,1,0:T(8,128)S(1)}, f32[4,8,16,128]{3,2,1,0:T(8,128)S(1)}, u32[]{:S(2)}, u32[]{:S(2)}) collective-permute-start(f32[4,8,16,128]{3,2,1,0:T(8,128)S(1)} %get-tuple-element.62), channel_id=1, source_target_pairs={{0,1},{2,3},{1,0},{3,2},{4,5},{6,7},{5,4},{7,6},{8,9},{10,11},{9,8... | collective-permute-start | bytes 786440 | tf_op jit(solution)/shard_map/ppermute | solution.py:505
  36.3 9.7 %collective-permute-start.7 = (f32[4,8,16,128]{3,2,1,0:T(8,128)S(1)}, f32[4,8,16,128]{3,2,1,0:T(8,128)S(1)}, u32[]{:S(2)}, u32[]{:S(2)}) collective-permute-start(f32[4,8,16,128]{3,2,1,0:T(8,128)S(1)} %get-tuple-element.63), channel_id=1, source_target_pairs={{1,2},{3,0},{2,1},{0,3},{5,6},{7,4},{6,5},{4,7},{9,10},{11,8},{10,... | collective-permute-start | bytes 786440 | tf_op jit(solution)/shard_map/ppermute | solution.py:505
  46.3 10.7 %collective-permute-start.10 = (f32[640,128]{1,0:T(8,128)S(1)}, f32[640,128]{1,0:T(8,128)S(1)}, u32[]{:S(2)}, u32[]{:S(2)}) collective-permute-start(f32[640,128]{1,0:T(8,128)S(1)} %get-tuple-element.70), channel_id=1, source_target_pairs={{128,0},{0,128},{129,1},{1,129},{130,2},{2,130},{131,3},{3,131},{1... | collective-permute-start | bytes 983048 | tf_op jit(solution)/shard_map/ppermute | solution.py:516
  50.6 9.7 %collective-permute-start.11 = (f32[384,128]{1,0:T(8,128)S(1)}, f32[384,128]{1,0:T(8,128)S(1)}, u32[]{:S(2)}, u32[]{:S(2)}) collective-permute-start(f32[384,128]{1,0:T(8,128)S(1)} %get-tuple-element.72), channel_id=1, source_target_pairs={{128,0},{0,128},{129,1},{1,129},{130,2},{2,130},{131,3},{3,131},{1... | collective-permute-start | bytes 589832 | tf_op jit(solution)/shard_map/ppermute | solution.py:516
